TPU v7x, 32 devices: a whole 2x2x4 slice. The times are simulated.
32 devices in a mesh: group: 2 (over y), feat: 4 (over z), tok: 2 (over x), sub: 2 (over core).
Axes of the slice: x: 2, y: 2, z: 4, core: 2. Of those that a mesh axis runs over, the one named last changes fastest.
Arguments:
- inputs: bfloat16 [2048, 8192], P(('group', 'tok', 'sub'), 'feat'), parts along dimension 0, may hold values from -6 to 6
- cotangent: bfloat16 [2048, 8192], P(('group', 'tok', 'sub'), 'feat'), parts along dimension 0, may hold values from -6 to 6
- w_in: bfloat16 [64, 7, 128, 128], P('feat'), may hold values from -0.1875 to 0.1875
- w_out: bfloat16 [64, 7, 128, 128], P('feat'), may hold values from -0.1875 to 0.1875
- u_in: bfloat16 [8192, 128], P('feat'), may hold values from -0.0625 to 0.0625
- v_in: bfloat16 [128, 8192], P(None, 'feat'), may hold values from -0.5 to 0.5
- u_out: bfloat16 [8192, 128], P('feat'), may hold values from -0.0625 to 0.0625
- v_out: bfloat16 [128, 8192], P(None, 'feat'), may hold values from -0.5 to 0.5
Outputs:
- output: bfloat16 [2048, 8192], P(('group', 'tok', 'sub'), 'feat'), parts along dimension 0
- input_grad: bfloat16 [2048, 8192], P(('group', 'tok', 'sub'), 'feat'), parts along dimension 0
- grad_w_in: float32 [128, 7, 128, 128], P(('group', 'feat'), None, ('tok', 'sub')), parts along dimension 0
- grad_w_out: float32 [128, 7, 128, 128], P(('group', 'feat'), None, ('tok', 'sub')), parts along dimension 0
- grad_u_in: float32 [16384, 128], P(('group', 'feat'), ('tok', 'sub')), parts along dimension 0
- grad_v_in: float32 [256, 8192], P(('group', 'tok', 'sub'), 'feat'), parts along dimension 0
- grad_u_out: float32 [16384, 128], P(('group', 'feat'), ('tok', 'sub')), parts along dimension 0
- grad_v_out: float32 [256, 8192], P(('group', 'tok', 'sub'), 'feat'), parts along dimension 0
There are 2 independent parts, one for each index of `group`. A program takes and returns all parts, laid end to end along the dimension named above; an argument that names none is the same for every part. Nothing has to cross between parts.
All inputs are finite; a program needn't handle non-finite values.
Results may differ from a plain program's by a relative error of at most 0.023.
Values may be sent and summed in bfloat16 or wider, within the bound.
No kernel may reach another device: no remote copies, remote signals or barrier semaphores. Data moves between devices by JAX's collectives and lax.ppermute only.
A program may use at most 192 MiB of HBM per device.

v0:
```python
import math

import jax
import jax.numpy as jnp
from jax import lax
from jax.sharding import PartitionSpec as P


def partner(value, axis, bit):
    mask = 2**bit
    pairs = [(source, source ^ mask) for source in range(lax.axis_size(axis))]
    return lax.ppermute(value, axis, pairs)


def flip_level(array_in, level, dim_index):
    count = array_in.shape[dim_index]
    stride = 1 << level
    shape = (
        array_in.shape[:dim_index]
        + (count // (2 * stride), 2, stride)
        + array_in.shape[dim_index + 1 :]
    )
    folded = jnp.flip(array_in.reshape(shape), axis=dim_index + 1)
    return folded.reshape(array_in.shape)


def gelu_parts(pre):
    factor = math.sqrt(2.0 / math.pi)
    tangent = jnp.tanh(factor * (pre + 0.044715 * pre * pre * pre))
    active = 0.5 * pre * (1.0 + tangent)
    slope = 0.5 * (1.0 + tangent) + 0.5 * pre * (1.0 - tangent * tangent) * factor * (
        1.0 + 3.0 * 0.044715 * pre * pre
    )
    return (active, slope)


def shards(inputs, cotangent, w_in, w_out, u_in, v_in, u_out, v_out):
    row_count, col_count = inputs.shape
    local_blocks = w_in.shape[0]
    slot_count = w_in.shape[1]
    block_size = w_in.shape[2]
    local_bits = local_blocks.bit_length() - 1
    far_bits = slot_count - 1 - local_bits
    my_index = lax.axis_index("feat")

    def far_blocks(blocks):
        whole = lax.all_gather(blocks, "feat", axis=1, tiled=True)
        grouped = whole.reshape(row_count, lax.axis_size("feat"), local_blocks, block_size)
        return [
            lax.dynamic_index_in_dim(grouped, my_index ^ 1 << level, 1, keepdims=False)
            for level in range(far_bits)
        ]

    def stack_partners(blocks, remote_blocks):
        parts = (
            [blocks] + [flip_level(blocks, level, 1) for level in range(local_bits)] + remote_blocks
        )
        return jnp.stack(parts, axis=2)

    def apply_back(grads, weights):
        grad_parts = [grads] + [flip_level(grads, level, 1) for level in range(local_bits)]
        weight_parts = [weights[:, 0]] + [
            flip_level(weights[:, 1 + level], level, 0) for level in range(local_bits)
        ]
        for level in range(far_bits):
            got_grad, got_weight = partner(
                (grads, weights[:, 1 + local_bits + level]), "feat", level
            )
            grad_parts.append(got_grad)
            weight_parts.append(got_weight)
        stacked = jnp.stack(grad_parts, axis=2)
        moved = jnp.stack(weight_parts, axis=1)
        return jnp.einsum(
            "tisc,isbc->tib", stacked, moved, preferred_element_type=jnp.float32
        ).reshape(row_count, col_count)

    blocks_in = inputs.reshape(row_count, local_blocks, block_size)
    stacked_in = stack_partners(blocks_in, far_blocks(blocks_in))
    code_in = lax.psum(
        jnp.dot(inputs, u_in, preferred_element_type=jnp.float32).astype(jnp.bfloat16), "feat"
    )
    pre = jnp.einsum(
        "tisb,isbc->tic", stacked_in, w_in, preferred_element_type=jnp.float32
    ).reshape(row_count, col_count)
    pre = pre + jnp.dot(code_in, v_in, preferred_element_type=jnp.float32)
    active, slope = gelu_parts(pre)
    act = active.astype(jnp.bfloat16)
    act_blocks = act.reshape(row_count, local_blocks, block_size)
    stacked_act = stack_partners(act_blocks, far_blocks(act_blocks))
    code_out = lax.psum(
        jnp.dot(act, u_out, preferred_element_type=jnp.float32).astype(jnp.bfloat16), "feat"
    )
    result = jnp.einsum(
        "tisb,isbc->tic", stacked_act, w_out, preferred_element_type=jnp.float32
    ).reshape(row_count, col_count)
    result = (result + jnp.dot(code_out, v_out, preferred_element_type=jnp.float32)).astype(
        jnp.bfloat16
    )
    cot_blocks = cotangent.reshape(row_count, local_blocks, block_size)
    back_out = lax.psum(
        jnp.dot(cotangent, v_out.T, preferred_element_type=jnp.float32).astype(jnp.bfloat16), "feat"
    )
    act_grad = apply_back(cot_blocks, w_out) + jnp.dot(
        back_out, u_out.T, preferred_element_type=jnp.float32
    )
    pre_grad = (act_grad * slope).astype(jnp.bfloat16)
    pre_blocks = pre_grad.reshape(row_count, local_blocks, block_size)
    out_grads = (
        jnp.einsum("tosb,toc->osbc", stacked_act, cot_blocks, preferred_element_type=jnp.float32),
        jnp.dot(act.T, back_out, preferred_element_type=jnp.float32),
        jnp.dot(code_out.T, cotangent, preferred_element_type=jnp.float32),
    )
    back_in = lax.psum(
        jnp.dot(pre_grad, v_in.T, preferred_element_type=jnp.float32).astype(jnp.bfloat16), "feat"
    )
    in_grad = (
        apply_back(pre_blocks, w_in) + jnp.dot(back_in, u_in.T, preferred_element_type=jnp.float32)
    ).astype(jnp.bfloat16)
    in_grads = (
        jnp.einsum("tosb,toc->osbc", stacked_in, pre_blocks, preferred_element_type=jnp.float32),
        jnp.dot(inputs.T, back_in, preferred_element_type=jnp.float32),
        jnp.dot(code_in.T, pre_grad, preferred_element_type=jnp.float32),
    )
    summed = (
        lax.psum_scatter(
            in_grads[0].astype(jnp.bfloat16), ("tok", "sub"), scatter_dimension=2, tiled=True
        ).astype(jnp.float32),
        lax.psum_scatter(
            out_grads[0].astype(jnp.bfloat16), ("tok", "sub"), scatter_dimension=2, tiled=True
        ).astype(jnp.float32),
        lax.psum_scatter(
            in_grads[1].astype(jnp.bfloat16), ("tok", "sub"), scatter_dimension=1, tiled=True
        ).astype(jnp.float32),
        lax.psum_scatter(
            in_grads[2].astype(jnp.bfloat16), ("tok", "sub"), scatter_dimension=0, tiled=True
        ).astype(jnp.float32),
        lax.psum_scatter(
            out_grads[1].astype(jnp.bfloat16), ("tok", "sub"), scatter_dimension=1, tiled=True
        ).astype(jnp.float32),
        lax.psum_scatter(
            out_grads[2].astype(jnp.bfloat16), ("tok", "sub"), scatter_dimension=0, tiled=True
        ).astype(jnp.float32),
    )
    grad_w_in, grad_w_out, grad_u_in, grad_v_in, grad_u_out, grad_v_out = summed
    return (result, in_grad, grad_w_in, grad_w_out, grad_u_in, grad_v_in, grad_u_out, grad_v_out)


def solution(mesh):
    placed = (
        P(("group", "tok", "sub"), "feat"),
        P(("group", "tok", "sub"), "feat"),
        P("feat", None, None, None),
        P("feat", None, None, None),
        P("feat", None),
        P(None, "feat"),
        P("feat", None),
        P(None, "feat"),
    )
    return jax.shard_map(
        shards,
        mesh=mesh,
        in_specs=placed,
        out_specs=(
            P(("group", "tok", "sub"), "feat"),
            P(("group", "tok", "sub"), "feat"),
            P(("group", "feat"), None, ("tok", "sub"), None),
            P(("group", "feat"), None, ("tok", "sub"), None),
            P(("group", "feat"), ("tok", "sub")),
            P(("group", "tok", "sub"), "feat"),
            P(("group", "feat"), ("tok", "sub")),
            P(("group", "tok", "sub"), "feat"),
        ),
        check_vma=False,
    )
```

profile of v0, /device:TPU:0, one launch (start us, length us, event | category | flops | bytes accessed | tf_op | source)
XLA Modules:
  0.0 509.5 jit_solution(9896155615454637409)
XLA Ops:
  7.3 2.6 convolution_convert_fusion.7
  17.2 3.0 collective-permute-start.4
  20.3 2.6 collective-permute-start.5
  22.9 4.3 slice_bitcast_fusion
  98.5 2.7 fusion.15
  105.2 2.6 bitcast_dynamic-update-slice_fusion.3
  110.3 6.9 %fusion.14 = f32[16,128,256,1]{2,1,3,0:T(8,128)} fusion(bf16[16,7,128,128]{3,2,1,0:T(8,128)(2,1)S(1)} %copy-done.15, bf16[256,16,7,128]{3,0,2,1:T(8,128)(2,1)} %bitcast_dynamic-update-slice_fusion.2), kind=kOutput, calls=%fused_computation.79 | convolution fusion | flops 939524096 | bytes 13107200 | tf_op jit(solution)/shard_map/tisc,isbc->tib/dot_general | solution.py:73
  117.2 2.9 copy.107
  120.1 57.3 %all-gather.3.cloned.1.call-done = bf16[256,64,128]{2,1,0:T(8,128)(2,1)} async-done(((bf16[256,16,128]{2,1,0:T(8,128)(2,1)}), bf16[256,64,128]{2,1,0:T(8,128)(2,1)}) %all-gather.3.cloned.1.call-update) | async-done | bytes 4194320 | tf_op jit(solution)/shard_map/all_gather | solution.py:47
  177.4 4.9 copy.58
  185.0 7.0 %fusion.12 = f32[16,256,128,1]{1,2,3,0:T(8,128)} fusion(bf16[256,16,7,128]{3,0,2,1:T(8,128)(2,1)} %bitcast_dynamic-update-slice_fusion.4, bf16[16,7,128,128]{3,2,1,0:T(8,128)(2,1)S(1)} %copy-done.10), kind=kOutput, calls=%fused_computation.77 | convolution fusion | flops 939524096 | bytes 13107200 | tf_op jit(solution)/shard_map/tisb,isbc->tic/dot_general | solution.py:82
  192.0 3.4 copy.61
  208.2 26.6 %all-reduce.5.cloned.1.call-done = (bf16[256,128]{1,0:T(8,128)(2,1)}, bf16[256,128]{1,0:T(8,128)(2,1)}) async-done(((bf16[256,128]{1,0:T(8,128)(2,1)}, bf16[256,128]{1,0:T(8,128)(2,1)}), (bf16[256,128]{1,0:T(8,128)(2,1)}, bf16[256,128]{1,0:T(8,128)(2,1)})) %all-reduce.5.cloned.1.call-update) | async-done | bytes 131088 | tf_op jit(solution)/shard_map/psum | solution.py:90
  240.7 7.5 %convolution_convert_fusion.1 = bf16[16,7,128,128]{3,2,1,0:T(8,128)(2,1)} fusion(bf16[256,16,7,128]{3,0,2,1:T(8,128)(2,1)} %bitcast_dynamic-update-slice_fusion.4, bf16[256,16,128,1]{2,1,0,3:T(8,128)(2,1)S(1)} %bitcast.190), kind=kOutput, calls=%fused_computation.6 | convolution fusion | flops 941359104 | bytes 12058624 | tf_op jit(solution)/shard_map/tosb,toc->osbc/dot_general | solution.py:120
  254.2 10.3 %rev.84 = bf16[256,8,2,1,128]{4,2,1,0,3:T(2,128)(2,1)} reverse(bf16[256,8,2,1,128]{4,2,1,0,3:T(2,128)(2,1)} %reshape_reshape.52), dimensions={2} | reverse | bytes 2097152 | tf_op jit(solution)/shard_map/jit(_flip)/rev | solution.py:23
  286.3 30.9 %all-gather.5.cloned.1.call-done = bf16[256,64,128]{2,1,0:T(8,128)(2,1)} async-done(((bf16[256,16,128]{2,1,0:T(8,128)(2,1)}), bf16[256,64,128]{2,1,0:T(8,128)(2,1)}) %all-gather.5.cloned.1.call-update) | async-done | bytes 4194320 | tf_op jit(solution)/shard_map/all_gather | solution.py:47
  321.7 7.3 %convolution_convert_fusion = bf16[16,7,128,128]{3,2,1,0:T(8,128)(2,1)} fusion(bf16[256,16,7,128]{3,0,2,1:T(8,128)(2,1)} %fusion.9, bf16[256,16,128,1]{0,2,3,1:T(8,128)(2,1)S(1)} %bitcast.189), kind=kOutput, calls=%fused_computation.5 | convolution fusion | flops 941359104 | bytes 12058624 | tf_op jit(solution)/shard_map/tosb,toc->osbc/dot_general | solution.py:109
  329.0 4.4 slice_bitcast_fusion.2
  340.0 16.7 %collective-permute-done = bf16[16,128,128]{2,1,0:T(8,128)(2,1)} collective-permute-done((bf16[16,128,128]{2,1,0:T(8,128)(2,1)}, bf16[16,128,128]{2,1,0:T(8,128)(2,1)}, u32[]{:S(2)}, u32[]{:S(2)}) %collective-permute-start) | collective-permute-done | bytes 524320 | tf_op jit(solution)/shard_map/ppermute | solution.py:12
  366.5 10.2 %rev.100 = bf16[256,8,2,1,128]{4,2,1,0,3:T(2,128)(2,1)} reverse(bf16[256,8,2,1,128]{4,2,1,0,3:T(2,128)(2,1)} %reshape_reshape.60), dimensions={2} | reverse | bytes 2097152 | tf_op jit(solution)/shard_map/jit(_flip)/rev | solution.py:23
  383.9 2.9 rev.101
  401.4 9.1 %collective-permute-done.6 = bf16[256,16,128]{2,0,1:T(8,128)(2,1)} collective-permute-done((bf16[256,16,128]{2,0,1:T(8,128)(2,1)}, bf16[256,16,128]{2,0,1:T(8,128)(2,1)}, u32[]{:S(2)}, u32[]{:S(2)}) %collective-permute-start.6) | collective-permute-done | bytes 1048608 | tf_op jit(solution)/shard_map/ppermute | solution.py:12
  415.4 6.9 %fusion.16 = f32[16,128,256,1]{2,1,3,0:T(8,128)} fusion(bf16[16,7,128,128]{3,2,1,0:T(8,128)(2,1)S(1)} %copy-done.16, bf16[256,16,7,128]{3,0,2,1:T(8,128)(2,1)} %bitcast_dynamic-update-slice_fusion), kind=kOutput, calls=%fused_computation.81 | convolution fusion | flops 939524096 | bytes 13107200 | tf_op jit(solution)/shard_map/tisc,isbc->tib/dot_general | solution.py:73
  422.3 3.4 copy.92
  429.0 3.5 add_convert_fusion
  435.8 8.1 %fusion.13 = f32[16,256,128,1]{1,2,3,0:T(8,128)} fusion(bf16[256,16,7,128]{3,0,2,1:T(8,128)(2,1)} %fusion.9, bf16[16,7,128,128]{3,2,1,0:T(8,128)(2,1)} %param.11), kind=kOutput, calls=%fused_computation.78 | convolution fusion | flops 939524096 | bytes 13107200 | tf_op jit(solution)/shard_map/tisb,isbc->tic/dot_general | solution.py:93
  443.8 3.0 copy.70
  446.8 3.0 fusion
  449.9 6.1 %reduce-scatter.7.cloned.1.call-done = bf16[16,7,32,128]{3,2,1,0:T(8,128)(2,1)} async-done(((bf16[16,7,128,128]{3,2,1,0:T(8,128)(2,1)}), bf16[16,7,32,128]{3,2,1,0:T(8,128)(2,1)}) %reduce-scatter.7.cloned.1.call-update) | async-done | bytes 917520 | tf_op jit(solution)/shard_map/reduce_scatter | solution.py:125
  455.9 2.7 convert_element_type.72
  458.6 41.2 %reduce-scatter.9.cloned.1.call-done = bf16[16,7,32,128]{3,2,1,0:T(8,128)(2,1)} async-done(((bf16[16,7,128,128]{3,2,1,0:T(8,128)(2,1)}), bf16[16,7,32,128]{3,2,1,0:T(8,128)(2,1)}) %reduce-scatter.9.cloned.1.call-update) | async-done | bytes 917520 | tf_op jit(solution)/shard_map/reduce_scatter | solution.py:128
  499.7 2.7 convert_element_type.74
  (228 shorter events, 188.0 us)
Async XLA Ops:
  7.2 188.3 %copy-start = (bf16[128,2048]{1,0:T(8,128)(2,1)S(1)}, bf16[128,2048]{1,0:T(8,128)(2,1)}, u32[]{:S(2)}) copy-start(bf16[128,2048]{1,0:T(8,128)(2,1)} %param.13) | copy-start | bytes 1572868
  7.2 6.5 %copy-start.3 = (bf16[256,2048]{1,0:T(8,128)(2,1)S(1)}, bf16[256,2048]{1,0:T(8,128)(2,1)}, u32[]{:S(2)}) copy-start(bf16[256,2048]{1,0:T(8,128)(2,1)} %param.9) | copy-start | bytes 3145732
  7.2 5.1 %copy-start.2 = (bf16[256,2048]{1,0:T(8,128)(2,1)S(1)}, bf16[256,2048]{1,0:T(8,128)(2,1)}, u32[]{:S(2)}) copy-start(bf16[256,2048]{1,0:T(8,128)(2,1)} %param.8) | copy-start | bytes 3145732
  7.2 91.3 %all-reduce.7.cloned.1.call-start = ((), (), s32[]{:S(2)}) async-start(), calls=%async_computation.15 | async-start | bytes 262144 | tf_op jit(solution)/shard_map/psum | solution.py:79
  12.3 165.2 %all-gather.3.cloned.1.call-start = ((), (), s32[]{:S(2)}) async-start(), calls=%async_computation.6 | async-start | bytes 5242880 | tf_op jit(solution)/shard_map/all_gather | solution.py:47
  13.6 221.3 %all-reduce.5.cloned.1.call-start = ((), (), s32[]{:S(2)}) async-start(), calls=%async_computation.14 | async-start | bytes 262144 | tf_op jit(solution)/shard_map/psum | solution.py:90
  17.2 88.0 %collective-permute-start.4 = (bf16[256,16,128]{2,0,1:T(8,128)(2,1)}, bf16[256,16,128]{2,0,1:T(8,128)(2,1)}, u32[]{:S(2)}, u32[]{:S(2)}) collective-permute-start(bf16[256,16,128]{2,0,1:T(8,128)(2,1)} %copy.81), channel_id=1, source_target_pairs={{0,4},{4,0},{8,12},{12,8},{1,5},{5,1},{9,13},{13,9},{2,6},{6,2},{1... | collective-permute-start | bytes 3145736 | tf_op jit(solution)/shard_map/ppermute | solution.py:12
  20.3 87.5 %collective-permute-start.5 = (bf16[256,16,128]{2,0,1:T(8,128)(2,1)}, bf16[256,16,128]{2,0,1:T(8,128)(2,1)}, u32[]{:S(2)}, u32[]{:S(2)}) collective-permute-start(bf16[256,16,128]{2,0,1:T(8,128)(2,1)} %copy.81), channel_id=1, source_target_pairs={{0,8},{4,12},{8,0},{12,4},{1,9},{5,13},{9,1},{13,5},{2,10},{6,14},... | collective-permute-start | bytes 3145736 | tf_op jit(solution)/shard_map/ppermute | solution.py:12
  27.2 74.0 %collective-permute-start.2 = (bf16[16,128,128]{2,1,0:T(8,128)(2,1)}, bf16[16,128,128]{2,1,0:T(8,128)(2,1)}, u32[]{:S(2)}, u32[]{:S(2)}) collective-permute-start(bf16[16,128,128]{2,1,0:T(8,128)(2,1)} %get-tuple-element.22), channel_id=1, source_target_pairs={{0,4},{4,0},{8,12},{12,8},{1,5},{5,1},{9,13},{13,9},{2,6},{6,2},{1... | collective-permute-start | bytes 1572872 | tf_op jit(solution)/shard_map/ppermute | solution.py:12
  27.6 75.5 %collective-permute-start.3 = (bf16[16,128,128]{2,1,0:T(8,128)(2,1)}, bf16[16,128,128]{2,1,0:T(8,128)(2,1)}, u32[]{:S(2)}, u32[]{:S(2)}) collective-permute-start(bf16[16,128,128]{2,1,0:T(8,128)(2,1)} %get-tuple-element.21), channel_id=1, source_target_pairs={{0,8},{4,12},{8,0},{12,4},{1,9},{5,13},{9,1},{13,5},{2,10},{6,14},... | collective-permute-start | bytes 1572872 | tf_op jit(solution)/shard_map/ppermute | solution.py:12
  79.9 8.9 %copy-start.34 = (bf16[2,2,4,128,128]{4,3,2,1,0:T(8,128)(2,1)S(1)}, bf16[2,2,4,128,128]{4,3,2,1,0:T(8,128)(2,1)}, u32[]{:S(2)}) copy-start(bf16[2,2,4,128,128]{4,3,2,1,0:T(8,128)(2,1)} %rev.94) | copy-start | bytes 1572868
  84.7 5.0 copy-start.18
  84.7 5.1 %copy-start.25 = (bf16[256,16,1,128]{3,0,2,1:T(8,128)(2,1)S(1)}, bf16[256,16,1,128]{3,0,2,1:T(8,128)(2,1)}, u32[]{:S(2)}) copy-start(bf16[256,16,1,128]{3,0,2,1:T(8,128)(2,1)} %copy.59) | copy-start | bytes 3145732
  84.7 6.3 %copy-start.17 = (bf16[256,8,2,1,128]{4,0,2,1,3:T(8,128)(2,1)S(1)}, bf16[256,8,2,1,128]{4,0,2,1,3:T(8,128)(2,1)}, u32[]{:S(2)}) copy-start(bf16[256,8,2,1,128]{4,0,2,1,3:T(8,128)(2,1)} %rev.96) | copy-start | bytes 3145732
  105.2 5.1 copy-start.15
  202.0 115.2 %all-gather.5.cloned.1.call-start = ((), (), s32[]{:S(2)}) async-start(), calls=%async_computation.7 | async-start | bytes 5242880 | tf_op jit(solution)/shard_map/all_gather | solution.py:47
  204.5 221.2 %reduce-scatter.13.cloned.1.call-start = ((), (), s32[]{:S(2)}) async-start(), calls=%async_computation.11 | async-start | bytes 655360 | tf_op jit(solution)/shard_map/reduce_scatter | solution.py:134
  205.7 221.6 %reduce-scatter.15.cloned.1.call-start = ((), (), s32[]{:S(2)}) async-start(), calls=%async_computation.12 | async-start | bytes 655360 | tf_op jit(solution)/shard_map/reduce_scatter | solution.py:137
  208.2 224.3 %reduce-scatter.11.cloned.1.call-start = ((), (), s32[]{:S(2)}) async-start(), calls=%async_computation.10 | async-start | bytes 655360 | tf_op jit(solution)/shard_map/reduce_scatter | solution.py:131
  236.9 197.3 %reduce-scatter.17.cloned.1.call-start = ((), (), s32[]{:S(2)}) async-start(), calls=%async_computation.13 | async-start | bytes 655360 | tf_op jit(solution)/shard_map/reduce_scatter | solution.py:140
  239.4 216.5 %reduce-scatter.7.cloned.1.call-start = ((), (), s32[]{:S(2)}) async-start(), calls=%async_computation.8 | async-start | bytes 4587520 | tf_op jit(solution)/shard_map/reduce_scatter | solution.py:125
  248.2 251.5 %reduce-scatter.9.cloned.1.call-start = ((), (), s32[]{:S(2)}) async-start(), calls=%async_computation.9 | async-start | bytes 4587520 | tf_op jit(solution)/shard_map/reduce_scatter | solution.py:128
  254.2 12.8 %copy-start.29 = (bf16[256,4,2,2,128]{4,3,2,1,0:T(2,128)(2,1)S(1)}, bf16[256,4,2,2,128]{4,3,2,1,0:T(2,128)(2,1)}, u32[]{:S(2)}) copy-start(bf16[256,4,2,2,128]{4,3,2,1,0:T(2,128)(2,1)} %reshape_reshape.53) | copy-start | bytes 3145732
  268.7 7.6 %copy-start.9 = (bf16[32,8,16,128]{3,2,1,0:T(8,128)(2,1)S(1)}, bf16[32,8,16,128]{3,2,1,0:T(8,128)(2,1)}, u32[]{:S(2)}) copy-start(bf16[32,8,16,128]{3,2,1,0:T(8,128)(2,1)} %copy.121) | copy-start | bytes 3145732
  277.4 5.4 %copy-start.26 = (bf16[256,4,2,2,128]{4,0,3,2,1:T(8,128)(2,1)S(1)}, bf16[256,4,2,2,128]{4,0,3,2,1:T(8,128)(2,1)}, u32[]{:S(2)}) copy-start(bf16[256,4,2,2,128]{4,0,3,2,1:T(8,128)(2,1)} %copy.63) | copy-start | bytes 3145732
  333.4 23.3 %collective-permute-start = (bf16[16,128,128]{2,1,0:T(8,128)(2,1)}, bf16[16,128,128]{2,1,0:T(8,128)(2,1)}, u32[]{:S(2)}, u32[]{:S(2)}) collective-permute-start(bf16[16,128,128]{2,1,0:T(8,128)(2,1)} %get-tuple-element.15), channel_id=1, source_target_pairs={{0,4},{4,0},{8,12},{12,8},{1,5},{5,1},{9,13},{13,9},{2,6},{6,2},{1... | collective-permute-start | bytes 1572872 | tf_op jit(solution)/shard_map/ppermute | solution.py:12
  333.4 26.3 %collective-permute-start.1 = (bf16[16,128,128]{2,1,0:T(8,128)(2,1)}, bf16[16,128,128]{2,1,0:T(8,128)(2,1)}, u32[]{:S(2)}, u32[]{:S(2)}) collective-permute-start(bf16[16,128,128]{2,1,0:T(8,128)(2,1)} %get-tuple-element.14), channel_id=1, source_target_pairs={{0,8},{4,12},{8,0},{12,4},{1,9},{5,13},{9,1},{13,5},{2,10},{6,14},... | collective-permute-start | bytes 1572872 | tf_op jit(solution)/shard_map/ppermute | solution.py:12
  363.2 15.0 %copy-start.8 = (bf16[32,8,16,128]{3,2,1,0:T(8,128)(2,1)S(1)}, bf16[32,8,16,128]{3,2,1,0:T(8,128)(2,1)}, u32[]{:S(2)}) copy-start(bf16[32,8,16,128]{3,2,1,0:T(8,128)(2,1)} %copy-done.7) | copy-start | bytes 3145732
  364.4 46.1 %collective-permute-start.6 = (bf16[256,16,128]{2,0,1:T(8,128)(2,1)}, bf16[256,16,128]{2,0,1:T(8,128)(2,1)}, u32[]{:S(2)}, u32[]{:S(2)}) collective-permute-start(bf16[256,16,128]{2,0,1:T(8,128)(2,1)} %copy_bitcast_fusion), channel_id=1, source_target_pairs={{0,4},{4,0},{8,12},{12,8},{1,5},{5,1},{9,13},{13,9},{2,6},{6,2},{1... | collective-permute-start | bytes 3145736 | tf_op jit(solution)/shard_map/ppermute | solution.py:12
  364.4 48.6 %collective-permute-start.7 = (bf16[256,16,128]{2,0,1:T(8,128)(2,1)}, bf16[256,16,128]{2,0,1:T(8,128)(2,1)}, u32[]{:S(2)}, u32[]{:S(2)}) collective-permute-start(bf16[256,16,128]{2,0,1:T(8,128)(2,1)} %copy_bitcast_fusion), channel_id=1, source_target_pairs={{0,8},{4,12},{8,0},{12,4},{1,9},{5,13},{9,1},{13,5},{2,10},{6,14},... | collective-permute-start | bytes 3145736 | tf_op jit(solution)/shard_map/ppermute | solution.py:12
  399.6 15.8 %copy-start.16 = (bf16[16,7,128,128]{3,2,1,0:T(8,128)(2,1)S(1)}, bf16[16,7,128,128]{3,2,1,0:T(8,128)(2,1)}, u32[]{:S(2)}) copy-start(bf16[16,7,128,128]{3,2,1,0:T(8,128)(2,1)} %bitcast_dynamic-update-slice_fusion.8) | copy-start | bytes 11010052
  446.8 55.6 %copy-start.1 = (bf16[128,2048]{1,0:T(8,128)(2,1)S(1)}, bf16[128,2048]{1,0:T(8,128)(2,1)}, u32[]{:S(2)}) copy-start(bf16[128,2048]{1,0:T(8,128)(2,1)} %param.13) | copy-start | bytes 1572868
  (25 other events, 74.5 us)
Sparse Core Ops, SparseCore 0:
  12.4 83.3 all-reduce.6
  97.4 79.9 all-gather.2
  202.1 32.7 all-reduce.4
  236.9 80.2 all-gather.4
  319.5 19.8 reduce-scatter.12
  341.8 21.6 reduce-scatter.14
  366.0 21.6 reduce-scatter.10
  390.4 21.6 reduce-scatter.16
  414.6 41.2 reduce-scatter.6
  458.5 41.2 reduce-scatter.8
where the time goes:
time: 519 us; the launch traced here: 509 us
  local copies, waits for them, and re-layouts  211 us (41%)
  waiting for transfers between devices  189 us (36%)
  matrix products  68.4 us (13%)
  other arithmetic  16.9 us (3%)
  between operations  14.8 us (3%)
  starting transfers between devices  9.46 us (2%)
    all_gather x2, waiting for transfers between devices, far_blocks(): whole = lax.all_gather(blocks, 'feat', axis=1, tiled=True)  88.2 us
    rev x32, local copies, waits for them, and re-layouts, flip_level(): folded = jnp.flip(array_in.reshape(shape), axis=dim_index + 1)  73.6 us
    unnamed x118, local copies, waits for them, and re-layouts  53 us
    reduce_scatter x1, waiting for transfers between devices, shards(): lax.psum_scatter(out_grads[0].astype(jnp.bfloat16), ('tok', 'sub'), scatt...  41.2 us
    another operation x20, local copies, waits for them, and re-layouts, flip_level(): folded = jnp.flip(array_in.reshape(shape), axis=dim_index + 1)  36.1 us
    ppermute x8, waiting for transfers between devices, partner(): return lax.ppermute(value, axis, pairs)  26.9 us
    psum x1, waiting for transfers between devices, shards(): lax.psum(jnp.dot(act, u_out, preferred_element_type=jnp.float32).astype(j...  26.6 us
    dot_general x2, matrix products, apply_back(): jnp.einsum('tisc,isbc->tib', stacked, moved, preferred_element_type=jnp.f...  13.8 us
  transfers between devices with their start and end apart: 18, of which 8 were waited for; matrix products, arithmetic and copies ran while one was open for 51% of the time, Pallas kernels for 0%

commit v1 on v0

v1 whole, which is shorter than its diff:
```python
import functools
import math

import jax
import jax.numpy as jnp
from jax import lax
from jax.experimental import pallas as pl
from jax.experimental.pallas import tpu as pltpu
from jax.sharding import PartitionSpec as P

F32 = jnp.float32
BF16 = jnp.bfloat16
VMEM_LIMIT = 40 * 1024 * 1024


def exchange(value, axis, mask):
    pairs = [(source, source ^ mask) for source in range(lax.axis_size(axis))]
    return lax.ppermute(value, axis, pairs)


def gelu_parts(pre):
    factor = math.sqrt(2.0 / math.pi)
    square = pre * pre
    tangent = jnp.tanh(factor * (pre + 0.044715 * square * pre))
    active = 0.5 * pre * (1.0 + tangent)
    slope = 0.5 * (1.0 + tangent) + 0.5 * pre * (1.0 - tangent * tangent) * factor * (
        1.0 + 3.0 * 0.044715 * square
    )
    return (active, slope)


def dot(left, right):
    return jnp.dot(left, right, preferred_element_type=F32)


def dot_nt(left, right):
    return lax.dot_general(left, right, (((1,), (1,)), ((), ())), preferred_element_type=F32)


def dot_tn(left, right):
    return lax.dot_general(left, right, (((0,), (0,)), ((), ())), preferred_element_type=F32)


def whole(shape):
    return pl.BlockSpec(shape, lambda g: (0,) * len(shape))


def by_cols(rows, width):
    return pl.BlockSpec((rows, width), lambda g: (0, g))


def by_rows(height, cols):
    return pl.BlockSpec((height, cols), lambda g: (g, 0))


def shape_of(shape, dtype=BF16):
    return jax.ShapeDtypeStruct(shape, dtype)


def call(body, grid, ins, outs, out_shapes, scratch, flops, args, name):
    moved = sum(a.size * a.dtype.itemsize for a in args) + sum(
        math.prod(s.shape) * s.dtype.itemsize for s in out_shapes
    )
    return pl.pallas_call(
        body,
        grid=grid,
        in_specs=ins,
        out_specs=outs,
        out_shape=out_shapes,
        scratch_shapes=scratch,
        compiler_params=pltpu.CompilerParams(vmem_limit_bytes=VMEM_LIMIT),
        cost_estimate=pl.CostEstimate(flops=flops, bytes_accessed=moved, transcendentals=0),
        name=name,
    )(*args)


class Layer:
    def __init__(self, inputs, weights):
        self.rows, self.cols = inputs.shape
        self.blocks, self.slots, self.blk, _ = weights.shape
        self.local = self.blocks.bit_length() - 1
        self.far = self.slots - 1 - self.local
        self.group = min(4, self.blocks)
        self.steps = self.blocks // self.group
        self.width = self.group * self.blk
        self.rank = self.blk

    def cut(self, j):
        return slice(j * self.blk, (j + 1) * self.blk)

    def place(self, g, j, k):
        if k == 0:
            return g * self.group + j
        mask = 1 << (k - 1)
        if mask < self.group:
            return g * self.group + (j ^ mask)
        return (g ^ (mask // self.group)) * self.group + j

    def columns(self, ref, block):
        return ref[:, pl.ds(pl.multiple_of(block * self.blk, self.blk), self.blk)]

    def flops(self, per_block):
        return 2 * self.rows * self.blk * self.blk * self.blocks * per_block

    def first_codes(self, inputs, cotangent, u_in, v_out):
        def body(x_ref, c_ref, u_ref, v_ref, code_ref, back_ref):
            code_ref[...] = dot(x_ref[...], u_ref[...]).astype(BF16)
            back_ref[...] = dot_nt(c_ref[...], v_ref[...]).astype(BF16)

        return call(
            body,
            (1,),
            [whole(inputs.shape), whole(inputs.shape), whole(u_in.shape), whole(v_out.shape)],
            [whole((self.rows, self.rank))] * 2,
            [shape_of((self.rows, self.rank))] * 2,
            [],
            self.flops(2),
            (inputs, cotangent, u_in, v_out),
            "first_codes",
        )

    def far_products(self, grads, weights, after):
        def body(g_ref, w_ref, *refs):
            outs = refs[len(after) :]
            for j in range(self.group):
                block = g_ref[:, self.cut(j)]
                for k in range(self.far):
                    outs[k][:, self.cut(j)] = dot_nt(
                        block, w_ref[j, 1 + self.local + k]
                    ).astype(BF16)

        weight_spec = pl.BlockSpec(
            (self.group, self.slots, self.blk, self.blk), lambda g: (g, 0, 0, 0)
        )
        return call(
            body,
            (self.steps,),
            [by_cols(self.rows, self.width), weight_spec]
            + [pl.BlockSpec(memory_space=pl.ANY)] * len(after),
            [by_cols(self.rows, self.width)] * self.far,
            [shape_of((self.rows, self.cols))] * self.far,
            [],
            self.flops(self.far),
            (grads, weights, *after),
            "far_products",
        )

    def forward(self, acts, far_acts, weights, codes, v, finish, outs, out_shapes, extra, extra_specs, scratch, name):
        n_far, n_codes, n_extra = len(far_acts), len(codes), len(extra)

        def body(a_ref, *refs):
            far_refs, refs = refs[:n_far], refs[n_far:]
            w_ref, refs = refs[0], refs[1:]
            code_refs, refs = refs[:n_codes], refs[n_codes:]
            v_ref, refs = refs[0], refs[1:]
            g = pl.program_id(0)
            code = sum(ref[...].astype(F32) for ref in code_refs).astype(BF16)
            for j in range(self.group):
                parts = [
                    self.columns(a_ref, self.place(g, j, k)) for k in range(1 + self.local)
                ] + [ref[:, self.cut(j)] for ref in far_refs]
                stacked = jnp.concatenate(parts, axis=1)
                weight = w_ref[j].reshape(self.slots * self.blk, self.blk)
                total = dot(stacked, weight) + dot(code, v_ref[:, self.cut(j)])
                finish(g, j, total, refs)

        weight_spec = pl.BlockSpec(
            (self.group, self.slots, self.blk, self.blk), lambda g: (g, 0, 0, 0)
        )
        return call(
            body,
            (self.steps,),
            [whole(acts.shape)]
            + [by_cols(self.rows, self.width)] * n_far
            + [weight_spec]
            + [whole((self.rows, self.rank))] * n_codes
            + [by_cols(self.rank, self.width)]
            + extra_specs,
            outs,
            out_shapes,
            scratch,
            self.flops(self.slots + 2),
            (acts, *far_acts, weights, *codes, v, *extra),
            name,
        )

    def hidden(self, inputs, far_inputs, w_in, codes, v_in, u_out):
        def finish(g, j, pre, refs):
            u_ref, act_ref, slope_ref, code_ref, sum_ref = refs
            active, slope = gelu_parts(pre)
            act = active.astype(BF16)
            act_ref[:, self.cut(j)] = act
            slope_ref[:, self.cut(j)] = slope
            part = dot(act, u_ref[self.cut(j), :])
            if j == 0:
                sum_ref[...] = jnp.where(g == 0, part, sum_ref[...] + part)
            else:
                sum_ref[...] += part
            if j == self.group - 1:
                code_ref[...] = sum_ref[...].astype(BF16)

        return self.forward(
            inputs,
            far_inputs,
            w_in,
            codes,
            v_in,
            finish,
            [by_cols(self.rows, self.width)] * 2 + [whole((self.rows, self.rank))],
            [
                shape_of((self.rows, self.cols)),
                shape_of((self.rows, self.cols), F32),
                shape_of((self.rows, self.rank)),
            ],
            [u_out],
            [by_rows(self.width, self.rank)],
            [pltpu.VMEM((self.rows, self.rank), F32)],
            "hidden",
        )

    def result(self, act, far_acts, w_out, codes, v_out):
        def finish(g, j, total, refs):
            refs[0][:, self.cut(j)] = total.astype(BF16)

        return self.forward(
            act,
            far_acts,
            w_out,
            codes,
            v_out,
            finish,
            [by_cols(self.rows, self.width)],
            [shape_of((self.rows, self.cols))],
            [],
            [],
            [],
            "result",
        )[0]

    def backward(self, grads, weights, codes, u, far_parts, finish, outs, out_shapes, extra, extra_specs, scratch, name):
        n_far, n_codes, n_extra = len(far_parts), len(codes), len(extra)

        def body(g_ref, w_ref, *refs):
            code_refs, refs = refs[:n_codes], refs[n_codes:]
            u_ref, refs = refs[0], refs[1:]
            far_refs, refs = refs[:n_far], refs[n_far:]
            g = pl.program_id(0)
            code = sum(ref[...].astype(F32) for ref in code_refs).astype(BF16)
            for j in range(self.group):
                places = [self.place(g, j, k) for k in range(1 + self.local)]
                stacked = jnp.concatenate(
                    [self.columns(g_ref, place) for place in places] + [code], axis=1
                )
                weight = jnp.concatenate(
                    [w_ref[place, k] for k, place in enumerate(places)] + [u_ref[self.cut(j), :]],
                    axis=1,
                )
                total = dot_nt(stacked, weight)
                for ref in far_refs:
                    total = total + ref[:, self.cut(j)].astype(F32)
                finish(g, j, total, refs)

        return call(
            body,
            (self.steps,),
            [whole(grads.shape), whole(weights.shape)]
            + [whole((self.rows, self.rank))] * n_codes
            + [by_rows(self.width, self.rank)]
            + [by_cols(self.rows, self.width)] * n_far
            + extra_specs,
            outs,
            out_shapes,
            scratch,
            self.flops(2 + self.local),
            (grads, weights, *codes, u, *far_parts, *extra),
            name,
        )

    def hidden_grad(self, cotangent, w_out, backs, u_out, far_parts, slope, v_in, w_in):
        def finish(g, j, total, refs):
            s_ref, v_ref, w_ref, pg_ref, code_ref = refs[:5]
            outs = refs[5 : 5 + self.far]
            sum_ref = refs[-1]
            grad = (total * s_ref[:, self.cut(j)]).astype(BF16)
            pg_ref[:, self.cut(j)] = grad
            for k in range(self.far):
                outs[k][:, self.cut(j)] = dot_nt(grad, w_ref[j, 1 + self.local + k]).astype(BF16)
            part = dot_nt(grad, v_ref[:, self.cut(j)])
            if j == 0:
                sum_ref[...] = jnp.where(g == 0, part, sum_ref[...] + part)
            else:
                sum_ref[...] += part
            if j == self.group - 1:
                code_ref[...] = sum_ref[...].astype(BF16)

        weight_spec = pl.BlockSpec(
            (self.group, self.slots, self.blk, self.blk), lambda g: (g, 0, 0, 0)
        )
        got = self.backward(
            cotangent,
            w_out,
            backs,
            u_out,
            far_parts,
            finish,
            [by_cols(self.rows, self.width), whole((self.rows, self.rank))]
            + [by_cols(self.rows, self.width)] * self.far,
            [shape_of((self.rows, self.cols)), shape_of((self.rows, self.rank))]
            + [shape_of((self.rows, self.cols))] * self.far,
            [slope, v_in, w_in],
            [by_cols(self.rows, self.width), by_cols(self.rank, self.width), weight_spec],
            [pltpu.VMEM((self.rows, self.rank), F32)],
            "hidden_grad",
        )
        return got[0], got[1], got[2:]

    def input_grad(self, pre_grad, w_in, backs, u_in, far_parts):
        def finish(g, j, total, refs):
            refs[0][:, self.cut(j)] = total.astype(BF16)

        return self.backward(
            pre_grad,
            w_in,
            backs,
            u_in,
            far_parts,
            finish,
            [by_cols(self.rows, self.width)],
            [shape_of((self.rows, self.cols))],
            [],
            [],
            [],
            "input_grad",
        )[0]

    def weight_grads(self, acts, far_acts, grads, codes, backs, spot, n_tok, n_sub):
        n_far, n_codes = len(far_acts), len(codes)
        height = self.blk // (n_tok * n_sub)
        parts = self.slots + 2

        def body(spot_ref, a_ref, *refs):
            far_refs, refs = refs[:n_far], refs[n_far:]
            g_ref, refs = refs[0], refs[1:]
            code_refs, refs = refs[:n_codes], refs[n_codes:]
            back_refs, refs = refs[:n_codes], refs[n_codes:]
            outs, hold = refs[:n_sub], refs[n_sub]
            g = pl.program_id(0)
            code = sum(ref[...].astype(F32) for ref in code_refs).astype(BF16)
            back = sum(ref[...].astype(F32) for ref in back_refs).astype(BF16)
            for j in range(self.group):
                stacked = jnp.concatenate(
                    [self.columns(a_ref, self.place(g, j, k)) for k in range(1 + self.local)]
                    + [ref[:, self.cut(j)] for ref in far_refs]
                    + [code],
                    axis=1,
                )
                grad = g_ref[:, self.cut(j)]
                hold[: parts - 1] = dot_tn(stacked, grad).reshape(parts - 1, self.blk, self.blk)
                hold[parts - 1] = dot_tn(back, self.columns(a_ref, self.place(g, j, 0)))
                for m in range(n_tok):
                    for h in range(n_sub):
                        first = ((spot_ref[0] ^ m) * n_sub + (spot_ref[1] ^ h)) * height
                        outs[h][m, j] = hold[
                            :, pl.ds(pl.multiple_of(first, height), height), :
                        ].astype(BF16)

        shape = (n_tok, self.blocks, parts, height, self.blk)
        spec = pl.BlockSpec(
            (n_tok, self.group, parts, height, self.blk), lambda g: (0, g, 0, 0, 0)
        )
        args = (spot, acts, *far_acts, grads, *codes, *backs)
        return call(
            body,
            (self.steps,),
            [pl.BlockSpec(memory_space=pltpu.SMEM), whole(acts.shape)]
            + [by_cols(self.rows, self.width)] * (n_far + 1)
            + [whole((self.rows, self.rank))] * (2 * n_codes),
            [spec] * n_sub,
            [shape_of(shape)] * n_sub,
            [pltpu.VMEM((parts, self.blk, self.blk), F32)],
            self.flops(parts),
            args,
            "weight_grads",
        )

    def core_sums(self, kept, got):
        n_tok, blocks, parts, height, blk = kept.shape
        others = n_tok - 1

        def body(*refs):
            ins, outs = refs[: len(refs) - others], refs[len(refs) - others :]
            for m in range(others):
                outs[m][...] = sum(ref[1 + m].astype(F32) for ref in ins).astype(BF16)

        spec_in = pl.BlockSpec((n_tok, self.group, parts, height, blk), lambda g: (0, g, 0, 0, 0))
        spec_out = pl.BlockSpec((self.group, parts, height, blk), lambda g: (g, 0, 0, 0))
        return call(
            body,
            (self.steps,),
            [spec_in] * (1 + len(got)),
            [spec_out] * others,
            [shape_of((blocks, parts, height, blk))] * others,
            [],
            0,
            (kept, *got),
            "core_sums",
        )

    def last_sums(self, kept, got, arrived):
        n_tok, blocks, parts, height, blk = kept.shape
        n_near, n_far = 1 + len(got), len(arrived)

        def body(*refs):
            near, far, (w_ref, v_ref, u_ref) = refs[:n_near], refs[n_near:-3], refs[-3:]
            for j in range(self.group):
                total = sum(ref[0, j].astype(F32) for ref in near)
                for ref in far:
                    total = total + ref[j].astype(F32)
                w_ref[j] = total[: parts - 2]
                v_ref[:, self.cut(j)] = total[parts - 2]
                u_ref[self.cut(j), :] = total[parts - 1].T

        spec_near = pl.BlockSpec((1, self.group, parts, height, blk), lambda g: (0, g, 0, 0, 0))
        spec_far = pl.BlockSpec((self.group, parts, height, blk), lambda g: (g, 0, 0, 0))
        return call(
            body,
            (self.steps,),
            [spec_near] * n_near + [spec_far] * n_far,
            [
                pl.BlockSpec((self.group, parts - 2, height, blk), lambda g: (g, 0, 0, 0)),
                by_cols(height, self.width),
                by_rows(self.width, height),
            ],
            [
                shape_of((blocks, parts - 2, height, blk), F32),
                shape_of((height, self.cols), F32),
                shape_of((self.cols, height), F32),
            ],
            [],
            0,
            (kept, *got, *arrived),
            "last_sums",
        )


def shards(inputs, cotangent, w_in, w_out, u_in, v_in, u_out, v_out):
    layer = Layer(inputs, w_in)
    n_feat, n_tok, n_sub = (lax.axis_size(name) for name in ("feat", "tok", "sub"))
    spot = jnp.stack([lax.axis_index("tok"), lax.axis_index("sub")]).astype(jnp.int32)

    def to_partners(values):
        return [exchange(value, "feat", 1 << k) for k, value in enumerate(values)]

    def to_all(part):
        return [part] + [exchange(part, "feat", mask) for mask in range(1, n_feat)]

    def summed(parts):
        kept = parts[0]
        got = [exchange(parts[h], "sub", h) for h in range(1, n_sub)]
        sums = layer.core_sums(kept, got) if n_tok > 1 else []
        arrived = [exchange(value, "tok", 1 + m) for m, value in enumerate(sums)]
        return layer.last_sums(kept, got, arrived)

    far_inputs = to_partners([inputs] * layer.far)
    code_part, back_part = layer.first_codes(inputs, cotangent, u_in, v_out)
    codes_in, backs_out = to_all(code_part), to_all(back_part)
    far_cot = to_partners(layer.far_products(cotangent, w_out, far_inputs[:1]))

    act, slope, code_part = layer.hidden(inputs, far_inputs, w_in, codes_in, v_in, u_out)
    far_acts = to_partners([act] * layer.far)
    codes_out = to_all(code_part)

    pre_grad, back_part, products = layer.hidden_grad(
        cotangent, w_out, backs_out, u_out, far_cot, slope, v_in, w_in
    )
    far_pre = to_partners(products)
    backs_in = to_all(back_part)

    parts_in = layer.weight_grads(
        inputs, far_inputs, pre_grad, codes_in, backs_in, spot, n_tok, n_sub
    )
    grad_w_in, grad_v_in, grad_u_in = summed(parts_in)

    output = layer.result(act, far_acts, w_out, codes_out, v_out)
    parts_out = layer.weight_grads(
        act, far_acts, cotangent, codes_out, backs_out, spot, n_tok, n_sub
    )
    grad_w_out, grad_v_out, grad_u_out = summed(parts_out)
    in_grad = layer.input_grad(pre_grad, w_in, backs_in, u_in, far_pre)
    return (output, in_grad, grad_w_in, grad_w_out, grad_u_in, grad_v_in, grad_u_out, grad_v_out)


def solution(mesh):
    placed = (
        P(("group", "tok", "sub"), "feat"),
        P(("group", "tok", "sub"), "feat"),
        P("feat", None, None, None),
        P("feat", None, None, None),
        P("feat", None),
        P(None, "feat"),
        P("feat", None),
        P(None, "feat"),
    )
    return jax.shard_map(
        shards,
        mesh=mesh,
        in_specs=placed,
        out_specs=(
            P(("group", "tok", "sub"), "feat"),
            P(("group", "tok", "sub"), "feat"),
            P(("group", "feat"), None, ("tok", "sub"), None),
            P(("group", "feat"), None, ("tok", "sub"), None),
            P(("group", "feat"), ("tok", "sub")),
            P(("group", "tok", "sub"), "feat"),
            P(("group", "feat"), ("tok", "sub")),
            P(("group", "tok", "sub"), "feat"),
        ),
        check_vma=False,
    )
```

time: 519 us -> 271 us (0.52); the launches traced: 509 us -> 270 us
  local copies, waits for them, and re-layouts: 211 us -> 24.1 us
  matrix products: 68.4 us -> 0 us
  Pallas kernels: 0 us -> 45.5 us
  starting transfers between devices: 9.46 us -> 34.4 us
  waiting for transfers between devices: 189 us -> 165 us
  other arithmetic: 16.9 us -> 0.07 us
  between operations: 14.8 us -> 1 us
    ppermute x8 -> x24, waiting for transfers between devices: 26.9 us -> 165 us  [exchange(): return lax.ppermute(value, axis, pairs)]
    all_gather x2 -> x0, waiting for transfers between devices: 88.2 us -> none  [far_blocks(): whole = lax.all_gather(blocks, 'feat', axis=1, tiled=True)]
    rev x32 -> x0, local copies, waits for them, and re-layouts: 73.6 us -> none  [flip_level(): folded = jnp.flip(array_in.reshape(shape), axis=dim_index + 1)]
    dot_general x18 -> x0, matrix products: 68.4 us -> none  [the longest x2 13.8 us: apply_back(): jnp.einsum('tisc,isbc->tib', stacked, moved, preferred_element_type=jnp.f...]
    another operation x28 -> x0, local copies, waits for them, and re-layouts: 52.3 us -> none  [the longest x20 36.1 us: flip_level(): folded = jnp.flip(array_in.reshape(shape), axis=dim_index + 1)]
    reduce_scatter x6 -> x0, waiting for transfers between devices: 47.2 us -> none  [the longest x1 41.2 us: shards(): lax.psum_scatter(out_grads[0].astype(jnp.bfloat16), ('tok', 'sub'), scatt...]
    pallas_call x0 -> x12, Pallas kernels: none -> 45.5 us  [call(): pl.pallas_call(body, grid=grid, in_specs=ins, out_specs=outs, out_shape=o...]
    unnamed x118 -> x84, local copies, waits for them, and re-layouts: 53 us -> 24.1 us
  transfers between devices with their start and end apart: 18 -> 24, of which waited for: 8 -> 7; matrix products, arithmetic and copies ran while one was open for 51% -> 1% of each run, Pallas kernels for 0% -> 16%
where the time goes in v1:
time: 271 us; the launch traced here: 270 us
  waiting for transfers between devices  165 us (61%)
  Pallas kernels  45.5 us (17%)
  starting transfers between devices  34.4 us (13%)
  local copies, waits for them, and re-layouts  24.1 us (9%)
    ppermute x24, waiting for transfers between devices, exchange(): return lax.ppermute(value, axis, pairs)  165 us
    pallas_call x12, Pallas kernels, call(): pl.pallas_call(body, grid=grid, in_specs=ins, out_specs=outs, out_shape=o...  45.5 us
    ppermute x24, starting transfers between devices, exchange(): return lax.ppermute(value, axis, pairs)  34.4 us
    unnamed x84, local copies, waits for them, and re-layouts  24.1 us
  transfers between devices with their start and end apart: 24, of which 7 were waited for; matrix products, arithmetic and copies ran while one was open for 1% of the time, Pallas kernels for 16%

profile of v1, /device:TPU:0, one launch (start us, length us, event | category | flops | bytes accessed | tf_op | source)
XLA Modules:
  0.0 270.3 jit_solution(16748587531659826726)
XLA Ops:
  0.6 3.1 %collective-permute-start = (bf16[256,2048]{1,0:T(8,128)(2,1)}, bf16[256,2048]{1,0:T(8,128)(2,1)S(1)}, u32[]{:S(2)}, u32[]{:S(2)}) collective-permute-start(bf16[256,2048]{1,0:T(8,128)(2,1)} %a_ref.3), channel_id=1, source_target_pairs={{0,4},{4,0},{8,12},{12,8},{1,5},{5,1},{9,13},{13,9},{2,6},{6,2},{1... | collective-permute-start | bytes 3145736 | tf_op jit(solution)/shard_map/ppermute | solution.py:18
  3.7 2.6 collective-permute-start.1
  12.1 3.9 %collective-permute-start.4 = (bf16[256,128]{1,0:T(8,128)(2,1)S(1)}, bf16[256,128]{1,0:T(8,128)(2,1)S(1)}, u32[]{:S(2)}, u32[]{:S(2)}) collective-permute-start(bf16[256,128]{1,0:T(8,128)(2,1)S(1)} %get-tuple-element.29.refs_3_), channel_id=1, source_target_pairs={{0,12},{4,8},{8,4},{12,0},{1,13},{5,9},{9,5},{13,1},{2,14},{6,10},... | collective-permute-start | bytes 196616 | tf_op jit(solution)/shard_map/ppermute | solution.py:18
  16.0 34.1 %collective-permute-done.refs_0_ = bf16[256,2048]{1,0:T(8,128)(2,1)S(1)} collective-permute-done((bf16[256,2048]{1,0:T(8,128)(2,1)}, bf16[256,2048]{1,0:T(8,128)(2,1)S(1)}, u32[]{:S(2)}, u32[]{:S(2)}) %collective-permute-start) | collective-permute-done | bytes 1048608 | tf_op jit(solution)/shard_map/ppermute | solution.py:18
  50.1 2.0 copy-done
  52.2 2.6 far_products.1
  54.8 3.9 %collective-permute-start.14 = (bf16[256,2048]{1,0:T(8,128)(2,1)}, bf16[256,2048]{1,0:T(8,128)(2,1)}, u32[]{:S(2)}, u32[]{:S(2)}) collective-permute-start(bf16[256,2048]{1,0:T(8,128)(2,1)} %get-tuple-element.34), channel_id=1, source_target_pairs={{0,8},{4,12},{8,0},{12,4},{1,9},{5,13},{9,1},{13,5},{2,10},{6,14},... | collective-permute-start | bytes 3145736 | tf_op jit(solution)/shard_map/ppermute | solution.py:18
  58.7 5.7 %hidden.1 = (bf16[256,2048]{1,0:T(8,128)(2,1)S(1)}, f32[256,2048]{1,0:T(8,128)S(1)}, bf16[256,128]{1,0:T(8,128)(2,1)S(1)}) custom-call(bf16[256,2048]{1,0:T(8,128)(2,1)S(1)} %copy-done.7, bf16[256,2048]{1,0:T(8,128)(2,1)S(1)} %collective-permute-done.refs_0_, bf16[256,2048]{1,0:T(8,128)(2,1)S(1)} %collective-permute-done.1.refs_1_, ...), custom_call_target="tpu_custom_call" | custom-call | flops 1207959552 | bytes 11337728 | tf_op jit(solution)/shard_map/hidden/pallas_call | solution.py:64
  67.2 1.7 collective-permute-start.10
  68.9 79.3 %collective-permute-done.10.refs_1_.refs_8_ = bf16[256,128]{1,0:T(8,128)(2,1)S(1)} collective-permute-done((bf16[256,128]{1,0:T(8,128)(2,1)S(1)}, bf16[256,128]{1,0:T(8,128)(2,1)S(1)}, u32[]{:S(2)}, u32[]{:S(2)}) %collective-permute-start.10) | collective-permute-done | bytes 65568 | tf_op jit(solution)/shard_map/ppermute | solution.py:18
  148.7 5.4 %collective-permute-done.11.refs_2_.refs_9_ = bf16[256,128]{1,0:T(8,128)(2,1)S(1)} collective-permute-done((bf16[256,128]{1,0:T(8,128)(2,1)S(1)}, bf16[256,128]{1,0:T(8,128)(2,1)S(1)}, u32[]{:S(2)}, u32[]{:S(2)}) %collective-permute-start.11) | collective-permute-done | bytes 65568 | tf_op jit(solution)/shard_map/ppermute | solution.py:18
  154.1 2.1 collective-permute-start.12
  156.3 4.4 %collective-permute-done.12.refs_3_.refs_10_ = bf16[256,128]{1,0:T(8,128)(2,1)S(1)} collective-permute-done((bf16[256,128]{1,0:T(8,128)(2,1)S(1)}, bf16[256,128]{1,0:T(8,128)(2,1)S(1)}, u32[]{:S(2)}, u32[]{:S(2)}) %collective-permute-start.12) | collective-permute-done | bytes 65568 | tf_op jit(solution)/shard_map/ppermute | solution.py:18
  160.7 2.5 collective-permute-start.8
  163.1 1.9 collective-permute-start.9
  165.0 2.0 copy-done.1
  170.8 7.9 %hidden_grad.1 = (bf16[256,2048]{1,0:T(8,128)(2,1)S(1)}, bf16[256,128]{1,0:T(8,128)(2,1)S(1)}, bf16[256,2048]{1,0:T(8,128)(2,1)}, bf16[256,2048]{1,0:T(8,128)(2,1)}) custom-call(bf16[256,2048]{1,0:T(8,128)(2,1)S(1)} %copy-done.6, bf16[16,7,128,128]{3,2,1,0:T(8,128)(2,1)S(1)} %copy-done.1, bf16[256,128]{1,0:T(8,128)(2,1)S(1)} %get-tuple-element.32.refs_0_.refs_7_, ...), custom_call_target="tpu_custom_call" | custom-call | flops 805306368 | bytes 17104896 | tf_op jit(solution)/shard_map/hidden_grad/pallas_call | solution.py:64
  178.8 2.4 collective-permute-start.16
  181.3 1.9 collective-permute-start.17
  183.2 5.4 %weight_grads.3 = (bf16[2,16,9,32,128]{4,3,2,1,0:T(8,128)(2,1)S(1)}, bf16[2,16,9,32,128]{4,3,2,1,0:T(8,128)(2,1)S(1)}) custom-call(s32[2]{0:T(128)S(1)} %pad_add_fusion.spot_ref, bf16[256,2048]{1,0:T(8,128)(2,1)S(1)} %get-tuple-element.30.a_ref, bf16[256,2048]{1,0:T(8,128)(2,1)} %collective-permute-done.5.refs_0_, ...), custom_call_target="tpu_custom_call" | custom-call | flops 1207959552 | bytes 9437192 | tf_op jit(solution)/shard_map/weight_grads/pallas_call | solution.py:64
  188.8 5.0 %weight_grads.2 = (bf16[2,16,9,32,128]{4,3,2,1,0:T(8,128)(2,1)S(1)}, bf16[2,16,9,32,128]{4,3,2,1,0:T(8,128)(2,1)S(1)}) custom-call(s32[2]{0:T(128)S(1)} %pad_add_fusion.spot_ref, bf16[256,2048]{1,0:T(8,128)(2,1)S(1)} %copy-done.8, bf16[256,2048]{1,0:T(8,128)(2,1)S(1)} %collective-permute-done.refs_0_, bf16[256,2048]{1,0:T(8,128)(2,1)S(1)} %copy-done.14, ...), custom_call_target="tpu_custom_call" | custom-call | flops 1207959552 | bytes 9437192 | tf_op jit(solution)/shard_map/weight_grads/pallas_call | solution.py:64
  194.4 1.9 core_sums.3
  198.5 1.9 core_sums.2
  201.8 2.6 collective-permute-start.19
  204.5 5.2 %result.1 = bf16[256,2048]{1,0:T(8,128)(2,1)} custom-call(bf16[256,2048]{1,0:T(8,128)(2,1)S(1)} %copy-done.12, bf16[256,2048]{1,0:T(8,128)(2,1)} %collective-permute-done.5.refs_0_, bf16[256,2048]{1,0:T(8,128)(2,1)} %collective-permute-done.6.refs_1_, bf16[16,7,128,128]{3,2,1,0:T(8,128)(2,1)S(1)} %copy-done.2, bf16[256,128]{1,0:T(8,128)(2,1)S(1)} %copy-done.30, ...), custom_call_target="tpu_custom_call" | custom-call | flops 1207959552 | bytes 8650752 | tf_op jit(solution)/shard_map/result/pallas_call | solution.py:64
  209.7 39.3 %collective-permute-done.18.refs_5_ = bf16[256,2048]{1,0:T(8,128)(2,1)S(1)} collective-permute-done((bf16[256,2048]{1,0:T(8,128)(2,1)}, bf16[256,2048]{1,0:T(8,128)(2,1)S(1)}, u32[]{:S(2)}, u32[]{:S(2)}) %collective-permute-start.18) | collective-permute-done | bytes 1048608 | tf_op jit(solution)/shard_map/ppermute | solution.py:18
  249.0 1.7 collective-permute-done.19.refs_6_
  252.9 3.4 %input_grad.1 = bf16[256,2048]{1,0:T(8,128)(2,1)} custom-call(bf16[256,2048]{1,0:T(8,128)(2,1)S(1)} %get-tuple-element.36.g_ref.refs_2_, bf16[16,7,128,128]{3,2,1,0:T(8,128)(2,1)S(1)} %copy-done.4, bf16[256,128]{1,0:T(8,128)(2,1)S(1)} %get-tuple-element.37.refs_0_.refs_7_, bf16[256,128]{1,0:T(8,128)(2,1)S(1)} %collective-permute-done.15.refs_1_.refs_8_, ...), custom_call_target="tpu_custom_call" | custom-call | flops 805306368 | bytes 8650752 | tf_op jit(solution)/shard_map/input_grad/pallas_call | solution.py:64
  256.3 3.8 %last_sums.3 = (f32[16,7,32,128]{3,2,1,0:T(8,128)}, f32[32,2048]{1,0:T(8,128)}, f32[2048,32]{1,0:T(8,128)S(1)}) custom-call(bf16[2,16,9,32,128]{4,3,2,1,0:T(8,128)(2,1)S(1)} %get-tuple-element.43.refs_0_, bf16[2,16,9,32,128]{4,3,2,1,0:T(8,128)(2,1)S(1)} %collective-permute-done.22.refs_1_, bf16[16,9,32,128]{3,2,1,0:T(8,128)(2,1)} %collective-permute-done.23.refs_2_), custom_call_target="tpu_custom_call" | custom-call | bytes 8257536 | tf_op jit(solution)/shard_map/last_sums/pallas_call | solution.py:64
  261.1 2.2 copy.17
  265.0 2.0 last_sums.2
  268.1 2.2 copy.16
  (113 shorter events, 23.1 us)
Async XLA Ops:
  0.6 49.5 %collective-permute-start = (bf16[256,2048]{1,0:T(8,128)(2,1)}, bf16[256,2048]{1,0:T(8,128)(2,1)S(1)}, u32[]{:S(2)}, u32[]{:S(2)}) collective-permute-start(bf16[256,2048]{1,0:T(8,128)(2,1)} %a_ref.3), channel_id=1, source_target_pairs={{0,4},{4,0},{8,12},{12,8},{1,5},{5,1},{9,13},{13,9},{2,6},{6,2},{1... | collective-permute-start | bytes 3145736 | tf_op jit(solution)/shard_map/ppermute | solution.py:18
  3.7 54.9 %collective-permute-start.1 = (bf16[256,2048]{1,0:T(8,128)(2,1)}, bf16[256,2048]{1,0:T(8,128)(2,1)S(1)}, u32[]{:S(2)}, u32[]{:S(2)}) collective-permute-start(bf16[256,2048]{1,0:T(8,128)(2,1)} %a_ref.3), channel_id=1, source_target_pairs={{0,8},{4,12},{8,0},{12,4},{1,9},{5,13},{9,1},{13,5},{2,10},{6,14},... | collective-permute-start | bytes 3145736 | tf_op jit(solution)/shard_map/ppermute | solution.py:18
  10.8 47.8 %copy-start.21 = (bf16[128,2048]{1,0:T(8,128)(2,1)S(1)}, bf16[128,2048]{1,0:T(8,128)(2,1)}, u32[]{:S(2)}) copy-start(bf16[128,2048]{1,0:T(8,128)(2,1)} %refs_8_.3) | copy-start | bytes 1572868
  10.8 47.8 %copy-start.23 = (bf16[2048,128]{1,0:T(8,128)(2,1)S(1)}, bf16[2048,128]{1,0:T(8,128)(2,1)}, u32[]{:S(2)}) copy-start(bf16[2048,128]{1,0:T(8,128)(2,1)} %refs_4_.2) | copy-start | bytes 1572868
  11.6 43.2 %collective-permute-start.2 = (bf16[256,128]{1,0:T(8,128)(2,1)S(1)}, bf16[256,128]{1,0:T(8,128)(2,1)S(1)}, u32[]{:S(2)}, u32[]{:S(2)}) collective-permute-start(bf16[256,128]{1,0:T(8,128)(2,1)S(1)} %get-tuple-element.29.refs_3_), channel_id=1, source_target_pairs={{0,4},{4,0},{8,12},{12,8},{1,5},{5,1},{9,13},{13,9},{2,6},{6,2},{1... | collective-permute-start | bytes 196616 | tf_op jit(solution)/shard_map/ppermute | solution.py:18
  12.1 46.6 %collective-permute-start.3 = (bf16[256,128]{1,0:T(8,128)(2,1)S(1)}, bf16[256,128]{1,0:T(8,128)(2,1)S(1)}, u32[]{:S(2)}, u32[]{:S(2)}) collective-permute-start(bf16[256,128]{1,0:T(8,128)(2,1)S(1)} %get-tuple-element.29.refs_3_), channel_id=1, source_target_pairs={{0,8},{4,12},{8,0},{12,4},{1,9},{5,13},{9,1},{13,5},{2,10},{6,14},... | collective-permute-start | bytes 196616 | tf_op jit(solution)/shard_map/ppermute | solution.py:18
  12.1 46.6 %collective-permute-start.4 = (bf16[256,128]{1,0:T(8,128)(2,1)S(1)}, bf16[256,128]{1,0:T(8,128)(2,1)S(1)}, u32[]{:S(2)}, u32[]{:S(2)}) collective-permute-start(bf16[256,128]{1,0:T(8,128)(2,1)S(1)} %get-tuple-element.29.refs_3_), channel_id=1, source_target_pairs={{0,12},{4,8},{8,4},{12,0},{1,13},{5,9},{9,5},{13,1},{2,14},{6,10},... | collective-permute-start | bytes 196616 | tf_op jit(solution)/shard_map/ppermute | solution.py:18
  54.8 105.9 %collective-permute-start.13 = (bf16[256,2048]{1,0:T(8,128)(2,1)}, bf16[256,2048]{1,0:T(8,128)(2,1)}, u32[]{:S(2)}, u32[]{:S(2)}) collective-permute-start(bf16[256,2048]{1,0:T(8,128)(2,1)} %get-tuple-element.33), channel_id=1, source_target_pairs={{0,4},{4,0},{8,12},{12,8},{1,5},{5,1},{9,13},{13,9},{2,6},{6,2},{1... | collective-permute-start | bytes 3145736 | tf_op jit(solution)/shard_map/ppermute | solution.py:18
  54.8 108.4 %collective-permute-start.14 = (bf16[256,2048]{1,0:T(8,128)(2,1)}, bf16[256,2048]{1,0:T(8,128)(2,1)}, u32[]{:S(2)}, u32[]{:S(2)}) collective-permute-start(bf16[256,2048]{1,0:T(8,128)(2,1)} %get-tuple-element.34), channel_id=1, source_target_pairs={{0,8},{4,12},{8,0},{12,4},{1,9},{5,13},{9,1},{13,5},{2,10},{6,14},... | collective-permute-start | bytes 3145736 | tf_op jit(solution)/shard_map/ppermute | solution.py:18
  65.8 117.4 %copy-start.11 = (bf16[256,2048]{1,0:T(8,128)(2,1)}, bf16[256,2048]{1,0:T(8,128)(2,1)S(1)}, u32[]{:S(2)}) copy-start(bf16[256,2048]{1,0:T(8,128)(2,1)S(1)} %get-tuple-element.30.a_ref) | copy-start | bytes 3145732
  65.8 117.4 %copy-start.29 = (bf16[256,128]{1,0:T(8,128)(2,1)}, bf16[256,128]{1,0:T(8,128)(2,1)S(1)}, u32[]{:S(2)}) copy-start(bf16[256,128]{1,0:T(8,128)(2,1)S(1)} %get-tuple-element.31.refs_3_) | copy-start | bytes 196612
  65.8 117.4 %collective-permute-start.5 = (bf16[256,2048]{1,0:T(8,128)(2,1)S(1)}, bf16[256,2048]{1,0:T(8,128)(2,1)}, u32[]{:S(2)}, u32[]{:S(2)}) collective-permute-start(bf16[256,2048]{1,0:T(8,128)(2,1)S(1)} %get-tuple-element.30.a_ref), channel_id=1, source_target_pairs={{0,4},{4,0},{8,12},{12,8},{1,5},{5,1},{9,13},{13,9},{2,6},{6,2},{1... | collective-permute-start | bytes 3145736 | tf_op jit(solution)/shard_map/ppermute | solution.py:18
  65.9 117.3 %collective-permute-start.6 = (bf16[256,2048]{1,0:T(8,128)(2,1)S(1)}, bf16[256,2048]{1,0:T(8,128)(2,1)}, u32[]{:S(2)}, u32[]{:S(2)}) collective-permute-start(bf16[256,2048]{1,0:T(8,128)(2,1)S(1)} %get-tuple-element.30.a_ref), channel_id=1, source_target_pairs={{0,8},{4,12},{8,0},{12,4},{1,9},{5,13},{9,1},{13,5},{2,10},{6,14},... | collective-permute-start | bytes 3145736 | tf_op jit(solution)/shard_map/ppermute | solution.py:18
  67.2 81.0 %collective-permute-start.10 = (bf16[256,128]{1,0:T(8,128)(2,1)S(1)}, bf16[256,128]{1,0:T(8,128)(2,1)S(1)}, u32[]{:S(2)}, u32[]{:S(2)}) collective-permute-start(bf16[256,128]{1,0:T(8,128)(2,1)S(1)} %get-tuple-element.32.refs_0_.refs_7_), channel_id=1, source_target_pairs={{0,4},{4,0},{8,12},{12,8},{1,5},{5,1},{9,13},{13,9},{2,6},{6,2},{1... | collective-permute-start | bytes 196616 | tf_op jit(solution)/shard_map/ppermute | solution.py:18
  148.2 6.0 %collective-permute-start.11 = (bf16[256,128]{1,0:T(8,128)(2,1)S(1)}, bf16[256,128]{1,0:T(8,128)(2,1)S(1)}, u32[]{:S(2)}, u32[]{:S(2)}) collective-permute-start(bf16[256,128]{1,0:T(8,128)(2,1)S(1)} %get-tuple-element.32.refs_0_.refs_7_), channel_id=1, source_target_pairs={{0,8},{4,12},{8,0},{12,4},{1,9},{5,13},{9,1},{13,5},{2,10},{6,14},... | collective-permute-start | bytes 196616 | tf_op jit(solution)/shard_map/ppermute | solution.py:18
  154.1 6.5 %collective-permute-start.12 = (bf16[256,128]{1,0:T(8,128)(2,1)S(1)}, bf16[256,128]{1,0:T(8,128)(2,1)S(1)}, u32[]{:S(2)}, u32[]{:S(2)}) collective-permute-start(bf16[256,128]{1,0:T(8,128)(2,1)S(1)} %get-tuple-element.32.refs_0_.refs_7_), channel_id=1, source_target_pairs={{0,12},{4,8},{8,4},{12,0},{1,13},{5,9},{9,5},{13,1},{2,14},{6,10},... | collective-permute-start | bytes 196616 | tf_op jit(solution)/shard_map/ppermute | solution.py:18
  160.6 18.1 %collective-permute-start.7 = (bf16[256,128]{1,0:T(8,128)(2,1)S(1)}, bf16[256,128]{1,0:T(8,128)(2,1)S(1)}, u32[]{:S(2)}, u32[]{:S(2)}) collective-permute-start(bf16[256,128]{1,0:T(8,128)(2,1)S(1)} %get-tuple-element.31.refs_3_), channel_id=1, source_target_pairs={{0,4},{4,0},{8,12},{12,8},{1,5},{5,1},{9,13},{13,9},{2,6},{6,2},{1... | collective-permute-start | bytes 196616 | tf_op jit(solution)/shard_map/ppermute | solution.py:18
  160.7 18.2 %collective-permute-start.8 = (bf16[256,128]{1,0:T(8,128)(2,1)S(1)}, bf16[256,128]{1,0:T(8,128)(2,1)S(1)}, u32[]{:S(2)}, u32[]{:S(2)}) collective-permute-start(bf16[256,128]{1,0:T(8,128)(2,1)S(1)} %get-tuple-element.31.refs_3_), channel_id=1, source_target_pairs={{0,8},{4,12},{8,0},{12,4},{1,9},{5,13},{9,1},{13,5},{2,10},{6,14},... | collective-permute-start | bytes 196616 | tf_op jit(solution)/shard_map/ppermute | solution.py:18
  163.1 18.1 %collective-permute-start.9 = (bf16[256,128]{1,0:T(8,128)(2,1)S(1)}, bf16[256,128]{1,0:T(8,128)(2,1)S(1)}, u32[]{:S(2)}, u32[]{:S(2)}) collective-permute-start(bf16[256,128]{1,0:T(8,128)(2,1)S(1)} %get-tuple-element.31.refs_3_), channel_id=1, source_target_pairs={{0,12},{4,8},{8,4},{12,0},{1,13},{5,9},{9,5},{13,1},{2,14},{6,10},... | collective-permute-start | bytes 196616 | tf_op jit(solution)/shard_map/ppermute | solution.py:18
  178.7 10.0 %collective-permute-start.15 = (bf16[256,128]{1,0:T(8,128)(2,1)S(1)}, bf16[256,128]{1,0:T(8,128)(2,1)S(1)}, u32[]{:S(2)}, u32[]{:S(2)}) collective-permute-start(bf16[256,128]{1,0:T(8,128)(2,1)S(1)} %get-tuple-element.37.refs_0_.refs_7_), channel_id=1, source_target_pairs={{0,4},{4,0},{8,12},{12,8},{1,5},{5,1},{9,13},{13,9},{2,6},{6,2},{1... | collective-permute-start | bytes 196616 | tf_op jit(solution)/shard_map/ppermute | solution.py:18
  178.8 9.9 %collective-permute-start.16 = (bf16[256,128]{1,0:T(8,128)(2,1)S(1)}, bf16[256,128]{1,0:T(8,128)(2,1)S(1)}, u32[]{:S(2)}, u32[]{:S(2)}) collective-permute-start(bf16[256,128]{1,0:T(8,128)(2,1)S(1)} %get-tuple-element.37.refs_0_.refs_7_), channel_id=1, source_target_pairs={{0,8},{4,12},{8,0},{12,4},{1,9},{5,13},{9,1},{13,5},{2,10},{6,14},... | collective-permute-start | bytes 196616 | tf_op jit(solution)/shard_map/ppermute | solution.py:18
  181.3 7.4 %collective-permute-start.17 = (bf16[256,128]{1,0:T(8,128)(2,1)S(1)}, bf16[256,128]{1,0:T(8,128)(2,1)S(1)}, u32[]{:S(2)}, u32[]{:S(2)}) collective-permute-start(bf16[256,128]{1,0:T(8,128)(2,1)S(1)} %get-tuple-element.37.refs_0_.refs_7_), channel_id=1, source_target_pairs={{0,12},{4,8},{8,4},{12,0},{1,13},{5,9},{9,5},{13,1},{2,14},{6,10},... | collective-permute-start | bytes 196616 | tf_op jit(solution)/shard_map/ppermute | solution.py:18
  188.6 5.7 %collective-permute-start.22 = (bf16[2,16,9,32,128]{4,3,2,1,0:T(8,128)(2,1)S(1)}, bf16[2,16,9,32,128]{4,3,2,1,0:T(8,128)(2,1)S(1)}, u32[]{:S(2)}, u32[]{:S(2)}) collective-permute-start(bf16[2,16,9,32,128]{4,3,2,1,0:T(8,128)(2,1)S(1)} %get-tuple-element.44), channel_id=1, source_target_pairs={{0,1},{1,0},{2,3},{3,2},{4,5},{5,4},{6,7},{7,6},{8,9},{9,8},{10,11... | collective-permute-start | bytes 7077896 | tf_op jit(solution)/shard_map/ppermute | solution.py:18
  193.8 4.7 %collective-permute-start.20 = (bf16[2,16,9,32,128]{4,3,2,1,0:T(8,128)(2,1)S(1)}, bf16[2,16,9,32,128]{4,3,2,1,0:T(8,128)(2,1)S(1)}, u32[]{:S(2)}, u32[]{:S(2)}) collective-permute-start(bf16[2,16,9,32,128]{4,3,2,1,0:T(8,128)(2,1)S(1)} %get-tuple-element.41), channel_id=1, source_target_pairs={{0,1},{1,0},{2,3},{3,2},{4,5},{5,4},{6,7},{7,6},{8,9},{9,8},{10,11... | collective-permute-start | bytes 7077896 | tf_op jit(solution)/shard_map/ppermute | solution.py:18
  196.3 60.0 %collective-permute-start.23 = (bf16[16,9,32,128]{3,2,1,0:T(8,128)(2,1)}, bf16[16,9,32,128]{3,2,1,0:T(8,128)(2,1)}, u32[]{:S(2)}, u32[]{:S(2)}) collective-permute-start(bf16[16,9,32,128]{3,2,1,0:T(8,128)(2,1)} %core_sums.3), channel_id=1, source_target_pairs={{0,2},{2,0},{1,3},{3,1},{4,6},{6,4},{5,7},{7,5},{8,10},{10,8},{9,1... | collective-permute-start | bytes 3538952 | tf_op jit(solution)/shard_map/ppermute | solution.py:18
  200.5 62.9 %collective-permute-start.21 = (bf16[16,9,32,128]{3,2,1,0:T(8,128)(2,1)}, bf16[16,9,32,128]{3,2,1,0:T(8,128)(2,1)S(1)}, u32[]{:S(2)}, u32[]{:S(2)}) collective-permute-start(bf16[16,9,32,128]{3,2,1,0:T(8,128)(2,1)} %core_sums.2), channel_id=1, source_target_pairs={{0,2},{2,0},{1,3},{3,1},{4,6},{6,4},{5,7},{7,5},{8,10},{10,8},{9,1... | collective-permute-start | bytes 3538952 | tf_op jit(solution)/shard_map/ppermute | solution.py:18
  201.8 47.2 %collective-permute-start.18 = (bf16[256,2048]{1,0:T(8,128)(2,1)}, bf16[256,2048]{1,0:T(8,128)(2,1)S(1)}, u32[]{:S(2)}, u32[]{:S(2)}) collective-permute-start(bf16[256,2048]{1,0:T(8,128)(2,1)} %get-tuple-element.38), channel_id=1, source_target_pairs={{0,4},{4,0},{8,12},{12,8},{1,5},{5,1},{9,13},{13,9},{2,6},{6,2},{1... | collective-permute-start | bytes 3145736 | tf_op jit(solution)/shard_map/ppermute | solution.py:18
  201.8 49.8 %copy-start.4 = (bf16[16,7,128,128]{3,2,1,0:T(8,128)(2,1)S(1)}, bf16[16,7,128,128]{3,2,1,0:T(8,128)(2,1)}, u32[]{:S(2)}) copy-start(bf16[16,7,128,128]{3,2,1,0:T(8,128)(2,1)} %w_ref.5) | copy-start | bytes 11010052
  201.8 49.8 %copy-start.18 = (bf16[2048,128]{1,0:T(8,128)(2,1)S(1)}, bf16[2048,128]{1,0:T(8,128)(2,1)}, u32[]{:S(2)}) copy-start(bf16[2048,128]{1,0:T(8,128)(2,1)} %refs_4_.3) | copy-start | bytes 1572868
  201.8 49.8 %copy-start.38 = (bf16[256,128]{1,0:T(8,128)(2,1)S(1)}, bf16[256,128]{1,0:T(8,128)(2,1)}, u32[]{:S(2)}) copy-start(bf16[256,128]{1,0:T(8,128)(2,1)} %copy-done.37) | copy-start | bytes 196612
  201.8 49.8 %copy-start.40 = (bf16[256,128]{1,0:T(8,128)(2,1)S(1)}, bf16[256,128]{1,0:T(8,128)(2,1)}, u32[]{:S(2)}) copy-start(bf16[256,128]{1,0:T(8,128)(2,1)} %copy-done.39) | copy-start | bytes 196612
  201.8 48.8 %collective-permute-start.19 = (bf16[256,2048]{1,0:T(8,128)(2,1)}, bf16[256,2048]{1,0:T(8,128)(2,1)S(1)}, u32[]{:S(2)}, u32[]{:S(2)}) collective-permute-start(bf16[256,2048]{1,0:T(8,128)(2,1)} %get-tuple-element.39), channel_id=1, source_target_pairs={{0,8},{4,12},{8,0},{12,4},{1,9},{5,13},{9,1},{13,5},{2,10},{6,14},... | collective-permute-start | bytes 3145736 | tf_op jit(solution)/shard_map/ppermute | solution.py:18
  (33 other events, 172.1 us)

commit v2 on v1

v2 whole, which is shorter than its diff:
```python
import math

import jax
import jax.numpy as jnp
from jax import lax
from jax.experimental import pallas as pl
from jax.experimental.pallas import tpu as pltpu
from jax.sharding import PartitionSpec as P

F32 = jnp.float32
BF16 = jnp.bfloat16
VMEM_LIMIT = 60 * 1024 * 1024


def exchange(value, axis, mask):
    pairs = [(source, source ^ mask) for source in range(lax.axis_size(axis))]
    return lax.ppermute(value, axis, pairs)


def gelu_parts(pre):
    factor = math.sqrt(2.0 / math.pi)
    square = pre * pre
    tangent = jnp.tanh(factor * (pre + 0.044715 * square * pre))
    active = 0.5 * pre * (1.0 + tangent)
    slope = 0.5 * (1.0 + tangent) + 0.5 * pre * (1.0 - tangent * tangent) * factor * (
        1.0 + 3.0 * 0.044715 * square
    )
    return (active, slope)


def dot(left, right):
    return jnp.dot(left, right, preferred_element_type=F32)


def dot_nt(left, right):
    return lax.dot_general(left, right, (((1,), (1,)), ((), ())), preferred_element_type=F32)


def dot_tn(left, right):
    return lax.dot_general(left, right, (((0,), (0,)), ((), ())), preferred_element_type=F32)


def whole(shape):
    return pl.BlockSpec(shape, lambda g: (0,) * len(shape))


def by_cols(rows, width):
    return pl.BlockSpec((rows, width), lambda g: (0, g))


def by_rows(height, cols):
    return pl.BlockSpec((height, cols), lambda g: (g, 0))


def shape_of(shape, dtype=BF16):
    return jax.ShapeDtypeStruct(shape, dtype)


def call(body, grid, ins, outs, out_shapes, scratch, flops, args, name, after=()):
    moved = sum(a.size * a.dtype.itemsize for a in args) + sum(
        math.prod(s.shape) * s.dtype.itemsize for s in out_shapes
    )
    count = len(args)

    def kernel(*refs):
        body(*refs[:count], *refs[count + len(after) :])

    return pl.pallas_call(
        kernel,
        grid=grid,
        in_specs=list(ins) + [pl.BlockSpec(memory_space=pl.ANY)] * len(after),
        out_specs=outs,
        out_shape=out_shapes,
        scratch_shapes=scratch,
        compiler_params=pltpu.CompilerParams(vmem_limit_bytes=VMEM_LIMIT),
        cost_estimate=pl.CostEstimate(flops=flops, bytes_accessed=moved, transcendentals=0),
        name=name,
    )(*args, *after)


def pin(values, *after):
    def body(*refs):
        del refs

    count = len(values)
    anywhere = pl.BlockSpec(memory_space=pl.ANY)
    return pl.pallas_call(
        body,
        in_specs=[anywhere] * (count + len(after)),
        out_specs=[anywhere] * count,
        out_shape=[shape_of(value.shape, value.dtype) for value in values],
        input_output_aliases={i: i for i in range(count)},
        cost_estimate=pl.CostEstimate(flops=0, bytes_accessed=0, transcendentals=0),
        name="pin",
    )(*values, *after)


class Layer:
    def __init__(self, inputs, weights):
        self.rows, self.cols = inputs.shape
        self.blocks, self.slots, self.blk, _ = weights.shape
        self.local = self.blocks.bit_length() - 1
        self.far = self.slots - 1 - self.local
        self.group = min(4, self.blocks)
        self.steps = self.blocks // self.group
        self.width = self.group * self.blk
        self.rank = self.blk

    def cut(self, j):
        return slice(j * self.blk, (j + 1) * self.blk)

    def place(self, g, j, k):
        if k == 0:
            return g * self.group + j
        mask = 1 << (k - 1)
        if mask < self.group:
            return g * self.group + (j ^ mask)
        return (g ^ (mask // self.group)) * self.group + j

    def columns(self, ref, block):
        return ref[:, pl.ds(pl.multiple_of(block * self.blk, self.blk), self.blk)]

    def code_specs(self, codes):
        return [
            pl.BlockSpec((self.rows, self.rank), lambda g, at=at: (at, 0)) for _, at in codes
        ]

    def code_of(self, refs):
        return sum(ref[...].astype(F32) for ref in refs).astype(BF16) if refs else None

    def flops(self, per_block):
        return 2 * self.rows * self.blk * self.blk * self.blocks * per_block

    def first_codes(self, inputs, cotangent, u_in, v_out, after=()):
        def body(x_ref, c_ref, u_ref, v_ref, code_ref):
            code_ref[: self.rows] = dot(x_ref[...], u_ref[...]).astype(BF16)
            code_ref[self.rows :] = dot_nt(c_ref[...], v_ref[...]).astype(BF16)

        return call(
            body,
            (1,),
            [whole(inputs.shape), whole(inputs.shape), whole(u_in.shape), whole(v_out.shape)],
            [whole((2 * self.rows, self.rank))],
            [shape_of((2 * self.rows, self.rank))],
            [],
            self.flops(2),
            (inputs, cotangent, u_in, v_out),
            "first_codes",
            after,
        )[0]

    def far_products(self, grads, weights, after=()):
        def body(g_ref, w_ref, *outs):
            for j in range(self.group):
                block = g_ref[:, self.cut(j)]
                for k in range(self.far):
                    outs[k][:, self.cut(j)] = dot_nt(
                        block, w_ref[j, 1 + self.local + k]
                    ).astype(BF16)

        weight_spec = pl.BlockSpec(
            (self.group, self.slots, self.blk, self.blk), lambda g: (g, 0, 0, 0)
        )
        return call(
            body,
            (self.steps,),
            [by_cols(self.rows, self.width), weight_spec],
            [by_cols(self.rows, self.width)] * self.far,
            [shape_of((self.rows, self.cols))] * self.far,
            [],
            self.flops(self.far),
            (grads, weights),
            "far_products",
            after,
        )

    def forward(self, acts, far_acts, weights, codes, v, finish, outs, out_shapes, extra, extra_specs, scratch, name, after=()):
        n_far, n_codes, n_extra = len(far_acts), len(codes), len(extra)

        def body(a_ref, *refs):
            far_refs, refs = refs[:n_far], refs[n_far:]
            w_ref, refs = refs[0], refs[1:]
            code_refs, refs = refs[:n_codes], refs[n_codes:]
            v_ref, refs = refs[0], refs[1:]
            g = pl.program_id(0)
            code = self.code_of(code_refs)
            for j in range(self.group):
                parts = [
                    self.columns(a_ref, self.place(g, j, k)) for k in range(1 + self.local)
                ] + [ref[:, self.cut(j)] for ref in far_refs]
                stacked = jnp.concatenate(parts, axis=1)
                weight = w_ref[j].reshape(self.slots * self.blk, self.blk)
                total = dot(stacked, weight) + dot(code, v_ref[:, self.cut(j)])
                finish(g, j, total, refs)

        weight_spec = pl.BlockSpec(
            (self.group, self.slots, self.blk, self.blk), lambda g: (g, 0, 0, 0)
        )
        return call(
            body,
            (self.steps,),
            [whole(acts.shape)]
            + [by_cols(self.rows, self.width)] * n_far
            + [weight_spec]
            + self.code_specs(codes)
            + [by_cols(self.rank, self.width)]
            + extra_specs,
            outs,
            out_shapes,
            scratch,
            self.flops(self.slots + 2),
            (acts, *far_acts, weights, *(value for value, _ in codes), v, *extra),
            name,
            after,
        )

    def hidden(self, inputs, far_inputs, w_in, codes, v_in, u_out, after=()):
        def finish(g, j, pre, refs):
            u_ref, act_ref, slope_ref, code_ref, sum_ref = refs
            active, slope = gelu_parts(pre)
            act = active.astype(BF16)
            act_ref[:, self.cut(j)] = act
            slope_ref[:, self.cut(j)] = slope
            part = dot(act, u_ref[self.cut(j), :])
            if j == 0:
                sum_ref[...] = jnp.where(g == 0, part, sum_ref[...] + part)
            else:
                sum_ref[...] += part
            if j == self.group - 1:
                code_ref[...] = sum_ref[...].astype(BF16)

        return self.forward(
            inputs,
            far_inputs,
            w_in,
            codes,
            v_in,
            finish,
            [by_cols(self.rows, self.width)] * 2 + [whole((self.rows, self.rank))],
            [
                shape_of((self.rows, self.cols)),
                shape_of((self.rows, self.cols), F32),
                shape_of((self.rows, self.rank)),
            ],
            [u_out],
            [by_rows(self.width, self.rank)],
            [pltpu.VMEM((self.rows, self.rank), F32)],
            "hidden",
            after,
        )

    def result(self, act, far_acts, w_out, codes, v_out, after=()):
        def finish(g, j, total, refs):
            refs[0][:, self.cut(j)] = total.astype(BF16)

        return self.forward(
            act,
            far_acts,
            w_out,
            codes,
            v_out,
            finish,
            [by_cols(self.rows, self.width)],
            [shape_of((self.rows, self.cols))],
            [],
            [],
            [],
            "result",
            after,
        )[0]

    def backward(self, grads, weights, codes, u, far_parts, finish, outs, out_shapes, extra, extra_specs, scratch, name, after=()):
        n_far, n_codes, n_extra = len(far_parts), len(codes), len(extra)

        def body(g_ref, w_ref, *refs):
            code_refs, refs = refs[:n_codes], refs[n_codes:]
            u_ref, refs = refs[0], refs[1:]
            far_refs, refs = refs[:n_far], refs[n_far:]
            g = pl.program_id(0)
            code = self.code_of(code_refs)
            for j in range(self.group):
                places = [self.place(g, j, k) for k in range(1 + self.local)]
                stacked = jnp.concatenate(
                    [self.columns(g_ref, place) for place in places] + [code], axis=1
                )
                weight = jnp.concatenate(
                    [w_ref[place, k] for k, place in enumerate(places)] + [u_ref[self.cut(j), :]],
                    axis=1,
                )
                total = dot_nt(stacked, weight)
                for ref in far_refs:
                    total = total + ref[:, self.cut(j)].astype(F32)
                finish(g, j, total, refs)

        return call(
            body,
            (self.steps,),
            [whole(grads.shape), whole(weights.shape)]
            + self.code_specs(codes)
            + [by_rows(self.width, self.rank)]
            + [by_cols(self.rows, self.width)] * n_far
            + extra_specs,
            outs,
            out_shapes,
            scratch,
            self.flops(2 + self.local),
            (grads, weights, *(value for value, _ in codes), u, *far_parts, *extra),
            name,
            after,
        )

    def hidden_grad(self, cotangent, w_out, backs, u_out, far_parts, slope, v_in, w_in, code_part, after=()):
        def finish(g, j, total, refs):
            s_ref, v_ref, w_ref, c_ref, pg_ref, code_ref = refs[:6]
            outs = refs[6 : 6 + self.far]
            sum_ref = refs[-1]
            grad = (total * s_ref[:, self.cut(j)]).astype(BF16)
            pg_ref[:, self.cut(j)] = grad
            for k in range(self.far):
                outs[k][:, self.cut(j)] = dot_nt(grad, w_ref[j, 1 + self.local + k]).astype(BF16)
            part = dot_nt(grad, v_ref[:, self.cut(j)])
            if j == 0:
                sum_ref[...] = jnp.where(g == 0, part, sum_ref[...] + part)
            else:
                sum_ref[...] += part
            if j == self.group - 1:
                code_ref[: self.rows] = c_ref[...]
                code_ref[self.rows :] = sum_ref[...].astype(BF16)

        weight_spec = pl.BlockSpec(
            (self.group, self.slots, self.blk, self.blk), lambda g: (g, 0, 0, 0)
        )
        got = self.backward(
            cotangent,
            w_out,
            backs,
            u_out,
            far_parts,
            finish,
            [by_cols(self.rows, self.width), whole((2 * self.rows, self.rank))]
            + [by_cols(self.rows, self.width)] * self.far,
            [shape_of((self.rows, self.cols)), shape_of((2 * self.rows, self.rank))]
            + [shape_of((self.rows, self.cols))] * self.far,
            [slope, v_in, w_in, code_part],
            [
                by_cols(self.rows, self.width),
                by_cols(self.rank, self.width),
                weight_spec,
                whole(code_part.shape),
            ],
            [pltpu.VMEM((self.rows, self.rank), F32)],
            "hidden_grad",
            after,
        )
        return got[0], got[1], got[2:]

    def input_grad(self, pre_grad, w_in, backs, u_in, after=()):
        def finish(g, j, total, refs):
            refs[0][:, self.cut(j)] = total

        return self.backward(
            pre_grad,
            w_in,
            backs,
            u_in,
            [],
            finish,
            [by_cols(self.rows, self.width)],
            [shape_of((self.rows, self.cols), F32)],
            [],
            [],
            [],
            "input_grad",
            after,
        )[0]

    def weight_grads(self, cuts, grads, acts=None, far_acts=(), codes=(), backs=(), u_acts=None, after=()):
        spot, n_tok, n_sub = cuts
        height = self.blk // (n_tok * n_sub)
        n_local = 0 if acts is None else 1 + self.local
        n_stack = n_local + len(far_acts) + (1 if codes else 0)
        parts = n_stack + (1 if backs else 0)

        def body(spot_ref, *refs):
            refs = list(refs)
            take = lambda count: [refs.pop(0) for _ in range(count)]
            (g_ref,) = take(1)
            acts_ref = take(0 if acts is None else 1)
            far_refs = take(len(far_acts))
            code_refs, back_refs = take(len(codes)), take(len(backs))
            u_ref = take(1 if backs else 0)
            outs, hold = refs[:n_sub], refs[n_sub]
            g = pl.program_id(0)
            code, back = self.code_of(code_refs), self.code_of(back_refs)
            for j in range(self.group):
                pieces = [self.columns(acts_ref[0], self.place(g, j, k)) for k in range(n_local)]
                pieces += [ref[:, self.cut(j)] for ref in far_refs]
                pieces += [code] if codes else []
                grad = g_ref[:, self.cut(j)]
                hold[:n_stack] = dot_tn(jnp.concatenate(pieces, axis=1), grad).reshape(
                    n_stack, self.blk, self.blk
                )
                if backs:
                    hold[n_stack] = dot_tn(back, u_ref[0][:, self.cut(j)])
                for m in range(n_tok):
                    for h in range(n_sub):
                        first = ((spot_ref[0] ^ m) * n_sub + (spot_ref[1] ^ h)) * height
                        outs[h][m, j] = hold[
                            :, pl.ds(pl.multiple_of(first, height), height), :
                        ].astype(BF16)

        shape = (n_tok, self.blocks, parts, height, self.blk)
        spec = pl.BlockSpec(
            (n_tok, self.group, parts, height, self.blk), lambda g: (0, g, 0, 0, 0)
        )
        cols = by_cols(self.rows, self.width)
        return call(
            body,
            (self.steps,),
            [pl.BlockSpec(memory_space=pltpu.SMEM), cols]
            + ([] if acts is None else [whole(acts.shape)])
            + [cols] * len(far_acts)
            + self.code_specs(codes)
            + self.code_specs(backs)
            + ([cols] if backs else []),
            [spec] * n_sub,
            [shape_of(shape)] * n_sub,
            [pltpu.VMEM((parts, self.blk, self.blk), F32)],
            self.flops(parts),
            [spot, grads]
            + ([] if acts is None else [acts])
            + list(far_acts)
            + [value for value, _ in (*codes, *backs)]
            + ([u_acts] if backs else []),
            "weight_grads",
            after,
        )

    def core_sums(self, kept, got, after=()):
        n_tok, blocks, parts, height, blk = kept.shape
        others = n_tok - 1

        def body(*refs):
            ins, outs = refs[: len(refs) - others], refs[len(refs) - others :]
            for m in range(others):
                outs[m][...] = sum(ref[1 + m].astype(F32) for ref in ins).astype(BF16)

        spec_in = pl.BlockSpec((n_tok, self.group, parts, height, blk), lambda g: (0, g, 0, 0, 0))
        spec_out = pl.BlockSpec((self.group, parts, height, blk), lambda g: (g, 0, 0, 0))
        return call(
            body,
            (self.steps,),
            [spec_in] * (1 + len(got)),
            [spec_out] * others,
            [shape_of((blocks, parts, height, blk))] * others,
            [],
            0,
            (kept, *got),
            "core_sums",
            after,
        )

    def last_sums(self, sums, targets, after=()):
        sizes = [1 + len(got) + len(arrived) for _, got, arrived in sums]
        near = [1 + len(got) for _, got, _ in sums]
        height, blk = sums[0][0].shape[3:]

        def body(*refs):
            ins, outs = refs[: sum(sizes)], refs[sum(sizes) :]
            for j in range(self.group):
                totals, at = [], 0
                for size, count in zip(sizes, near):
                    totals.append(
                        sum(
                            (ref[0, j] if i < count else ref[j]).astype(F32)
                            for i, ref in enumerate(ins[at : at + size])
                        )
                    )
                    at += size
                for target, ref in zip(targets, outs):
                    if isinstance(target, list):
                        to = 0
                        for which, first, count in target:
                            ref[j, to : to + count] = totals[which][first : first + count]
                            to += count
                    else:
                        ref[:, self.cut(j)] = totals[target[0]][target[1]]

        ins, args = [], []
        for kept, got, arrived in sums:
            n_tok, blocks, parts = kept.shape[:3]
            spec_near = pl.BlockSpec(
                (1, self.group, parts, height, blk), lambda g: (0, g, 0, 0, 0)
            )
            spec_far = pl.BlockSpec((self.group, parts, height, blk), lambda g: (g, 0, 0, 0))
            ins += [spec_near] * (1 + len(got)) + [spec_far] * len(arrived)
            args += [kept, *got, *arrived]
        outs, shapes = [], []
        for target in targets:
            if isinstance(target, list):
                count = sum(c for _, _, c in target)
                outs.append(pl.BlockSpec((self.group, count, height, blk), lambda g: (g, 0, 0, 0)))
                shapes.append(shape_of((self.blocks, count, height, blk), F32))
            else:
                outs.append(by_cols(height, self.width))
                shapes.append(shape_of((height, self.cols), F32))
        return call(body, (self.steps,), ins, outs, shapes, [], 0, args, "last_sums", after)

    def final(self, local, far_parts, after=()):
        def body(l_ref, *refs):
            total = l_ref[...]
            for ref in refs[:-1]:
                total = total + ref[...].astype(F32)
            refs[-1][...] = total.astype(BF16)

        cols = by_cols(self.rows, self.width)
        return call(
            body,
            (self.steps,),
            [cols] * (1 + len(far_parts)),
            [cols],
            [shape_of((self.rows, self.cols))],
            [],
            0,
            (local, *far_parts),
            "final",
            after,
        )[0]


def shards(inputs, cotangent, w_in, w_out, u_in, v_in, u_out, v_out):
    layer = Layer(inputs, w_in)
    n_feat, n_tok, n_sub = (lax.axis_size(name) for name in ("feat", "tok", "sub"))
    spot = jnp.stack([lax.axis_index("tok"), lax.axis_index("sub")]).astype(jnp.int32)
    cuts = (spot, n_tok, n_sub)

    def to_partners(values):
        return [exchange(value, "feat", 1 << k) for k, value in enumerate(values)]

    def to_all(part):
        return [part] + [exchange(part, "feat", mask) for mask in range(1, n_feat)]

    def by_levels(part):
        parts = [part]
        for level in range(n_feat.bit_length() - 1):
            if level:
                part = (parts[0].astype(F32) + parts[1].astype(F32)).astype(BF16)
            parts = [part, exchange(part, "feat", 1 << level)]
        return parts

    def halves(parts):
        return [(value, 0) for value in parts], [(value, 1) for value in parts]

    def block(work, *args):
        shapes = jax.eval_shape(work, *args)
        empty = lambda *_: jax.tree.map(lambda x: jnp.zeros(x.shape, x.dtype), shapes)
        return lax.cond(lax.axis_index("feat") < n_feat, work, empty, *args)

    def summed(parts):
        kept = parts[0]
        got = [exchange(parts[h], "sub", h) for h in range(1, n_sub)]
        sums = layer.core_sums(kept, got) if n_tok > 1 else []
        return kept, got, [exchange(value, "tok", 1 + m) for m, value in enumerate(sums)]

    def start_step(inputs, cotangent, w_out, u_in, v_out):
        products = layer.far_products(cotangent, w_out)
        return products, to_all(layer.first_codes(inputs, cotangent, u_in, v_out))

    def hidden_step(inputs, cotangent, w_in, v_in, u_out, far_inputs, first):
        codes, backs = halves(first)
        act, slope, code = layer.hidden(inputs, far_inputs, w_in, codes, v_in, u_out)
        parts = layer.weight_grads(cuts, cotangent, acts=act, backs=backs, u_acts=act)
        return act, slope, code, summed(parts)

    def grad_step(
        inputs, cotangent, w_in, w_out, v_in, u_out, far_inputs, far_cot, slope, code, first
    ):
        codes, backs = halves(first)
        pre_grad, code, products = layer.hidden_grad(
            cotangent, w_out, backs, u_out, far_cot, slope, v_in, w_in, code
        )
        parts = layer.weight_grads(cuts, pre_grad, acts=inputs, far_acts=far_inputs, codes=codes)
        return pre_grad, by_levels(code), products, summed(parts)

    def last_step(inputs, cotangent, w_in, w_out, v_out, u_in, act, far_acts, last, pre_grad):
        codes, backs = halves(last)
        parts = layer.weight_grads(
            cuts, cotangent, far_acts=far_acts, codes=codes, backs=backs, u_acts=inputs
        )
        output = layer.result(act, far_acts, w_out, codes, v_out, after=parts[:1])
        return output, layer.input_grad(pre_grad, w_in, backs, u_in), summed(parts)

    far_inputs = to_partners([inputs] * layer.far)
    products, first = block(start_step, inputs, cotangent, w_out, u_in, v_out)
    far_cot = to_partners(products)
    act, slope, code, sums_early = block(
        hidden_step, inputs, cotangent, w_in, v_in, u_out, far_inputs, first
    )
    far_acts = to_partners([act] * layer.far)
    pre_grad, last, products, sums_in = block(
        grad_step,
        inputs, cotangent, w_in, w_out, v_in, u_out, far_inputs, far_cot, slope, code, first,
    )
    far_pre = to_partners(pin(products, *far_acts))
    output, local_grad, sums_late = block(
        last_step, inputs, cotangent, w_in, w_out, v_out, u_in, act, far_acts, last, pre_grad
    )
    near, slots = 1 + layer.local, layer.slots
    grad_w_in, grad_v_in = layer.last_sums(
        [sums_in], [[(0, 0, slots)], (0, slots)], after=[output]
    )
    grad_w_out, grad_u_out, grad_v_out, grad_u_in = layer.last_sums(
        [sums_early, sums_late],
        [[(0, 0, near), (1, 0, layer.far)], (0, near), (1, layer.far), (1, layer.far + 1)],
    )
    total = local_grad
    for value in far_pre:
        total = total + value.astype(F32)
    in_grad = total.astype(BF16)
    return (
        output,
        in_grad,
        grad_w_in,
        grad_w_out,
        grad_u_in.T,
        grad_v_in,
        grad_u_out.T,
        grad_v_out,
    )


def solution(mesh):
    placed = (
        P(("group", "tok", "sub"), "feat"),
        P(("group", "tok", "sub"), "feat"),
        P("feat", None, None, None),
        P("feat", None, None, None),
        P("feat", None),
        P(None, "feat"),
        P("feat", None),
        P(None, "feat"),
    )
    return jax.shard_map(
        shards,
        mesh=mesh,
        in_specs=placed,
        out_specs=(
            P(("group", "tok", "sub"), "feat"),
            P(("group", "tok", "sub"), "feat"),
            P(("group", "feat"), None, ("tok", "sub"), None),
            P(("group", "feat"), None, ("tok", "sub"), None),
            P(("group", "feat"), ("tok", "sub")),
            P(("group", "tok", "sub"), "feat"),
            P(("group", "feat"), ("tok", "sub")),
            P(("group", "tok", "sub"), "feat"),
        ),
        check_vma=False,
    )
```

time: 271 us -> 219 us (0.81)
  waiting for transfers between devices: 165 us -> 111 us
  Pallas kernels: 45.5 us -> 74.9 us
  local copies, waits for them, and re-layouts: 24.1 us -> 2.68 us
  starting transfers between devices: 34.4 us -> 24.7 us
  other arithmetic: 0.07 us -> 4.41 us
    ppermute x24 -> x19, waiting for transfers between devices: 165 us -> 111 us  [exchange(): return lax.ppermute(value, axis, pairs)]
    pallas_call x12 -> x15, Pallas kernels: 45.5 us -> 74.9 us  [the longest x14 74.9 us: call(): pl.pallas_call(kernel, grid=grid, in_specs=list(ins) + [pl.BlockSpec(memo...]
    unnamed x84 -> x6, local copies, waits for them, and re-layouts: 24.1 us -> 1.31 us
    ppermute x24 -> x19, starting transfers between devices: 34.4 us -> 24.7 us  [exchange(): return lax.ppermute(value, axis, pairs)]
    convert_element_type x0 -> x2, other arithmetic: none -> 4.34 us  [the longest x1 3.64 us: shards(): in_grad = total.astype(BF16)]
  transfers between devices with their start and end apart: 24 -> 19, of which waited for: 7 -> 12; matrix products, arithmetic and copies ran while one was open for 1% -> 0% of each run, Pallas kernels for 16% -> 34%
where the time goes in v2:
time: 219 us; the launch traced here: 218 us
  waiting for transfers between devices  111 us (51%)
  Pallas kernels  74.9 us (34%)
  starting transfers between devices  24.7 us (11%)
  other arithmetic  4.41 us (2%)
  local copies, waits for them, and re-layouts  2.68 us (1%)
    ppermute x19, waiting for transfers between devices, exchange(): return lax.ppermute(value, axis, pairs)  111 us
    pallas_call x14, Pallas kernels, call(): pl.pallas_call(kernel, grid=grid, in_specs=list(ins) + [pl.BlockSpec(memo...  74.9 us
    ppermute x19, starting transfers between devices, exchange(): return lax.ppermute(value, axis, pairs)  24.7 us
  transfers between devices with their start and end apart: 19, of which 12 were waited for; matrix products, arithmetic and copies ran while one was open for 0% of the time, Pallas kernels for 34%

profile of v2, /device:TPU:0, one launch (start us, length us, event | category | flops | bytes accessed | tf_op | source)
XLA Modules:
  0.0 218.0 jit_solution(2678212267107422624)
XLA Ops:
  0.6 3.1 %collective-permute-start.11 = (bf16[256,2048]{1,0:T(8,128)(2,1)}, bf16[256,2048]{1,0:T(8,128)(2,1)S(1)}, u32[]{:S(2)}, u32[]{:S(2)}) collective-permute-start(bf16[256,2048]{1,0:T(8,128)(2,1)} %param.16), channel_id=1, source_target_pairs={{0,4},{4,0},{8,12},{12,8},{1,5},{5,1},{9,13},{13,9},{2,6},{6,2},{1... | collective-permute-start | bytes 3145736 | tf_op jit(solution)/shard_map/ppermute | solution.py:17
  6.3 55.6 %conditional.4 = (bf16[256,2048]{1,0:T(8,128)(2,1)}, bf16[256,2048]{1,0:T(8,128)(2,1)}, bf16[512,128]{1,0:T(8,128)(2,1)}, bf16[512,128]{1,0:T(8,128)(2,1)}, bf16...) conditional(s32[]{:T(128)} %convert_element_type.24, () %tuple.42, (bf16[256,2048]{1,0:T(8,128)(2,1)}, ...), branch_computations={%region_0.0_spmd, %region_1.0_spmd} | conditional | flops 536870912 | bytes 15859908 | solution.py:557
  6.3 3.3 %first_codes.1 = bf16[512,128]{1,0:T(8,128)(2,1)} custom-call(bf16[256,2048]{1,0:T(8,128)(2,1)} %get-tuple-element.98.refs_0_, bf16[256,2048]{1,0:T(8,128)(2,1)} %get-tuple-element.94.refs_0_.refs_1_, bf16[2048,128]{1,0:T(8,128)(2,1)} %get-tuple-element.99.refs_2_, bf16[128,2048]{1,0:T(8,128)(2,1)} %get-tuple-element.100.refs_3_), custom_call_target="tpu_custom_call" | custom-call | flops 268435456 | bytes 3276800 | tf_op jit(solution)/shard_map/cond/branch_1_fun/first_codes/pallas_call | solution.py:68
  10.1 3.9 %collective-permute-start.2 = (bf16[512,128]{1,0:T(8,128)(2,1)}, bf16[512,128]{1,0:T(8,128)(2,1)}, u32[]{:S(2)}, u32[]{:S(2)}) collective-permute-start(bf16[512,128]{1,0:T(8,128)(2,1)} %first_codes.1), channel_id=1, source_target_pairs={{0,12},{4,8},{8,4},{12,0},{1,13},{5,9},{9,5},{13,1},{2,14},{6,10},... | collective-permute-start | bytes 393224 | tf_op jit(solution)/shard_map/cond/branch_1_fun/ppermute | solution.py:17
  14.0 4.6 %far_products.1 = (bf16[256,2048]{1,0:T(8,128)(2,1)}, bf16[256,2048]{1,0:T(8,128)(2,1)}) custom-call(bf16[256,2048]{1,0:T(8,128)(2,1)S(1)} %copy-done.1, bf16[16,7,128,128]{3,2,1,0:T(8,128)(2,1)} %get-tuple-element.95.refs_1_), custom_call_target="tpu_custom_call" | custom-call | flops 268435456 | bytes 6815744 | tf_op jit(solution)/shard_map/cond/branch_1_fun/far_products/pallas_call | solution.py:68
  18.6 35.4 %collective-permute-done = bf16[512,128]{1,0:T(8,128)(2,1)} collective-permute-done((bf16[512,128]{1,0:T(8,128)(2,1)}, bf16[512,128]{1,0:T(8,128)(2,1)}, u32[]{:S(2)}, u32[]{:S(2)}) %collective-permute-start) | collective-permute-done | bytes 131104 | tf_op jit(solution)/shard_map/cond/branch_1_fun/ppermute | solution.py:17
  54.0 7.9 %collective-permute-done.1 = bf16[512,128]{1,0:T(8,128)(2,1)} collective-permute-done((bf16[512,128]{1,0:T(8,128)(2,1)}, bf16[512,128]{1,0:T(8,128)(2,1)}, u32[]{:S(2)}, u32[]{:S(2)}) %collective-permute-start.1) | collective-permute-done | bytes 131104 | tf_op jit(solution)/shard_map/cond/branch_1_fun/ppermute | solution.py:17
  66.4 41.2 %conditional.5 = (bf16[256,2048]{1,0:T(8,128)(2,1)}, f32[256,2048]{1,0:T(8,128)}, bf16[256,128]{1,0:T(8,128)(2,1)S(1)}, bf16[2,16,6,32,128]{4,3,2,1,0:T(8,128)(2...) conditional(s32[]{:T(128)} %convert_element_type.24, () %tuple.41, ...), branch_computations={%region_2.0_spmd, %region_3.0_spmd} | conditional | flops 2013265920 | bytes 35979428 | solution.py:557
  66.4 8.0 %hidden.1 = (bf16[256,2048]{1,0:T(8,128)(2,1)}, f32[256,2048]{1,0:T(8,128)}, bf16[256,128]{1,0:T(8,128)(2,1)S(1)}) custom-call(bf16[256,2048]{1,0:T(8,128)(2,1)} %get-tuple-element.101.refs_0_, bf16[256,2048]{1,0:T(8,128)(2,1)S(1)} %get-tuple-element.102.refs_1_, bf16[256,2048]{1,0:T(8,128)(2,1)S(1)} %get-tuple-element.103.refs_2_, ...), custom_call_target="tpu_custom_call" | custom-call | flops 1207959552 | bytes 11599872 | tf_op jit(solution)/shard_map/cond/branch_1_fun/hidden/pallas_call | solution.py:68
  74.3 5.8 %weight_grads.3 = (bf16[2,16,6,32,128]{4,3,2,1,0:T(8,128)(2,1)}, bf16[2,16,6,32,128]{4,3,2,1,0:T(8,128)(2,1)}) custom-call(s32[2]{0:T(128)S(1)} %get-tuple-element.114.refs_0_, bf16[256,2048]{1,0:T(8,128)(2,1)S(1)} %copy-done.2, bf16[256,2048]{1,0:T(8,128)(2,1)} %get-tuple-element.248.refs_2_.refs_7_, bf16[512,128]{1,0:T(8,128)(2,1)} %get-tuple-element.105.refs_4_.refs_3_, ...), custom_call_target="tpu_custom_call" | custom-call | flops 805306368 | bytes 6815752 | tf_op jit(solution)/shard_map/cond/branch_1_fun/weight_grads/pallas_call | solution.py:68
  80.2 3.7 %collective-permute-done.3.refs_1_ = bf16[2,16,6,32,128]{4,3,2,1,0:T(8,128)(2,1)} collective-permute-done((bf16[2,16,6,32,128]{4,3,2,1,0:T(8,128)(2,1)}, bf16[2,16,6,32,128]{4,3,2,1,0:T(8,128)(2,1)}, u32[]{:S(2)}, u32[]{:S(2)}) %collective-permute-start.3) | collective-permute-done | bytes 1572896 | tf_op jit(solution)/shard_map/cond/branch_1_fun/ppermute | solution.py:17
  83.9 3.7 %core_sums.3 = bf16[16,6,32,128]{3,2,1,0:T(8,128)(2,1)} custom-call(bf16[2,16,6,32,128]{4,3,2,1,0:T(8,128)(2,1)} %get-tuple-element.251.refs_0_, bf16[2,16,6,32,128]{4,3,2,1,0:T(8,128)(2,1)} %collective-permute-done.3.refs_1_), custom_call_target="tpu_custom_call" | custom-call | bytes 3932160 | tf_op jit(solution)/shard_map/cond/branch_1_fun/core_sums/pallas_call | solution.py:68
  89.1 18.4 %collective-permute-done.4 = bf16[16,6,32,128]{3,2,1,0:T(8,128)(2,1)} collective-permute-done((bf16[16,6,32,128]{3,2,1,0:T(8,128)(2,1)}, bf16[16,6,32,128]{3,2,1,0:T(8,128)(2,1)}, u32[]{:S(2)}, u32[]{:S(2)}) %collective-permute-start.4) | collective-permute-done | bytes 786464 | tf_op jit(solution)/shard_map/cond/branch_1_fun/ppermute | solution.py:17
  110.9 55.5 %conditional.6 = (bf16[256,2048]{1,0:T(8,128)(2,1)}, bf16[512,128]{1,0:T(8,128)(2,1)}, bf16[512,128]{1,0:T(8,128)(2,1)}, bf16[256,2048]{1,0:T(8,128)(2,1)}, bf16...) conditional(s32[]{:T(128)} %convert_element_type.24, () %tuple.45, ...), branch_computations={%region_4.0_spmd, %region_5.0_spmd} | conditional | flops 1879310336 | bytes 50397472 | solution.py:557
  110.9 10.2 %hidden_grad.1 = (bf16[256,2048]{1,0:T(8,128)(2,1)}, bf16[512,128]{1,0:T(8,128)(2,1)}, bf16[256,2048]{1,0:T(8,128)(2,1)}, bf16[256,2048]{1,0:T(8,128)(2,1)}) custom-call(bf16[256,2048]{1,0:T(8,128)(2,1)} %get-tuple-element.118.refs_0_, bf16[16,7,128,128]{3,2,1,0:T(8,128)(2,1)} %get-tuple-element.119.refs_1_, ...), custom_call_target="tpu_custom_call" | custom-call | flops 805306368 | bytes 17498112 | tf_op jit(solution)/shard_map/cond/branch_1_fun/hidden_grad/pallas_call | solution.py:68
  121.1 6.6 %weight_grads.4 = (bf16[2,16,8,32,128]{4,3,2,1,0:T(8,128)(2,1)}, bf16[2,16,8,32,128]{4,3,2,1,0:T(8,128)(2,1)}) custom-call(s32[2]{0:T(128)S(1)} %get-tuple-element.135.refs_0_, bf16[256,2048]{1,0:T(8,128)(2,1)} %get-tuple-element.262.refs_1_, bf16[256,2048]{1,0:T(8,128)(2,1)S(1)} %copy-done.3, bf16[256,2048]{1,0:T(8,128)(2,1)} %get-tuple-element.137.refs_3_, ...), custom_call_target="tpu_custom_call" | custom-call | flops 1073741824 | bytes 8912904 | tf_op jit(solution)/shard_map/cond/branch_1_fun/weight_grads/pallas_call | solution.py:68
  127.7 4.5 %collective-permute-done.9.refs_1_ = bf16[2,16,8,32,128]{4,3,2,1,0:T(8,128)(2,1)} collective-permute-done((bf16[2,16,8,32,128]{4,3,2,1,0:T(8,128)(2,1)}, bf16[2,16,8,32,128]{4,3,2,1,0:T(8,128)(2,1)}, u32[]{:S(2)}, u32[]{:S(2)}) %collective-permute-start.9) | collective-permute-done | bytes 2097184 | tf_op jit(solution)/shard_map/cond/branch_1_fun/ppermute | solution.py:17
  132.2 4.0 %core_sums.4 = bf16[16,8,32,128]{3,2,1,0:T(8,128)(2,1)} custom-call(bf16[2,16,8,32,128]{4,3,2,1,0:T(8,128)(2,1)} %get-tuple-element.267.refs_0_, bf16[2,16,8,32,128]{4,3,2,1,0:T(8,128)(2,1)} %collective-permute-done.9.refs_1_), custom_call_target="tpu_custom_call" | custom-call | bytes 5242880 | tf_op jit(solution)/shard_map/cond/branch_1_fun/core_sums/pallas_call | solution.py:68
  138.3 19.5 %collective-permute-done.7 = bf16[512,128]{1,0:T(8,128)(2,1)S(1)} collective-permute-done((bf16[512,128]{1,0:T(8,128)(2,1)S(1)}, bf16[512,128]{1,0:T(8,128)(2,1)S(1)}, u32[]{:S(2)}, u32[]{:S(2)}) %collective-permute-start.7) | collective-permute-done | bytes 131104 | tf_op jit(solution)/shard_map/cond/branch_1_fun/ppermute | solution.py:17
  160.0 6.4 %collective-permute-done.8 = bf16[512,128]{1,0:T(8,128)(2,1)} collective-permute-done((bf16[512,128]{1,0:T(8,128)(2,1)}, bf16[512,128]{1,0:T(8,128)(2,1)}, u32[]{:S(2)}, u32[]{:S(2)}) %collective-permute-start.8) | collective-permute-done | bytes 131104 | tf_op jit(solution)/shard_map/cond/branch_1_fun/ppermute | solution.py:17
  166.5 3.0 %collective-permute-start.18 = (bf16[256,2048]{1,0:T(8,128)(2,1)}, bf16[256,2048]{1,0:T(8,128)(2,1)}, u32[]{:S(2)}, u32[]{:S(2)}) collective-permute-start(bf16[256,2048]{1,0:T(8,128)(2,1)} %get-tuple-element.214), channel_id=1, source_target_pairs={{0,8},{4,12},{8,0},{12,4},{1,9},{5,13},{9,1},{13,5},{2,10},{6,14},... | collective-permute-start | bytes 3145736 | tf_op jit(solution)/shard_map/ppermute | solution.py:17
  169.5 27.5 %conditional.7 = (bf16[256,2048]{1,0:T(8,128)(2,1)}, f32[256,2048]{1,0:T(8,128)}, bf16[2,16,4,32,128]{4,3,2,1,0:T(8,128)(2,1)}, bf16[2,16,4,32,128]{4,3,2,1,0:T(8,128)(2,1)}, bf16[16,4,32,128]{3,2,1,0:T(8,128)(2,1)}) conditional(s32[]{:T(128)} %convert_element_type.24, () %tuple.40, (s32[2]{0:T(128)S(1)}, bf16[256,2048]{1,0:T(8,128)(2,1)}, ...), branch_computations={%region_6.0_spmd, %region_7.0_spmd} | conditional | flops 2550136832 | bytes 55050452 | solution.py:557
  170.9 5.3 %weight_grads.5 = (bf16[2,16,4,32,128]{4,3,2,1,0:T(8,128)(2,1)}, bf16[2,16,4,32,128]{4,3,2,1,0:T(8,128)(2,1)}) custom-call(s32[2]{0:T(128)S(1)} %get-tuple-element.148.refs_0_, bf16[256,2048]{1,0:T(8,128)(2,1)} %get-tuple-element.149.refs_1_, bf16[256,2048]{1,0:T(8,128)(2,1)} %copy-done.4, bf16[256,2048]{1,0:T(8,128)(2,1)} %copy-done.5, ...), custom_call_target="tpu_custom_call" | custom-call | flops 536870912 | bytes 6815752 | tf_op jit(solution)/shard_map/cond/branch_1_fun/weight_grads/pallas_call | solution.py:68
  176.2 3.0 %collective-permute-done.5.refs_1_ = bf16[2,16,4,32,128]{4,3,2,1,0:T(8,128)(2,1)} collective-permute-done((bf16[2,16,4,32,128]{4,3,2,1,0:T(8,128)(2,1)}, bf16[2,16,4,32,128]{4,3,2,1,0:T(8,128)(2,1)}, u32[]{:S(2)}, u32[]{:S(2)}) %collective-permute-start.5) | collective-permute-done | bytes 1048608 | tf_op jit(solution)/shard_map/cond/branch_1_fun/ppermute | solution.py:17
  179.2 3.5 %core_sums.5 = bf16[16,4,32,128]{3,2,1,0:T(8,128)(2,1)} custom-call(bf16[2,16,4,32,128]{4,3,2,1,0:T(8,128)(2,1)} %get-tuple-element.277.refs_7_.refs_0_, bf16[2,16,4,32,128]{4,3,2,1,0:T(8,128)(2,1)} %collective-permute-done.5.refs_1_), custom_call_target="tpu_custom_call" | custom-call | bytes 2621440 | tf_op jit(solution)/shard_map/cond/branch_1_fun/core_sums/pallas_call | solution.py:68
  184.2 5.2 %input_grad.1 = f32[256,2048]{1,0:T(8,128)} custom-call(bf16[256,2048]{1,0:T(8,128)(2,1)} %get-tuple-element.152.refs_0_, bf16[16,7,128,128]{3,2,1,0:T(8,128)(2,1)S(1)} %copy-done, bf16[512,128]{1,0:T(8,128)(2,1)} %get-tuple-element.145.refs_4_.refs_6_.refs_2_, bf16[512,128]{1,0:T(8,128)(2,1)} %get-tuple-element.146.refs_5_.refs_7_.refs_3_, ...), custom_call_target="tpu_custom_call" | custom-call | flops 805306368 | bytes 7602176 | tf_op jit(solution)/shard_map/cond/branch_1_fun/input_grad/pallas_call | solution.py:68
  189.3 6.4 %result.1 = bf16[256,2048]{1,0:T(8,128)(2,1)} custom-call(bf16[256,2048]{1,0:T(8,128)(2,1)} %get-tuple-element.141.refs_0_, bf16[256,2048]{1,0:T(8,128)(2,1)} %copy-done.4, bf16[256,2048]{1,0:T(8,128)(2,1)} %copy-done.5, bf16[16,7,128,128]{3,2,1,0:T(8,128)(2,1)} %get-tuple-element.144.refs_3_, bf16[512,128]{1,0:T(8,128)(2,1)} %get-tuple-element.145.refs_4_.refs_6_.refs_2_, ...), custom_call_target="tpu_custom_call" | custom-call | flops 1207959552 | bytes 8650752 | tf_op jit(solution)/shard_map/cond/branch_1_fun/result/pallas_call | solution.py:68
  197.0 4.0 %last_sums.2 = (f32[16,7,32,128]{3,2,1,0:T(8,128)}, f32[32,2048]{1,0:T(8,128)}) custom-call(bf16[2,16,8,32,128]{4,3,2,1,0:T(8,128)(2,1)} %get-tuple-element.215.refs_0_, bf16[2,16,8,32,128]{4,3,2,1,0:T(8,128)(2,1)} %get-tuple-element.216.refs_1_, bf16[16,8,32,128]{3,2,1,0:T(8,128)(2,1)} %get-tuple-element.217.refs_2_, ...), custom_call_target="tpu_custom_call" | custom-call | bytes 7340032 | tf_op jit(solution)/shard_map/last_sums/pallas_call | solution.py:68
  201.0 4.3 %last_sums.3 = (f32[16,7,32,128]{3,2,1,0:T(8,128)}, f32[32,2048]{1,0:T(8,128)}, f32[32,2048]{1,0:T(8,128)}, f32[32,2048]{1,0:T(8,128)}) custom-call(bf16[2,16,6,32,128]{4,3,2,1,0:T(8,128)(2,1)} %get-tuple-element.219.refs_0_, bf16[2,16,6,32,128]{4,3,2,1,0:T(8,128)(2,1)} %get-tuple-element.220.refs_1_, bf16[16,6,32,128]{3,2,1,0:T(8,128)(2,1)} %get-tuple-element.221.refs_2_, ...), custom_call_target="tpu_custom_call" | custom-call | bytes 9175040 | tf_op jit(solution)/shard_map/last_sums/pallas_call | solution.py:68
  205.3 6.3 %collective-permute-done.17 = bf16[256,2048]{1,0:T(8,128)(2,1)} collective-permute-done((bf16[256,2048]{1,0:T(8,128)(2,1)}, bf16[256,2048]{1,0:T(8,128)(2,1)}, u32[]{:S(2)}, u32[]{:S(2)}) %collective-permute-start.17) | collective-permute-done | bytes 1048608 | tf_op jit(solution)/shard_map/ppermute | solution.py:17
  211.6 2.8 %collective-permute-done.18 = bf16[256,2048]{1,0:T(8,128)(2,1)} collective-permute-done((bf16[256,2048]{1,0:T(8,128)(2,1)}, bf16[256,2048]{1,0:T(8,128)(2,1)}, u32[]{:S(2)}, u32[]{:S(2)}) %collective-permute-start.18) | collective-permute-done | bytes 1048608 | tf_op jit(solution)/shard_map/ppermute | solution.py:17
  214.4 3.6 %add_convert_fusion.1 = bf16[256,2048]{1,0:T(8,128)(2,1)} fusion(bf16[256,2048]{1,0:T(8,128)(2,1)} %collective-permute-done.18, f32[256,2048]{1,0:T(8,128)} %get-tuple-element.210, bf16[256,2048]{1,0:T(8,128)(2,1)} %collective-permute-done.17), kind=kLoop, calls=%fused_computation.1 | loop fusion | flops 2621440 | bytes 5242880 | tf_op jit(solution)/shard_map/convert_element_type | solution.py:619
  (48 shorter events, 20.8 us)
Async XLA Ops:
  0.6 64.4 %collective-permute-start.11 = (bf16[256,2048]{1,0:T(8,128)(2,1)}, bf16[256,2048]{1,0:T(8,128)(2,1)S(1)}, u32[]{:S(2)}, u32[]{:S(2)}) collective-permute-start(bf16[256,2048]{1,0:T(8,128)(2,1)} %param.16), channel_id=1, source_target_pairs={{0,4},{4,0},{8,12},{12,8},{1,5},{5,1},{9,13},{13,9},{2,6},{6,2},{1... | collective-permute-start | bytes 3145736 | tf_op jit(solution)/shard_map/ppermute | solution.py:17
  3.7 61.3 %collective-permute-start.12 = (bf16[256,2048]{1,0:T(8,128)(2,1)}, bf16[256,2048]{1,0:T(8,128)(2,1)S(1)}, u32[]{:S(2)}, u32[]{:S(2)}) collective-permute-start(bf16[256,2048]{1,0:T(8,128)(2,1)} %param.16), channel_id=1, source_target_pairs={{0,8},{4,12},{8,0},{12,4},{1,9},{5,13},{9,1},{13,5},{2,10},{6,14},... | collective-permute-start | bytes 3145736 | tf_op jit(solution)/shard_map/ppermute | solution.py:17
  6.3 58.7 %copy-start.8 = (bf16[128,2048]{1,0:T(8,128)(2,1)S(1)}, bf16[128,2048]{1,0:T(8,128)(2,1)}, u32[]{:S(2)}) copy-start(bf16[128,2048]{1,0:T(8,128)(2,1)} %param.21) | copy-start | bytes 1572868
  6.3 7.7 %copy-start.1 = (bf16[256,2048]{1,0:T(8,128)(2,1)S(1)}, bf16[256,2048]{1,0:T(8,128)(2,1)}, u32[]{:S(2)}) copy-start(bf16[256,2048]{1,0:T(8,128)(2,1)} %get-tuple-element.94.refs_0_.refs_1_) | copy-start | bytes 3145732 | tf_op jit(solution)/shard_map/cond
  9.6 44.4 %collective-permute-start = (bf16[512,128]{1,0:T(8,128)(2,1)}, bf16[512,128]{1,0:T(8,128)(2,1)}, u32[]{:S(2)}, u32[]{:S(2)}) collective-permute-start(bf16[512,128]{1,0:T(8,128)(2,1)} %first_codes.1), channel_id=1, source_target_pairs={{0,4},{4,0},{8,12},{12,8},{1,5},{5,1},{9,13},{13,9},{2,6},{6,2},{1... | collective-permute-start | bytes 393224 | tf_op jit(solution)/shard_map/cond/branch_1_fun/ppermute | solution.py:17
  10.1 51.9 %collective-permute-start.1 = (bf16[512,128]{1,0:T(8,128)(2,1)}, bf16[512,128]{1,0:T(8,128)(2,1)}, u32[]{:S(2)}, u32[]{:S(2)}) collective-permute-start(bf16[512,128]{1,0:T(8,128)(2,1)} %first_codes.1), channel_id=1, source_target_pairs={{0,8},{4,12},{8,0},{12,4},{1,9},{5,13},{9,1},{13,5},{2,10},{6,14},... | collective-permute-start | bytes 393224 | tf_op jit(solution)/shard_map/cond/branch_1_fun/ppermute | solution.py:17
  10.1 51.8 %collective-permute-start.2 = (bf16[512,128]{1,0:T(8,128)(2,1)}, bf16[512,128]{1,0:T(8,128)(2,1)}, u32[]{:S(2)}, u32[]{:S(2)}) collective-permute-start(bf16[512,128]{1,0:T(8,128)(2,1)} %first_codes.1), channel_id=1, source_target_pairs={{0,12},{4,8},{8,4},{12,0},{1,13},{5,9},{9,5},{13,1},{2,14},{6,10},... | collective-permute-start | bytes 393224 | tf_op jit(solution)/shard_map/cond/branch_1_fun/ppermute | solution.py:17
  61.9 47.6 %collective-permute-start.15 = (bf16[256,2048]{1,0:T(8,128)(2,1)}, bf16[256,2048]{1,0:T(8,128)(2,1)}, u32[]{:S(2)}, u32[]{:S(2)}) collective-permute-start(bf16[256,2048]{1,0:T(8,128)(2,1)} %get-tuple-element.202), channel_id=1, source_target_pairs={{0,4},{4,0},{8,12},{12,8},{1,5},{5,1},{9,13},{13,9},{2,6},{6,2},{1... | collective-permute-start | bytes 3145736 | tf_op jit(solution)/shard_map/ppermute | solution.py:17
  63.9 47.0 %collective-permute-start.16 = (bf16[256,2048]{1,0:T(8,128)(2,1)}, bf16[256,2048]{1,0:T(8,128)(2,1)}, u32[]{:S(2)}, u32[]{:S(2)}) collective-permute-start(bf16[256,2048]{1,0:T(8,128)(2,1)} %get-tuple-element.203), channel_id=1, source_target_pairs={{0,8},{4,12},{8,0},{12,4},{1,9},{5,13},{9,1},{13,5},{2,10},{6,14},... | collective-permute-start | bytes 3145736 | tf_op jit(solution)/shard_map/ppermute | solution.py:17
  65.0 1.0 copy-start.6
  65.0 1.3 copy-start.7
  66.4 8.0 %copy-start.2 = (bf16[256,2048]{1,0:T(8,128)(2,1)S(1)}, bf16[256,2048]{1,0:T(8,128)(2,1)}, u32[]{:S(2)}) copy-start(bf16[256,2048]{1,0:T(8,128)(2,1)} %get-tuple-element.115.refs_1_) | copy-start | bytes 3145732 | tf_op jit(solution)/shard_map/cond
  80.2 3.8 %collective-permute-start.3 = (bf16[2,16,6,32,128]{4,3,2,1,0:T(8,128)(2,1)}, bf16[2,16,6,32,128]{4,3,2,1,0:T(8,128)(2,1)}, u32[]{:S(2)}, u32[]{:S(2)}) collective-permute-start(bf16[2,16,6,32,128]{4,3,2,1,0:T(8,128)(2,1)} %get-tuple-element.117), channel_id=1, source_target_pairs={{0,1},{1,0},{2,3},{3,2},{4,5},{5,4},{6,7},{7,6},{8,9},{9,8},{10,11... | collective-permute-start | bytes 4718600 | tf_op jit(solution)/shard_map/cond/branch_1_fun/ppermute | solution.py:17
  87.7 19.9 %collective-permute-start.4 = (bf16[16,6,32,128]{3,2,1,0:T(8,128)(2,1)}, bf16[16,6,32,128]{3,2,1,0:T(8,128)(2,1)}, u32[]{:S(2)}, u32[]{:S(2)}) collective-permute-start(bf16[16,6,32,128]{3,2,1,0:T(8,128)(2,1)} %core_sums.3), channel_id=1, source_target_pairs={{0,2},{2,0},{1,3},{3,1},{4,6},{6,4},{5,7},{7,5},{8,10},{10,8},{9,1... | collective-permute-start | bytes 2359304 | tf_op jit(solution)/shard_map/cond/branch_1_fun/ppermute | solution.py:17
  107.6 58.9 %collective-permute-start.13 = (bf16[256,2048]{1,0:T(8,128)(2,1)}, bf16[256,2048]{1,0:T(8,128)(2,1)S(1)}, u32[]{:S(2)}, u32[]{:S(2)}) collective-permute-start(bf16[256,2048]{1,0:T(8,128)(2,1)} %get-tuple-element.201), channel_id=1, source_target_pairs={{0,4},{4,0},{8,12},{12,8},{1,5},{5,1},{9,13},{13,9},{2,6},{6,2},{1... | collective-permute-start | bytes 3145736 | tf_op jit(solution)/shard_map/ppermute | solution.py:17
  109.5 56.9 %collective-permute-start.14 = (bf16[256,2048]{1,0:T(8,128)(2,1)}, bf16[256,2048]{1,0:T(8,128)(2,1)S(1)}, u32[]{:S(2)}, u32[]{:S(2)}) collective-permute-start(bf16[256,2048]{1,0:T(8,128)(2,1)} %get-tuple-element.201), channel_id=1, source_target_pairs={{0,8},{4,12},{8,0},{12,4},{1,9},{5,13},{9,1},{13,5},{2,10},{6,14},... | collective-permute-start | bytes 3145736 | tf_op jit(solution)/shard_map/ppermute | solution.py:17
  110.9 10.2 %copy-start.3 = (bf16[256,2048]{1,0:T(8,128)(2,1)S(1)}, bf16[256,2048]{1,0:T(8,128)(2,1)}, u32[]{:S(2)}) copy-start(bf16[256,2048]{1,0:T(8,128)(2,1)} %get-tuple-element.136.refs_2_) | copy-start | bytes 3145732 | tf_op jit(solution)/shard_map/cond
  127.7 4.5 %collective-permute-start.9 = (bf16[2,16,8,32,128]{4,3,2,1,0:T(8,128)(2,1)}, bf16[2,16,8,32,128]{4,3,2,1,0:T(8,128)(2,1)}, u32[]{:S(2)}, u32[]{:S(2)}) collective-permute-start(bf16[2,16,8,32,128]{4,3,2,1,0:T(8,128)(2,1)} %get-tuple-element.140), channel_id=1, source_target_pairs={{0,1},{1,0},{2,3},{3,2},{4,5},{5,4},{6,7},{7,6},{8,9},{9,8},{10,11... | collective-permute-start | bytes 6291464 | tf_op jit(solution)/shard_map/cond/branch_1_fun/ppermute | solution.py:17
  132.2 5.5 %copy-start.9 = (bf16[512,128]{1,0:T(8,128)(2,1)S(1)}, bf16[512,128]{1,0:T(8,128)(2,1)}, u32[]{:S(2)}) copy-start(bf16[512,128]{1,0:T(8,128)(2,1)} %get-tuple-element.132) | copy-start | bytes 393220 | tf_op jit(solution)/shard_map/cond
  136.2 30.2 %collective-permute-start.10 = (bf16[16,8,32,128]{3,2,1,0:T(8,128)(2,1)}, bf16[16,8,32,128]{3,2,1,0:T(8,128)(2,1)}, u32[]{:S(2)}, u32[]{:S(2)}) collective-permute-start(bf16[16,8,32,128]{3,2,1,0:T(8,128)(2,1)} %core_sums.4), channel_id=1, source_target_pairs={{0,2},{2,0},{1,3},{3,1},{4,6},{6,4},{5,7},{7,5},{8,10},{10,8},{9,1... | collective-permute-start | bytes 3145736 | tf_op jit(solution)/shard_map/cond/branch_1_fun/ppermute | solution.py:17
  137.7 20.1 %collective-permute-start.7 = (bf16[512,128]{1,0:T(8,128)(2,1)S(1)}, bf16[512,128]{1,0:T(8,128)(2,1)S(1)}, u32[]{:S(2)}, u32[]{:S(2)}) collective-permute-start(bf16[512,128]{1,0:T(8,128)(2,1)S(1)} %copy-done.9), channel_id=1, source_target_pairs={{0,4},{4,0},{8,12},{12,8},{1,5},{5,1},{9,13},{13,9},{2,6},{6,2},{1... | collective-permute-start | bytes 393224 | tf_op jit(solution)/shard_map/cond/branch_1_fun/ppermute | solution.py:17
  158.5 7.9 %collective-permute-start.8 = (bf16[512,128]{1,0:T(8,128)(2,1)}, bf16[512,128]{1,0:T(8,128)(2,1)}, u32[]{:S(2)}, u32[]{:S(2)}) collective-permute-start(bf16[512,128]{1,0:T(8,128)(2,1)} %add_convert_fusion), channel_id=1, source_target_pairs={{0,8},{4,12},{8,0},{12,4},{1,9},{5,13},{9,1},{13,5},{2,10},{6,14},... | collective-permute-start | bytes 393224 | tf_op jit(solution)/shard_map/cond/branch_1_fun/ppermute | solution.py:17
  166.4 45.2 %collective-permute-start.17 = (bf16[256,2048]{1,0:T(8,128)(2,1)}, bf16[256,2048]{1,0:T(8,128)(2,1)}, u32[]{:S(2)}, u32[]{:S(2)}) collective-permute-start(bf16[256,2048]{1,0:T(8,128)(2,1)} %get-tuple-element.213), channel_id=1, source_target_pairs={{0,4},{4,0},{8,12},{12,8},{1,5},{5,1},{9,13},{13,9},{2,6},{6,2},{1... | collective-permute-start | bytes 3145736 | tf_op jit(solution)/shard_map/ppermute | solution.py:17
  166.5 47.9 %collective-permute-start.18 = (bf16[256,2048]{1,0:T(8,128)(2,1)}, bf16[256,2048]{1,0:T(8,128)(2,1)}, u32[]{:S(2)}, u32[]{:S(2)}) collective-permute-start(bf16[256,2048]{1,0:T(8,128)(2,1)} %get-tuple-element.214), channel_id=1, source_target_pairs={{0,8},{4,12},{8,0},{12,4},{1,9},{5,13},{9,1},{13,5},{2,10},{6,14},... | collective-permute-start | bytes 3145736 | tf_op jit(solution)/shard_map/ppermute | solution.py:17
  169.5 1.0 copy-start.4
  169.5 1.4 copy-start.5
  170.9 13.3 %copy-start = (bf16[16,7,128,128]{3,2,1,0:T(8,128)(2,1)S(1)}, bf16[16,7,128,128]{3,2,1,0:T(8,128)(2,1)}, u32[]{:S(2)}) copy-start(bf16[16,7,128,128]{3,2,1,0:T(8,128)(2,1)} %get-tuple-element.153.refs_1_) | copy-start | bytes 11010052 | tf_op jit(solution)/shard_map/cond
  176.2 3.0 %collective-permute-start.5 = (bf16[2,16,4,32,128]{4,3,2,1,0:T(8,128)(2,1)}, bf16[2,16,4,32,128]{4,3,2,1,0:T(8,128)(2,1)}, u32[]{:S(2)}, u32[]{:S(2)}) collective-permute-start(bf16[2,16,4,32,128]{4,3,2,1,0:T(8,128)(2,1)} %get-tuple-element.155), channel_id=1, source_target_pairs={{0,1},{1,0},{2,3},{3,2},{4,5},{5,4},{6,7},{7,6},{8,9},{9,8},{10,11... | collective-permute-start | bytes 3145736 | tf_op jit(solution)/shard_map/cond/branch_1_fun/ppermute | solution.py:17
  182.7 14.3 %collective-permute-start.6 = (bf16[16,4,32,128]{3,2,1,0:T(8,128)(2,1)}, bf16[16,4,32,128]{3,2,1,0:T(8,128)(2,1)}, u32[]{:S(2)}, u32[]{:S(2)}) collective-permute-start(bf16[16,4,32,128]{3,2,1,0:T(8,128)(2,1)} %core_sums.5), channel_id=1, source_target_pairs={{0,2},{2,0},{1,3},{3,1},{4,6},{6,4},{5,7},{7,5},{8,10},{10,8},{9,1... | collective-permute-start | bytes 1572872 | tf_op jit(solution)/shard_map/cond/branch_1_fun/ppermute | solution.py:17

commit v3 on v2

--- a/solution.py
+++ b/solution.py
@@ -535,18 +535,21 @@
     cuts = (spot, n_tok, n_sub)
 
     def to_partners(values):
-        return [exchange(value, "feat", 1 << k) for k, value in enumerate(values)]
-
-    def to_all(part):
-        return [part] + [exchange(part, "feat", mask) for mask in range(1, n_feat)]
+        sent = [exchange(value, "feat", 1 << k) for k, value in reversed(list(enumerate(values)))]
+        return sent[::-1]
+
+    def add(parts):
+        return (parts[0].astype(F32) + parts[1].astype(F32)).astype(BF16)
 
     def by_levels(part):
-        parts = [part]
-        for level in range(n_feat.bit_length() - 1):
-            if level:
-                part = (parts[0].astype(F32) + parts[1].astype(F32)).astype(BF16)
+        parts = [part, exchange(part, "feat", 1)]
+        for level in range(1, n_feat.bit_length() - 2):
+            part = add(parts)
             parts = [part, exchange(part, "feat", 1 << level)]
-        return parts
+        return add(parts)
+
+    def last_level(part):
+        return [part, exchange(part, "feat", n_feat // 2)]
 
     def halves(parts):
         return [(value, 0) for value in parts], [(value, 1) for value in parts]
@@ -556,31 +559,36 @@
         empty = lambda *_: jax.tree.map(lambda x: jnp.zeros(x.shape, x.dtype), shapes)
         return lax.cond(lax.axis_index("feat") < n_feat, work, empty, *args)
 
-    def summed(parts):
+    def by_cores(parts):
         kept = parts[0]
         got = [exchange(parts[h], "sub", h) for h in range(1, n_sub)]
-        sums = layer.core_sums(kept, got) if n_tok > 1 else []
+        return kept, got, list(layer.core_sums(kept, got)) if n_tok > 1 else []
+
+    def by_chips(kept, got, sums):
         return kept, got, [exchange(value, "tok", 1 + m) for m, value in enumerate(sums)]
+
+    def summed(parts):
+        return by_chips(*by_cores(parts))
 
     def start_step(inputs, cotangent, w_out, u_in, v_out):
         products = layer.far_products(cotangent, w_out)
-        return products, to_all(layer.first_codes(inputs, cotangent, u_in, v_out))
+        return products, by_levels(layer.first_codes(inputs, cotangent, u_in, v_out))
 
     def hidden_step(inputs, cotangent, w_in, v_in, u_out, far_inputs, first):
         codes, backs = halves(first)
         act, slope, code = layer.hidden(inputs, far_inputs, w_in, codes, v_in, u_out)
         parts = layer.weight_grads(cuts, cotangent, acts=act, backs=backs, u_acts=act)
-        return act, slope, code, summed(parts)
+        return act, slope, code, by_cores(parts)
 
     def grad_step(
-        inputs, cotangent, w_in, w_out, v_in, u_out, far_inputs, far_cot, slope, code, first
+        inputs, cotangent, w_in, w_out, v_in, u_out, far_inputs, far_cot, slope, code, first, done
     ):
         codes, backs = halves(first)
         pre_grad, code, products = layer.hidden_grad(
-            cotangent, w_out, backs, u_out, far_cot, slope, v_in, w_in, code
+            cotangent, w_out, backs, u_out, far_cot, slope, v_in, w_in, code, after=done
         )
         parts = layer.weight_grads(cuts, pre_grad, acts=inputs, far_acts=far_inputs, codes=codes)
-        return pre_grad, by_levels(code), products, summed(parts)
+        return pre_grad, last_level(by_levels(code)), products, summed(parts)
 
     def last_step(inputs, cotangent, w_in, w_out, v_out, u_in, act, far_acts, last, pre_grad):
         codes, backs = halves(last)
@@ -592,14 +600,17 @@
 
     far_inputs = to_partners([inputs] * layer.far)
     products, first = block(start_step, inputs, cotangent, w_out, u_in, v_out)
+    first = last_level(first)
     far_cot = to_partners(products)
     act, slope, code, sums_early = block(
         hidden_step, inputs, cotangent, w_in, v_in, u_out, far_inputs, first
     )
     far_acts = to_partners([act] * layer.far)
+    sums_early = by_chips(*sums_early)
     pre_grad, last, products, sums_in = block(
         grad_step,
         inputs, cotangent, w_in, w_out, v_in, u_out, far_inputs, far_cot, slope, code, first,
+        sums_early[2],
     )
     far_pre = to_partners(pin(products, *far_acts))
     output, local_grad, sums_late = block(

time: 219 us -> 213 us (0.973)
  waiting for transfers between devices: 111 us -> 104 us
    ppermute x19 -> x18, waiting for transfers between devices: 111 us -> 104 us  [exchange(): return lax.ppermute(value, axis, pairs)]
    ppermute x19 -> x18, starting transfers between devices: 24.7 us -> 24.2 us  [exchange(): return lax.ppermute(value, axis, pairs)]
  transfers between devices with their start and end apart: 19 -> 18, of which waited for: 12 -> 14; matrix products, arithmetic and copies ran while one was open for 0% -> 0% of each run, Pallas kernels for 34% -> 35%
where the time goes in v3:
time: 213 us; the launch traced here: 212 us
  waiting for transfers between devices  104 us (49%)
  Pallas kernels  74.5 us (35%)
  starting transfers between devices  24.2 us (11%)
  local copies, waits for them, and re-layouts  4.46 us (2%)
  other arithmetic  4.45 us (2%)
    ppermute x18, waiting for transfers between devices, exchange(): return lax.ppermute(value, axis, pairs)  104 us
    pallas_call x14, Pallas kernels, call(): pl.pallas_call(kernel, grid=grid, in_specs=list(ins) + [pl.BlockSpec(memo...  74.5 us
    ppermute x18, starting transfers between devices, exchange(): return lax.ppermute(value, axis, pairs)  24.2 us
  transfers between devices with their start and end apart: 18, of which 14 were waited for; matrix products, arithmetic and copies ran while one was open for 0% of the time, Pallas kernels for 35%

profile of v3, /device:TPU:0, one launch (start us, length us, event | category | flops | bytes accessed | tf_op | source)
XLA Modules:
  0.0 212.1 jit_solution(8324395260670084628)
XLA Ops:
  0.6 3.1 %collective-permute-start.8 = (bf16[256,2048]{1,0:T(8,128)(2,1)}, bf16[256,2048]{1,0:T(8,128)(2,1)S(1)}, u32[]{:S(2)}, u32[]{:S(2)}) collective-permute-start(bf16[256,2048]{1,0:T(8,128)(2,1)} %param.16), channel_id=1, source_target_pairs={{0,4},{4,0},{8,12},{12,8},{1,5},{5,1},{9,13},{13,9},{2,6},{6,2},{1... | collective-permute-start | bytes 3145736 | tf_op jit(solution)/shard_map/ppermute | solution.py:17
  6.3 46.1 %conditional.4 = (bf16[256,2048]{1,0:T(8,128)(2,1)}, bf16[256,2048]{1,0:T(8,128)(2,1)}, bf16[512,128]{1,0:T(8,128)(2,1)S(1)}) conditional(s32[]{:T(128)} %convert_element_type.33, () %tuple.42, (bf16[256,2048]{1,0:T(8,128)(2,1)}, bf16[16,7,128,128]{3,2,1,0:T(8,128)(2,1)}, bf16[256,2048]{1,0:T(8,128)(2,1)}, bf16[2048,128]{1,0:T(8,128)(2,1)}, ...), branch_computations={%region_0.0_spmd, %region_1.0_spmd} | conditional | flops 537133056 | bytes 15728760 | solution.py:560
  6.3 3.3 %first_codes.1 = bf16[512,128]{1,0:T(8,128)(2,1)} custom-call(bf16[256,2048]{1,0:T(8,128)(2,1)} %get-tuple-element.92.refs_0_, bf16[256,2048]{1,0:T(8,128)(2,1)} %get-tuple-element.88.refs_0_.refs_1_, bf16[2048,128]{1,0:T(8,128)(2,1)} %get-tuple-element.93.refs_2_, bf16[128,2048]{1,0:T(8,128)(2,1)} %get-tuple-element.94.refs_3_), custom_call_target="tpu_custom_call" | custom-call | flops 268435456 | bytes 3276800 | tf_op jit(solution)/shard_map/cond/branch_1_fun/first_codes/pallas_call | solution.py:68
  10.1 4.7 %far_products.1 = (bf16[256,2048]{1,0:T(8,128)(2,1)}, bf16[256,2048]{1,0:T(8,128)(2,1)}) custom-call(bf16[256,2048]{1,0:T(8,128)(2,1)S(1)} %copy-done.1, bf16[16,7,128,128]{3,2,1,0:T(8,128)(2,1)} %get-tuple-element.89.refs_1_), custom_call_target="tpu_custom_call" | custom-call | flops 268435456 | bytes 6815744 | tf_op jit(solution)/shard_map/cond/branch_1_fun/far_products/pallas_call | solution.py:68
  14.8 37.6 %collective-permute-done.3 = bf16[512,128]{1,0:T(8,128)(2,1)S(1)} collective-permute-done((bf16[512,128]{1,0:T(8,128)(2,1)}, bf16[512,128]{1,0:T(8,128)(2,1)S(1)}, u32[]{:S(2)}, u32[]{:S(2)}) %collective-permute-start.3) | collective-permute-done | bytes 131104 | tf_op jit(solution)/shard_map/cond/branch_1_fun/ppermute | solution.py:17
  52.4 2.9 %collective-permute-start.10 = (bf16[512,128]{1,0:T(8,128)(2,1)S(1)}, bf16[512,128]{1,0:T(8,128)(2,1)S(1)}, u32[]{:S(2)}, u32[]{:S(2)}) collective-permute-start(bf16[512,128]{1,0:T(8,128)(2,1)S(1)} %get-tuple-element.185), channel_id=1, source_target_pairs={{0,8},{4,12},{8,0},{12,4},{1,9},{5,13},{9,1},{13,5},{2,10},{6,14},... | collective-permute-start | bytes 393224 | tf_op jit(solution)/shard_map/ppermute | solution.py:17
  57.3 4.5 %collective-permute-done.10 = bf16[512,128]{1,0:T(8,128)(2,1)S(1)} collective-permute-done((bf16[512,128]{1,0:T(8,128)(2,1)S(1)}, bf16[512,128]{1,0:T(8,128)(2,1)S(1)}, u32[]{:S(2)}, u32[]{:S(2)}) %collective-permute-start.10) | collective-permute-done | bytes 131104 | tf_op jit(solution)/shard_map/ppermute | solution.py:17
  63.1 21.1 %conditional.5 = (bf16[256,2048]{1,0:T(8,128)(2,1)}, f32[256,2048]{1,0:T(8,128)}, bf16[256,128]{1,0:T(8,128)(2,1)S(1)}, bf16[2,16,6,32,128]{4,3,2,1,0:T(8,128)(2...) conditional(s32[]{:T(128)} %convert_element_type.33, () %tuple.41, ...), branch_computations={%region_2.0_spmd, %region_3.0_spmd} | conditional | flops 2013265920 | bytes 32309372 | solution.py:560
  63.1 7.9 %hidden.1 = (bf16[256,2048]{1,0:T(8,128)(2,1)}, f32[256,2048]{1,0:T(8,128)}, bf16[256,128]{1,0:T(8,128)(2,1)S(1)}) custom-call(bf16[256,2048]{1,0:T(8,128)(2,1)} %get-tuple-element.95.refs_0_, bf16[256,2048]{1,0:T(8,128)(2,1)S(1)} %get-tuple-element.96.refs_1_, bf16[256,2048]{1,0:T(8,128)(2,1)S(1)} %get-tuple-element.97.refs_2_, ...), custom_call_target="tpu_custom_call" | custom-call | flops 1207959552 | bytes 11337728 | tf_op jit(solution)/shard_map/cond/branch_1_fun/hidden/pallas_call | solution.py:68
  71.0 5.6 %weight_grads.3 = (bf16[2,16,6,32,128]{4,3,2,1,0:T(8,128)(2,1)}, bf16[2,16,6,32,128]{4,3,2,1,0:T(8,128)(2,1)}) custom-call(s32[2]{0:T(128)S(1)} %get-tuple-element.106.refs_0_, bf16[256,2048]{1,0:T(8,128)(2,1)S(1)} %copy-done.2, bf16[256,2048]{1,0:T(8,128)(2,1)} %get-tuple-element.227.refs_2_.refs_5_, ...), custom_call_target="tpu_custom_call" | custom-call | flops 805306368 | bytes 6553608 | tf_op jit(solution)/shard_map/cond/branch_1_fun/weight_grads/pallas_call | solution.py:68
  76.7 3.7 %collective-permute-done.refs_1_ = bf16[2,16,6,32,128]{4,3,2,1,0:T(8,128)(2,1)} collective-permute-done((bf16[2,16,6,32,128]{4,3,2,1,0:T(8,128)(2,1)}, bf16[2,16,6,32,128]{4,3,2,1,0:T(8,128)(2,1)}, u32[]{:S(2)}, u32[]{:S(2)}) %collective-permute-start) | collective-permute-done | bytes 1572896 | tf_op jit(solution)/shard_map/cond/branch_1_fun/ppermute | solution.py:17
  80.4 3.7 %core_sums.3 = bf16[16,6,32,128]{3,2,1,0:T(8,128)(2,1)} custom-call(bf16[2,16,6,32,128]{4,3,2,1,0:T(8,128)(2,1)} %get-tuple-element.230.refs_0_, bf16[2,16,6,32,128]{4,3,2,1,0:T(8,128)(2,1)} %collective-permute-done.refs_1_), custom_call_target="tpu_custom_call" | custom-call | bytes 3932160 | tf_op jit(solution)/shard_map/cond/branch_1_fun/core_sums/pallas_call | solution.py:68
  84.5 3.4 %collective-permute-start.12 = (bf16[256,2048]{1,0:T(8,128)(2,1)}, bf16[256,2048]{1,0:T(8,128)(2,1)S(1)}, u32[]{:S(2)}, u32[]{:S(2)}) collective-permute-start(bf16[256,2048]{1,0:T(8,128)(2,1)} %get-tuple-element.186), channel_id=1, source_target_pairs={{0,8},{4,12},{8,0},{12,4},{1,9},{5,13},{9,1},{13,5},{2,10},{6,14},... | collective-permute-start | bytes 3145736 | tf_op jit(solution)/shard_map/ppermute | solution.py:17
  89.5 14.8 %collective-permute-done.13 = bf16[256,2048]{1,0:T(8,128)(2,1)} collective-permute-done((bf16[256,2048]{1,0:T(8,128)(2,1)}, bf16[256,2048]{1,0:T(8,128)(2,1)}, u32[]{:S(2)}, u32[]{:S(2)}) %collective-permute-start.13) | collective-permute-done | bytes 1048608 | tf_op jit(solution)/shard_map/ppermute | solution.py:17
  108.1 51.6 %conditional.6 = (bf16[256,2048]{1,0:T(8,128)(2,1)}, bf16[512,128]{1,0:T(8,128)(2,1)}, bf16[512,128]{1,0:T(8,128)(2,1)}, bf16[256,2048]{1,0:T(8,128)(2,1)}, bf16...) conditional(s32[]{:T(128)} %convert_element_type.33, () %tuple.45, ...), branch_computations={%region_4.0_spmd, %region_5.0_spmd} | conditional | flops 1879310336 | bytes 53018940 | solution.py:560
  109.0 10.2 %hidden_grad.1 = (bf16[256,2048]{1,0:T(8,128)(2,1)}, bf16[512,128]{1,0:T(8,128)(2,1)}, bf16[256,2048]{1,0:T(8,128)(2,1)}, bf16[256,2048]{1,0:T(8,128)(2,1)}) custom-call(bf16[256,2048]{1,0:T(8,128)(2,1)} %get-tuple-element.110.refs_0_, bf16[16,7,128,128]{3,2,1,0:T(8,128)(2,1)} %get-tuple-element.111.refs_1_, ...), custom_call_target="tpu_custom_call" | custom-call | flops 805306368 | bytes 17235968 | tf_op jit(solution)/shard_map/cond/branch_1_fun/hidden_grad/pallas_call | solution.py:68
  119.2 6.4 %weight_grads.4 = (bf16[2,16,8,32,128]{4,3,2,1,0:T(8,128)(2,1)}, bf16[2,16,8,32,128]{4,3,2,1,0:T(8,128)(2,1)}) custom-call(s32[2]{0:T(128)S(1)} %get-tuple-element.126.refs_0_, bf16[256,2048]{1,0:T(8,128)(2,1)} %get-tuple-element.241.refs_1_, bf16[256,2048]{1,0:T(8,128)(2,1)S(1)} %copy-done.3, bf16[256,2048]{1,0:T(8,128)(2,1)} %get-tuple-element.128.refs_3_, ...), custom_call_target="tpu_custom_call" | custom-call | flops 1073741824 | bytes 8650760 | tf_op jit(solution)/shard_map/cond/branch_1_fun/weight_grads/pallas_call | solution.py:68
  125.6 4.5 %collective-permute-done.6.refs_1_ = bf16[2,16,8,32,128]{4,3,2,1,0:T(8,128)(2,1)} collective-permute-done((bf16[2,16,8,32,128]{4,3,2,1,0:T(8,128)(2,1)}, bf16[2,16,8,32,128]{4,3,2,1,0:T(8,128)(2,1)}, u32[]{:S(2)}, u32[]{:S(2)}) %collective-permute-start.6) | collective-permute-done | bytes 2097184 | tf_op jit(solution)/shard_map/cond/branch_1_fun/ppermute | solution.py:17
  130.1 4.0 %core_sums.4 = bf16[16,8,32,128]{3,2,1,0:T(8,128)(2,1)} custom-call(bf16[2,16,8,32,128]{4,3,2,1,0:T(8,128)(2,1)} %get-tuple-element.246.refs_0_, bf16[2,16,8,32,128]{4,3,2,1,0:T(8,128)(2,1)} %collective-permute-done.6.refs_1_), custom_call_target="tpu_custom_call" | custom-call | bytes 5242880 | tf_op jit(solution)/shard_map/cond/branch_1_fun/core_sums/pallas_call | solution.py:68
  136.0 15.3 %collective-permute-done.4 = bf16[512,128]{1,0:T(8,128)(2,1)S(1)} collective-permute-done((bf16[512,128]{1,0:T(8,128)(2,1)S(1)}, bf16[512,128]{1,0:T(8,128)(2,1)S(1)}, u32[]{:S(2)}, u32[]{:S(2)}) %collective-permute-start.4) | collective-permute-done | bytes 131104 | tf_op jit(solution)/shard_map/cond/branch_1_fun/ppermute | solution.py:17
  153.1 6.5 %collective-permute-done.5 = bf16[512,128]{1,0:T(8,128)(2,1)} collective-permute-done((bf16[512,128]{1,0:T(8,128)(2,1)}, bf16[512,128]{1,0:T(8,128)(2,1)}, u32[]{:S(2)}, u32[]{:S(2)}) %collective-permute-start.5) | collective-permute-done | bytes 131104 | tf_op jit(solution)/shard_map/cond/branch_1_fun/ppermute | solution.py:17
  160.1 3.2 %collective-permute-start.17 = (bf16[256,2048]{1,0:T(8,128)(2,1)}, bf16[256,2048]{1,0:T(8,128)(2,1)}, u32[]{:S(2)}, u32[]{:S(2)}) collective-permute-start(bf16[256,2048]{1,0:T(8,128)(2,1)} %get-tuple-element.200), channel_id=1, source_target_pairs={{0,8},{4,12},{8,0},{12,4},{1,9},{5,13},{9,1},{13,5},{2,10},{6,14},... | collective-permute-start | bytes 3145736 | tf_op jit(solution)/shard_map/ppermute | solution.py:17
  163.3 27.5 %conditional.7 = (bf16[256,2048]{1,0:T(8,128)(2,1)}, f32[256,2048]{1,0:T(8,128)}, bf16[2,16,4,32,128]{4,3,2,1,0:T(8,128)(2,1)}, bf16[2,16,4,32,128]{4,3,2,1,0:T(8,128)(2,1)}, bf16[16,4,32,128]{3,2,1,0:T(8,128)(2,1)}) conditional(s32[]{:T(128)} %convert_element_type.33, () %tuple.40, (s32[2]{0:T(128)S(1)}, bf16[256,2048]{1,0:T(8,128)(2,1)}, ...), branch_computations={%region_6.0_spmd, %region_7.0_spmd} | conditional | flops 2550136832 | bytes 55050452 | solution.py:560
  164.6 5.3 %weight_grads.5 = (bf16[2,16,4,32,128]{4,3,2,1,0:T(8,128)(2,1)}, bf16[2,16,4,32,128]{4,3,2,1,0:T(8,128)(2,1)}) custom-call(s32[2]{0:T(128)S(1)} %get-tuple-element.139.refs_0_, bf16[256,2048]{1,0:T(8,128)(2,1)} %get-tuple-element.140.refs_1_, bf16[256,2048]{1,0:T(8,128)(2,1)} %copy-done.4, bf16[256,2048]{1,0:T(8,128)(2,1)} %copy-done.5, ...), custom_call_target="tpu_custom_call" | custom-call | flops 536870912 | bytes 6815752 | tf_op jit(solution)/shard_map/cond/branch_1_fun/weight_grads/pallas_call | solution.py:68
  170.0 3.0 %collective-permute-done.1.refs_1_ = bf16[2,16,4,32,128]{4,3,2,1,0:T(8,128)(2,1)} collective-permute-done((bf16[2,16,4,32,128]{4,3,2,1,0:T(8,128)(2,1)}, bf16[2,16,4,32,128]{4,3,2,1,0:T(8,128)(2,1)}, u32[]{:S(2)}, u32[]{:S(2)}) %collective-permute-start.1) | collective-permute-done | bytes 1048608 | tf_op jit(solution)/shard_map/cond/branch_1_fun/ppermute | solution.py:17
  173.0 3.5 %core_sums.5 = bf16[16,4,32,128]{3,2,1,0:T(8,128)(2,1)} custom-call(bf16[2,16,4,32,128]{4,3,2,1,0:T(8,128)(2,1)} %get-tuple-element.256.refs_7_.refs_0_, bf16[2,16,4,32,128]{4,3,2,1,0:T(8,128)(2,1)} %collective-permute-done.1.refs_1_), custom_call_target="tpu_custom_call" | custom-call | bytes 2621440 | tf_op jit(solution)/shard_map/cond/branch_1_fun/core_sums/pallas_call | solution.py:68
  177.9 5.1 %input_grad.1 = f32[256,2048]{1,0:T(8,128)} custom-call(bf16[256,2048]{1,0:T(8,128)(2,1)} %get-tuple-element.143.refs_0_, bf16[16,7,128,128]{3,2,1,0:T(8,128)(2,1)S(1)} %copy-done, bf16[512,128]{1,0:T(8,128)(2,1)} %get-tuple-element.136.refs_4_.refs_6_.refs_2_, bf16[512,128]{1,0:T(8,128)(2,1)} %get-tuple-element.137.refs_5_.refs_7_.refs_3_, ...), custom_call_target="tpu_custom_call" | custom-call | flops 805306368 | bytes 7602176 | tf_op jit(solution)/shard_map/cond/branch_1_fun/input_grad/pallas_call | solution.py:68
  183.1 6.4 %result.1 = bf16[256,2048]{1,0:T(8,128)(2,1)} custom-call(bf16[256,2048]{1,0:T(8,128)(2,1)} %get-tuple-element.132.refs_0_, bf16[256,2048]{1,0:T(8,128)(2,1)} %copy-done.4, bf16[256,2048]{1,0:T(8,128)(2,1)} %copy-done.5, bf16[16,7,128,128]{3,2,1,0:T(8,128)(2,1)} %get-tuple-element.135.refs_3_, bf16[512,128]{1,0:T(8,128)(2,1)} %get-tuple-element.136.refs_4_.refs_6_.refs_2_, ...), custom_call_target="tpu_custom_call" | custom-call | flops 1207959552 | bytes 8650752 | tf_op jit(solution)/shard_map/cond/branch_1_fun/result/pallas_call | solution.py:68
  190.7 4.1 %last_sums.2 = (f32[16,7,32,128]{3,2,1,0:T(8,128)}, f32[32,2048]{1,0:T(8,128)}) custom-call(bf16[2,16,8,32,128]{4,3,2,1,0:T(8,128)(2,1)} %get-tuple-element.201.refs_0_, bf16[2,16,8,32,128]{4,3,2,1,0:T(8,128)(2,1)} %get-tuple-element.202.refs_1_, bf16[16,8,32,128]{3,2,1,0:T(8,128)(2,1)} %get-tuple-element.203.refs_2_, ...), custom_call_target="tpu_custom_call" | custom-call | bytes 7340032 | tf_op jit(solution)/shard_map/last_sums/pallas_call | solution.py:68
  194.8 4.2 %last_sums.3 = (f32[16,7,32,128]{3,2,1,0:T(8,128)}, f32[32,2048]{1,0:T(8,128)}, f32[32,2048]{1,0:T(8,128)}, f32[32,2048]{1,0:T(8,128)}) custom-call(bf16[2,16,6,32,128]{4,3,2,1,0:T(8,128)(2,1)} %get-tuple-element.205.refs_0_, bf16[2,16,6,32,128]{4,3,2,1,0:T(8,128)(2,1)} %get-tuple-element.206.refs_1_, bf16[16,6,32,128]{3,2,1,0:T(8,128)(2,1)S(1)} %copy-done.9, ...), custom_call_target="tpu_custom_call" | custom-call | bytes 9175040 | tf_op jit(solution)/shard_map/last_sums/pallas_call | solution.py:68
  199.0 7.7 %collective-permute-done.16 = bf16[256,2048]{1,0:T(8,128)(2,1)} collective-permute-done((bf16[256,2048]{1,0:T(8,128)(2,1)}, bf16[256,2048]{1,0:T(8,128)(2,1)}, u32[]{:S(2)}, u32[]{:S(2)}) %collective-permute-start.16) | collective-permute-done | bytes 1048608 | tf_op jit(solution)/shard_map/ppermute | solution.py:17
  208.4 3.6 %add_convert_fusion.2 = bf16[256,2048]{1,0:T(8,128)(2,1)} fusion(bf16[256,2048]{1,0:T(8,128)(2,1)} %collective-permute-done.17, f32[256,2048]{1,0:T(8,128)} %get-tuple-element.196, bf16[256,2048]{1,0:T(8,128)(2,1)} %collective-permute-done.16), kind=kLoop, calls=%fused_computation.2 | loop fusion | flops 2621440 | bytes 5242880 | tf_op jit(solution)/shard_map/convert_element_type | solution.py:630
  (55 shorter events, 23.0 us)
Async XLA Ops:
  0.6 61.1 %collective-permute-start.8 = (bf16[256,2048]{1,0:T(8,128)(2,1)}, bf16[256,2048]{1,0:T(8,128)(2,1)S(1)}, u32[]{:S(2)}, u32[]{:S(2)}) collective-permute-start(bf16[256,2048]{1,0:T(8,128)(2,1)} %param.16), channel_id=1, source_target_pairs={{0,4},{4,0},{8,12},{12,8},{1,5},{5,1},{9,13},{13,9},{2,6},{6,2},{1... | collective-permute-start | bytes 3145736 | tf_op jit(solution)/shard_map/ppermute | solution.py:17
  3.7 58.0 %collective-permute-start.9 = (bf16[256,2048]{1,0:T(8,128)(2,1)}, bf16[256,2048]{1,0:T(8,128)(2,1)S(1)}, u32[]{:S(2)}, u32[]{:S(2)}) collective-permute-start(bf16[256,2048]{1,0:T(8,128)(2,1)} %param.16), channel_id=1, source_target_pairs={{0,8},{4,12},{8,0},{12,4},{1,9},{5,13},{9,1},{13,5},{2,10},{6,14},... | collective-permute-start | bytes 3145736 | tf_op jit(solution)/shard_map/ppermute | solution.py:17
  6.3 55.5 %copy-start.11 = (bf16[128,2048]{1,0:T(8,128)(2,1)S(1)}, bf16[128,2048]{1,0:T(8,128)(2,1)}, u32[]{:S(2)}) copy-start(bf16[128,2048]{1,0:T(8,128)(2,1)} %param.21) | copy-start | bytes 1572868
  6.3 3.8 %copy-start.1 = (bf16[256,2048]{1,0:T(8,128)(2,1)S(1)}, bf16[256,2048]{1,0:T(8,128)(2,1)}, u32[]{:S(2)}) copy-start(bf16[256,2048]{1,0:T(8,128)(2,1)} %get-tuple-element.88.refs_0_.refs_1_) | copy-start | bytes 3145732 | tf_op jit(solution)/shard_map/cond
  9.6 42.8 %collective-permute-start.3 = (bf16[512,128]{1,0:T(8,128)(2,1)}, bf16[512,128]{1,0:T(8,128)(2,1)S(1)}, u32[]{:S(2)}, u32[]{:S(2)}) collective-permute-start(bf16[512,128]{1,0:T(8,128)(2,1)} %first_codes.1), channel_id=1, source_target_pairs={{0,4},{4,0},{8,12},{12,8},{1,5},{5,1},{9,13},{13,9},{2,6},{6,2},{1... | collective-permute-start | bytes 393224 | tf_op jit(solution)/shard_map/cond/branch_1_fun/ppermute | solution.py:17
  10.1 42.3 %copy-start.12 = (bf16[512,128]{1,0:T(8,128)(2,1)S(1)}, bf16[512,128]{1,0:T(8,128)(2,1)}, u32[]{:S(2)}) copy-start(bf16[512,128]{1,0:T(8,128)(2,1)} %first_codes.1) | copy-start | bytes 393220 | tf_op jit(solution)/shard_map/cond
  52.4 9.3 %collective-permute-start.10 = (bf16[512,128]{1,0:T(8,128)(2,1)S(1)}, bf16[512,128]{1,0:T(8,128)(2,1)S(1)}, u32[]{:S(2)}, u32[]{:S(2)}) collective-permute-start(bf16[512,128]{1,0:T(8,128)(2,1)S(1)} %get-tuple-element.185), channel_id=1, source_target_pairs={{0,8},{4,12},{8,0},{12,4},{1,9},{5,13},{9,1},{13,5},{2,10},{6,14},... | collective-permute-start | bytes 393224 | tf_op jit(solution)/shard_map/ppermute | solution.py:17
  55.3 49.0 %collective-permute-start.13 = (bf16[256,2048]{1,0:T(8,128)(2,1)}, bf16[256,2048]{1,0:T(8,128)(2,1)}, u32[]{:S(2)}, u32[]{:S(2)}) collective-permute-start(bf16[256,2048]{1,0:T(8,128)(2,1)} %get-tuple-element.187), channel_id=1, source_target_pairs={{0,4},{4,0},{8,12},{12,8},{1,5},{5,1},{9,13},{13,9},{2,6},{6,2},{1... | collective-permute-start | bytes 3145736 | tf_op jit(solution)/shard_map/ppermute | solution.py:17
  56.8 50.0 %collective-permute-start.14 = (bf16[256,2048]{1,0:T(8,128)(2,1)}, bf16[256,2048]{1,0:T(8,128)(2,1)}, u32[]{:S(2)}, u32[]{:S(2)}) collective-permute-start(bf16[256,2048]{1,0:T(8,128)(2,1)} %get-tuple-element.188), channel_id=1, source_target_pairs={{0,8},{4,12},{8,0},{12,4},{1,9},{5,13},{9,1},{13,5},{2,10},{6,14},... | collective-permute-start | bytes 3145736 | tf_op jit(solution)/shard_map/ppermute | solution.py:17
  61.8 1.0 copy-start.6
  61.8 1.3 copy-start.7
  63.1 7.9 %copy-start.2 = (bf16[256,2048]{1,0:T(8,128)(2,1)S(1)}, bf16[256,2048]{1,0:T(8,128)(2,1)}, u32[]{:S(2)}) copy-start(bf16[256,2048]{1,0:T(8,128)(2,1)} %get-tuple-element.107.refs_1_) | copy-start | bytes 3145732 | tf_op jit(solution)/shard_map/cond
  76.6 3.8 %collective-permute-start = (bf16[2,16,6,32,128]{4,3,2,1,0:T(8,128)(2,1)}, bf16[2,16,6,32,128]{4,3,2,1,0:T(8,128)(2,1)}, u32[]{:S(2)}, u32[]{:S(2)}) collective-permute-start(bf16[2,16,6,32,128]{4,3,2,1,0:T(8,128)(2,1)} %get-tuple-element.109), channel_id=1, source_target_pairs={{0,1},{1,0},{2,3},{3,2},{4,5},{5,4},{6,7},{7,6},{8,9},{9,8},{10,11... | collective-permute-start | bytes 4718600 | tf_op jit(solution)/shard_map/cond/branch_1_fun/ppermute | solution.py:17
  84.1 75.6 %collective-permute-start.11 = (bf16[256,2048]{1,0:T(8,128)(2,1)}, bf16[256,2048]{1,0:T(8,128)(2,1)S(1)}, u32[]{:S(2)}, u32[]{:S(2)}) collective-permute-start(bf16[256,2048]{1,0:T(8,128)(2,1)} %get-tuple-element.186), channel_id=1, source_target_pairs={{0,4},{4,0},{8,12},{12,8},{1,5},{5,1},{9,13},{13,9},{2,6},{6,2},{1... | collective-permute-start | bytes 3145736 | tf_op jit(solution)/shard_map/ppermute | solution.py:17
  84.5 75.2 %collective-permute-start.12 = (bf16[256,2048]{1,0:T(8,128)(2,1)}, bf16[256,2048]{1,0:T(8,128)(2,1)S(1)}, u32[]{:S(2)}, u32[]{:S(2)}) collective-permute-start(bf16[256,2048]{1,0:T(8,128)(2,1)} %get-tuple-element.186), channel_id=1, source_target_pairs={{0,8},{4,12},{8,0},{12,4},{1,9},{5,13},{9,1},{13,5},{2,10},{6,14},... | collective-permute-start | bytes 3145736 | tf_op jit(solution)/shard_map/ppermute | solution.py:17
  88.0 19.2 %collective-permute-start.15 = (bf16[16,6,32,128]{3,2,1,0:T(8,128)(2,1)}, bf16[16,6,32,128]{3,2,1,0:T(8,128)(2,1)S(1)}, u32[]{:S(2)}, u32[]{:S(2)}) collective-permute-start(bf16[16,6,32,128]{3,2,1,0:T(8,128)(2,1)} %get-tuple-element.191), channel_id=1, source_target_pairs={{0,2},{2,0},{1,3},{3,1},{4,6},{6,4},{5,7},{7,5},{8,10},{10,8},{9,1... | collective-permute-start | bytes 2359304 | tf_op jit(solution)/shard_map/ppermute | solution.py:17
  107.2 0.9 copy-start.8
  108.1 0.9 copy-start.10
  109.0 10.2 %copy-start.3 = (bf16[256,2048]{1,0:T(8,128)(2,1)S(1)}, bf16[256,2048]{1,0:T(8,128)(2,1)}, u32[]{:S(2)}) copy-start(bf16[256,2048]{1,0:T(8,128)(2,1)} %get-tuple-element.127.refs_2_) | copy-start | bytes 3145732 | tf_op jit(solution)/shard_map/cond
  125.6 4.5 %collective-permute-start.6 = (bf16[2,16,8,32,128]{4,3,2,1,0:T(8,128)(2,1)}, bf16[2,16,8,32,128]{4,3,2,1,0:T(8,128)(2,1)}, u32[]{:S(2)}, u32[]{:S(2)}) collective-permute-start(bf16[2,16,8,32,128]{4,3,2,1,0:T(8,128)(2,1)} %get-tuple-element.131), channel_id=1, source_target_pairs={{0,1},{1,0},{2,3},{3,2},{4,5},{5,4},{6,7},{7,6},{8,9},{9,8},{10,11... | collective-permute-start | bytes 6291464 | tf_op jit(solution)/shard_map/cond/branch_1_fun/ppermute | solution.py:17
  130.1 5.5 %copy-start.13 = (bf16[512,128]{1,0:T(8,128)(2,1)S(1)}, bf16[512,128]{1,0:T(8,128)(2,1)}, u32[]{:S(2)}) copy-start(bf16[512,128]{1,0:T(8,128)(2,1)} %get-tuple-element.123) | copy-start | bytes 393220 | tf_op jit(solution)/shard_map/cond
  134.2 25.5 %collective-permute-start.7 = (bf16[16,8,32,128]{3,2,1,0:T(8,128)(2,1)}, bf16[16,8,32,128]{3,2,1,0:T(8,128)(2,1)}, u32[]{:S(2)}, u32[]{:S(2)}) collective-permute-start(bf16[16,8,32,128]{3,2,1,0:T(8,128)(2,1)} %core_sums.4), channel_id=1, source_target_pairs={{0,2},{2,0},{1,3},{3,1},{4,6},{6,4},{5,7},{7,5},{8,10},{10,8},{9,1... | collective-permute-start | bytes 3145736 | tf_op jit(solution)/shard_map/cond/branch_1_fun/ppermute | solution.py:17
  135.7 15.6 %collective-permute-start.4 = (bf16[512,128]{1,0:T(8,128)(2,1)S(1)}, bf16[512,128]{1,0:T(8,128)(2,1)S(1)}, u32[]{:S(2)}, u32[]{:S(2)}) collective-permute-start(bf16[512,128]{1,0:T(8,128)(2,1)S(1)} %copy-done.13), channel_id=1, source_target_pairs={{0,4},{4,0},{8,12},{12,8},{1,5},{5,1},{9,13},{13,9},{2,6},{6,2},{1... | collective-permute-start | bytes 393224 | tf_op jit(solution)/shard_map/cond/branch_1_fun/ppermute | solution.py:17
  152.0 7.6 %collective-permute-start.5 = (bf16[512,128]{1,0:T(8,128)(2,1)}, bf16[512,128]{1,0:T(8,128)(2,1)}, u32[]{:S(2)}, u32[]{:S(2)}) collective-permute-start(bf16[512,128]{1,0:T(8,128)(2,1)} %add_convert_fusion.1), channel_id=1, source_target_pairs={{0,8},{4,12},{8,0},{12,4},{1,9},{5,13},{9,1},{13,5},{2,10},{6,14},... | collective-permute-start | bytes 393224 | tf_op jit(solution)/shard_map/cond/branch_1_fun/ppermute | solution.py:17
  159.7 47.0 %collective-permute-start.16 = (bf16[256,2048]{1,0:T(8,128)(2,1)}, bf16[256,2048]{1,0:T(8,128)(2,1)}, u32[]{:S(2)}, u32[]{:S(2)}) collective-permute-start(bf16[256,2048]{1,0:T(8,128)(2,1)} %get-tuple-element.199), channel_id=1, source_target_pairs={{0,4},{4,0},{8,12},{12,8},{1,5},{5,1},{9,13},{13,9},{2,6},{6,2},{1... | collective-permute-start | bytes 3145736 | tf_op jit(solution)/shard_map/ppermute | solution.py:17
  160.1 48.4 %collective-permute-start.17 = (bf16[256,2048]{1,0:T(8,128)(2,1)}, bf16[256,2048]{1,0:T(8,128)(2,1)}, u32[]{:S(2)}, u32[]{:S(2)}) collective-permute-start(bf16[256,2048]{1,0:T(8,128)(2,1)} %get-tuple-element.200), channel_id=1, source_target_pairs={{0,8},{4,12},{8,0},{12,4},{1,9},{5,13},{9,1},{13,5},{2,10},{6,14},... | collective-permute-start | bytes 3145736 | tf_op jit(solution)/shard_map/ppermute | solution.py:17
  163.3 1.0 copy-start.4
  163.3 1.4 copy-start.5
  164.6 13.3 %copy-start = (bf16[16,7,128,128]{3,2,1,0:T(8,128)(2,1)S(1)}, bf16[16,7,128,128]{3,2,1,0:T(8,128)(2,1)}, u32[]{:S(2)}) copy-start(bf16[16,7,128,128]{3,2,1,0:T(8,128)(2,1)} %get-tuple-element.144.refs_1_) | copy-start | bytes 11010052 | tf_op jit(solution)/shard_map/cond
  170.0 3.0 %collective-permute-start.1 = (bf16[2,16,4,32,128]{4,3,2,1,0:T(8,128)(2,1)}, bf16[2,16,4,32,128]{4,3,2,1,0:T(8,128)(2,1)}, u32[]{:S(2)}, u32[]{:S(2)}) collective-permute-start(bf16[2,16,4,32,128]{4,3,2,1,0:T(8,128)(2,1)} %get-tuple-element.146), channel_id=1, source_target_pairs={{0,1},{1,0},{2,3},{3,2},{4,5},{5,4},{6,7},{7,6},{8,9},{9,8},{10,11... | collective-permute-start | bytes 3145736 | tf_op jit(solution)/shard_map/cond/branch_1_fun/ppermute | solution.py:17
  176.5 14.3 %collective-permute-start.2 = (bf16[16,4,32,128]{3,2,1,0:T(8,128)(2,1)}, bf16[16,4,32,128]{3,2,1,0:T(8,128)(2,1)}, u32[]{:S(2)}, u32[]{:S(2)}) collective-permute-start(bf16[16,4,32,128]{3,2,1,0:T(8,128)(2,1)} %core_sums.5), channel_id=1, source_target_pairs={{0,2},{2,0},{1,3},{3,1},{4,6},{6,4},{5,7},{7,5},{8,10},{10,8},{9,1... | collective-permute-start | bytes 1572872 | tf_op jit(solution)/shard_map/cond/branch_1_fun/ppermute | solution.py:17
  190.7 4.1 %copy-start.9 = (bf16[16,6,32,128]{3,2,1,0:T(8,128)(2,1)S(1)}, bf16[16,6,32,128]{3,2,1,0:T(8,128)(2,1)}, u32[]{:S(2)}) copy-start(bf16[16,6,32,128]{3,2,1,0:T(8,128)(2,1)} %copy-done.8) | copy-start | bytes 2359300

commit v4 on v3

--- a/solution.py
+++ b/solution.py
@@ -72,7 +72,9 @@
         out_specs=outs,
         out_shape=out_shapes,
         scratch_shapes=scratch,
-        compiler_params=pltpu.CompilerParams(vmem_limit_bytes=VMEM_LIMIT),
+        compiler_params=pltpu.CompilerParams(
+            vmem_limit_bytes=VMEM_LIMIT if name != "input_grad" else 24 * 1024 * 1024
+        ),
         cost_estimate=pl.CostEstimate(flops=flops, bytes_accessed=moved, transcendentals=0),
         name=name,
     )(*args, *after)
@@ -309,15 +311,17 @@
             after,
         )
 
-    def hidden_grad(self, cotangent, w_out, backs, u_out, far_parts, slope, v_in, w_in, code_part, after=()):
+    def hidden_grad(self, cotangent, w_out, backs, u_out, far_parts, slope, v_in, w_in, code_part, cut, after=()):
         def finish(g, j, total, refs):
             s_ref, v_ref, w_ref, c_ref, pg_ref, code_ref = refs[:6]
-            outs = refs[6 : 6 + self.far]
+            outs = refs[6 : 6 + 2 * self.far]
             sum_ref = refs[-1]
             grad = (total * s_ref[:, self.cut(j)]).astype(BF16)
             pg_ref[:, self.cut(j)] = grad
             for k in range(self.far):
-                outs[k][:, self.cut(j)] = dot_nt(grad, w_ref[j, 1 + self.local + k]).astype(BF16)
+                part = dot_nt(grad, w_ref[j, 1 + self.local + k]).astype(BF16)
+                outs[k][:, self.cut(j)] = part[:cut]
+                outs[self.far + k][:, self.cut(j)] = part[cut:]
             part = dot_nt(grad, v_ref[:, self.cut(j)])
             if j == 0:
                 sum_ref[...] = jnp.where(g == 0, part, sum_ref[...] + part)
@@ -338,9 +342,11 @@
             far_parts,
             finish,
             [by_cols(self.rows, self.width), whole((2 * self.rows, self.rank))]
-            + [by_cols(self.rows, self.width)] * self.far,
+            + [by_cols(cut, self.width)] * self.far
+            + [by_cols(self.rows - cut, self.width)] * self.far,
             [shape_of((self.rows, self.cols)), shape_of((2 * self.rows, self.rank))]
-            + [shape_of((self.rows, self.cols))] * self.far,
+            + [shape_of((cut, self.cols))] * self.far
+            + [shape_of((self.rows - cut, self.cols))] * self.far,
             [slope, v_in, w_in, code_part],
             [
                 by_cols(self.rows, self.width),
@@ -352,7 +358,7 @@
             "hidden_grad",
             after,
         )
-        return got[0], got[1], got[2:]
+        return got[0], got[1], (got[2 : 2 + self.far], got[2 + self.far :])
 
     def input_grad(self, pre_grad, w_in, backs, u_in, after=()):
         def finish(g, j, total, refs):
@@ -506,26 +512,30 @@
                 shapes.append(shape_of((height, self.cols), F32))
         return call(body, (self.steps,), ins, outs, shapes, [], 0, args, "last_sums", after)
 
-    def final(self, local, far_parts, after=()):
-        def body(l_ref, *refs):
-            total = l_ref[...]
-            for ref in refs[:-1]:
-                total = total + ref[...].astype(F32)
-            refs[-1][...] = total.astype(BF16)
-
-        cols = by_cols(self.rows, self.width)
-        return call(
+    def final(self, local, far_parts, first, total=None):
+        height = far_parts[0].shape[0]
+        count = 0 if total is None else 1
+
+        def body(*refs):
+            refs = refs[count:]
+            value = refs[0][...]
+            for ref in refs[1:-1]:
+                value = value + ref[...].astype(F32)
+            refs[-1][...] = value.astype(BF16)
+
+        rows = pl.BlockSpec((height, self.width), lambda g: (first // height, g))
+        return pl.pallas_call(
             body,
-            (self.steps,),
-            [cols] * (1 + len(far_parts)),
-            [cols],
-            [shape_of((self.rows, self.cols))],
-            [],
-            0,
-            (local, *far_parts),
-            "final",
-            after,
-        )[0]
+            grid=(self.steps,),
+            in_specs=[pl.BlockSpec(memory_space=pl.ANY)] * count
+            + [rows]
+            + [by_cols(height, self.width)] * len(far_parts),
+            out_specs=rows,
+            out_shape=shape_of((self.rows, self.cols)),
+            input_output_aliases={0: 0} if count else {},
+            compiler_params=pltpu.CompilerParams(vmem_limit_bytes=24 * 1024 * 1024),
+            name="final",
+        )(*([total] if count else []), local, *far_parts)
 
 
 def shards(inputs, cotangent, w_in, w_out, u_in, v_in, u_out, v_out):
@@ -570,6 +580,8 @@
     def summed(parts):
         return by_chips(*by_cores(parts))
 
+    cut = layer.rows * 3 // 4
+
     def start_step(inputs, cotangent, w_out, u_in, v_out):
         products = layer.far_products(cotangent, w_out)
         return products, by_levels(layer.first_codes(inputs, cotangent, u_in, v_out))
@@ -585,18 +597,18 @@
     ):
         codes, backs = halves(first)
         pre_grad, code, products = layer.hidden_grad(
-            cotangent, w_out, backs, u_out, far_cot, slope, v_in, w_in, code, after=done
+            cotangent, w_out, backs, u_out, far_cot, slope, v_in, w_in, code, cut, after=done
         )
         parts = layer.weight_grads(cuts, pre_grad, acts=inputs, far_acts=far_inputs, codes=codes)
         return pre_grad, last_level(by_levels(code)), products, summed(parts)
 
-    def last_step(inputs, cotangent, w_in, w_out, v_out, u_in, act, far_acts, last, pre_grad):
+    def last_step(inputs, cotangent, w_out, v_out, act, far_acts, last):
         codes, backs = halves(last)
         parts = layer.weight_grads(
             cuts, cotangent, far_acts=far_acts, codes=codes, backs=backs, u_acts=inputs
         )
         output = layer.result(act, far_acts, w_out, codes, v_out, after=parts[:1])
-        return output, layer.input_grad(pre_grad, w_in, backs, u_in), summed(parts)
+        return output, summed(parts)
 
     far_inputs = to_partners([inputs] * layer.far)
     products, first = block(start_step, inputs, cotangent, w_out, u_in, v_out)
@@ -612,9 +624,11 @@
         inputs, cotangent, w_in, w_out, v_in, u_out, far_inputs, far_cot, slope, code, first,
         sums_early[2],
     )
-    far_pre = to_partners(pin(products, *far_acts))
-    output, local_grad, sums_late = block(
-        last_step, inputs, cotangent, w_in, w_out, v_out, u_in, act, far_acts, last, pre_grad
+    ready = pin(products[0], *far_acts)
+    far_pre = to_partners(ready)
+    far_rest = to_partners(pin(products[1], *ready))
+    output, sums_late = block(
+        last_step, inputs, cotangent, w_out, v_out, act, far_acts, last
     )
     near, slots = 1 + layer.local, layer.slots
     grad_w_in, grad_v_in = layer.last_sums(
@@ -624,10 +638,8 @@
         [sums_early, sums_late],
         [[(0, 0, near), (1, 0, layer.far)], (0, near), (1, layer.far), (1, layer.far + 1)],
     )
-    total = local_grad
-    for value in far_pre:
-        total = total + value.astype(F32)
-    in_grad = total.astype(BF16)
+    local_grad = layer.input_grad(pre_grad, w_in, halves(last)[1], u_in, after=[grad_v_out])
+    in_grad = layer.final(local_grad, far_rest, cut, layer.final(local_grad, far_pre, 0))
     return (
         output,
         in_grad,

time: 213 us -> 211 us (level)
  other arithmetic: 4.45 us -> 0.79 us
  Pallas kernels: 74.5 us -> 76.8 us
    convert_element_type x1 -> x0, other arithmetic: 3.64 us -> none  [shards(): in_grad = total.astype(BF16)]
    pallas_call x0 -> x2, Pallas kernels: none -> 3.18 us  [final(): pl.pallas_call(body, grid=(self.steps,), in_specs=[pl.BlockSpec(memory_sp...]
    unnamed x10 -> x26, local copies, waits for them, and re-layouts: 2.18 us -> 4.52 us
    cond x18 -> x14, local copies, waits for them, and re-layouts: 2.28 us -> 0.03 us
    ppermute x18 -> x20, waiting for transfers between devices: 104 us -> 102 us  [exchange(): return lax.ppermute(value, axis, pairs)]
    ppermute x18 -> x20, starting transfers between devices: 24.2 us -> 25.6 us  [exchange(): return lax.ppermute(value, axis, pairs)]
  transfers between devices with their start and end apart: 18 -> 20, of which waited for: 14 -> 12; matrix products, arithmetic and copies ran while one was open for 0% -> 0% of each run, Pallas kernels for 35% -> 36%
where the time goes in v4:
time: 211 us; the launch traced here: 210 us
  waiting for transfers between devices  102 us (48%)
  Pallas kernels  76.8 us (36%)
  starting transfers between devices  25.6 us (12%)
  local copies, waits for them, and re-layouts  4.54 us (2%)
    ppermute x20, waiting for transfers between devices, exchange(): return lax.ppermute(value, axis, pairs)  102 us
    pallas_call x14, Pallas kernels, call(): pl.pallas_call(kernel, grid=grid, in_specs=list(ins) + [pl.BlockSpec(memo...  73.6 us
    ppermute x20, starting transfers between devices, exchange(): return lax.ppermute(value, axis, pairs)  25.6 us
    unnamed x26, local copies, waits for them, and re-layouts  4.52 us
  transfers between devices with their start and end apart: 20, of which 12 were waited for; matrix products, arithmetic and copies ran while one was open for 0% of the time, Pallas kernels for 36%

profile of v4, /device:TPU:0, one launch (start us, length us, event | category | flops | bytes accessed | tf_op | source)
XLA Modules:
  0.0 210.1 jit_solution(17240458108015707776)
XLA Ops:
  0.6 3.1 %collective-permute-start.8 = (bf16[256,2048]{1,0:T(8,128)(2,1)}, bf16[256,2048]{1,0:T(8,128)(2,1)S(1)}, u32[]{:S(2)}, u32[]{:S(2)}) collective-permute-start(bf16[256,2048]{1,0:T(8,128)(2,1)} %param.16), channel_id=1, source_target_pairs={{0,4},{4,0},{8,12},{12,8},{1,5},{5,1},{9,13},{13,9},{2,6},{6,2},{1... | collective-permute-start | bytes 3145736 | tf_op jit(solution)/shard_map/ppermute | solution.py:17
  3.7 2.6 %collective-permute-start.9 = (bf16[256,2048]{1,0:T(8,128)(2,1)}, bf16[256,2048]{1,0:T(8,128)(2,1)S(1)}, u32[]{:S(2)}, u32[]{:S(2)}) collective-permute-start(bf16[256,2048]{1,0:T(8,128)(2,1)} %param.16), channel_id=1, source_target_pairs={{0,8},{4,12},{8,0},{12,4},{1,9},{5,13},{9,1},{13,5},{2,10},{6,14},... | collective-permute-start | bytes 3145736 | tf_op jit(solution)/shard_map/ppermute | solution.py:17
  6.3 46.1 %conditional.4 = (bf16[256,2048]{1,0:T(8,128)(2,1)}, bf16[256,2048]{1,0:T(8,128)(2,1)}, bf16[512,128]{1,0:T(8,128)(2,1)S(1)}) conditional(s32[]{:T(128)} %convert_element_type.24, () %tuple.42, (bf16[256,2048]{1,0:T(8,128)(2,1)}, bf16[16,7,128,128]{3,2,1,0:T(8,128)(2,1)}, bf16[256,2048]{1,0:T(8,128)(2,1)}, bf16[2048,128]{1,0:T(8,128)(2,1)}, ...), branch_computations={%region_0.0_spmd, %region_1.0_spmd} | conditional | flops 537133056 | bytes 15728760 | solution.py:570
  6.3 3.3 %first_codes.1 = bf16[512,128]{1,0:T(8,128)(2,1)} custom-call(bf16[256,2048]{1,0:T(8,128)(2,1)} %get-tuple-element.86.refs_0_, bf16[256,2048]{1,0:T(8,128)(2,1)} %get-tuple-element.82.refs_0_.refs_1_, bf16[2048,128]{1,0:T(8,128)(2,1)} %get-tuple-element.87.refs_2_, bf16[128,2048]{1,0:T(8,128)(2,1)} %get-tuple-element.88.refs_3_), custom_call_target="tpu_custom_call" | custom-call | flops 268435456 | bytes 3276800 | tf_op jit(solution)/shard_map/cond/branch_1_fun/first_codes/pallas_call | solution.py:68
  10.1 4.7 %far_products.1 = (bf16[256,2048]{1,0:T(8,128)(2,1)}, bf16[256,2048]{1,0:T(8,128)(2,1)}) custom-call(bf16[256,2048]{1,0:T(8,128)(2,1)S(1)} %copy-done.2, bf16[16,7,128,128]{3,2,1,0:T(8,128)(2,1)} %get-tuple-element.83.refs_1_), custom_call_target="tpu_custom_call" | custom-call | flops 268435456 | bytes 6815744 | tf_op jit(solution)/shard_map/cond/branch_1_fun/far_products/pallas_call | solution.py:68
  14.8 37.6 %collective-permute-done.3 = bf16[512,128]{1,0:T(8,128)(2,1)S(1)} collective-permute-done((bf16[512,128]{1,0:T(8,128)(2,1)}, bf16[512,128]{1,0:T(8,128)(2,1)S(1)}, u32[]{:S(2)}, u32[]{:S(2)}) %collective-permute-start.3) | collective-permute-done | bytes 131104 | tf_op jit(solution)/shard_map/cond/branch_1_fun/ppermute | solution.py:17
  52.4 2.9 %collective-permute-start.10 = (bf16[512,128]{1,0:T(8,128)(2,1)S(1)}, bf16[512,128]{1,0:T(8,128)(2,1)S(1)}, u32[]{:S(2)}, u32[]{:S(2)}) collective-permute-start(bf16[512,128]{1,0:T(8,128)(2,1)S(1)} %get-tuple-element.181), channel_id=1, source_target_pairs={{0,8},{4,12},{8,0},{12,4},{1,9},{5,13},{9,1},{13,5},{2,10},{6,14},... | collective-permute-start | bytes 393224 | tf_op jit(solution)/shard_map/ppermute | solution.py:17
  57.3 4.5 %collective-permute-done.10 = bf16[512,128]{1,0:T(8,128)(2,1)S(1)} collective-permute-done((bf16[512,128]{1,0:T(8,128)(2,1)S(1)}, bf16[512,128]{1,0:T(8,128)(2,1)S(1)}, u32[]{:S(2)}, u32[]{:S(2)}) %collective-permute-start.10) | collective-permute-done | bytes 131104 | tf_op jit(solution)/shard_map/ppermute | solution.py:17
  63.1 21.1 %conditional.5 = (bf16[256,2048]{1,0:T(8,128)(2,1)}, f32[256,2048]{1,0:T(8,128)}, bf16[256,128]{1,0:T(8,128)(2,1)S(1)}, bf16[2,16,6,32,128]{4,3,2,1,0:T(8,128)(2...) conditional(s32[]{:T(128)} %convert_element_type.24, () %tuple.41, ...), branch_computations={%region_2.0_spmd, %region_3.0_spmd} | conditional | flops 2013265920 | bytes 32309372 | solution.py:570
  63.1 7.9 %hidden.1 = (bf16[256,2048]{1,0:T(8,128)(2,1)}, f32[256,2048]{1,0:T(8,128)}, bf16[256,128]{1,0:T(8,128)(2,1)S(1)}) custom-call(bf16[256,2048]{1,0:T(8,128)(2,1)} %get-tuple-element.89.refs_0_, bf16[256,2048]{1,0:T(8,128)(2,1)S(1)} %get-tuple-element.90.refs_1_, bf16[256,2048]{1,0:T(8,128)(2,1)S(1)} %get-tuple-element.91.refs_2_, ...), custom_call_target="tpu_custom_call" | custom-call | flops 1207959552 | bytes 11337728 | tf_op jit(solution)/shard_map/cond/branch_1_fun/hidden/pallas_call | solution.py:68
  71.1 5.6 %weight_grads.3 = (bf16[2,16,6,32,128]{4,3,2,1,0:T(8,128)(2,1)}, bf16[2,16,6,32,128]{4,3,2,1,0:T(8,128)(2,1)}) custom-call(s32[2]{0:T(128)S(1)} %get-tuple-element.100.refs_0_, bf16[256,2048]{1,0:T(8,128)(2,1)S(1)} %copy-done.3, bf16[256,2048]{1,0:T(8,128)(2,1)} %get-tuple-element.226.refs_2_.refs_5_, ...), custom_call_target="tpu_custom_call" | custom-call | flops 805306368 | bytes 6553608 | tf_op jit(solution)/shard_map/cond/branch_1_fun/weight_grads/pallas_call | solution.py:68
  76.7 3.7 %collective-permute-done.refs_1_ = bf16[2,16,6,32,128]{4,3,2,1,0:T(8,128)(2,1)} collective-permute-done((bf16[2,16,6,32,128]{4,3,2,1,0:T(8,128)(2,1)}, bf16[2,16,6,32,128]{4,3,2,1,0:T(8,128)(2,1)}, u32[]{:S(2)}, u32[]{:S(2)}) %collective-permute-start) | collective-permute-done | bytes 1572896 | tf_op jit(solution)/shard_map/cond/branch_1_fun/ppermute | solution.py:17
  80.5 3.7 %core_sums.3 = bf16[16,6,32,128]{3,2,1,0:T(8,128)(2,1)} custom-call(bf16[2,16,6,32,128]{4,3,2,1,0:T(8,128)(2,1)} %get-tuple-element.229.refs_0_, bf16[2,16,6,32,128]{4,3,2,1,0:T(8,128)(2,1)} %collective-permute-done.refs_1_), custom_call_target="tpu_custom_call" | custom-call | bytes 3932160 | tf_op jit(solution)/shard_map/cond/branch_1_fun/core_sums/pallas_call | solution.py:68
  84.6 3.4 %collective-permute-start.12 = (bf16[256,2048]{1,0:T(8,128)(2,1)}, bf16[256,2048]{1,0:T(8,128)(2,1)S(1)}, u32[]{:S(2)}, u32[]{:S(2)}) collective-permute-start(bf16[256,2048]{1,0:T(8,128)(2,1)} %get-tuple-element.182), channel_id=1, source_target_pairs={{0,8},{4,12},{8,0},{12,4},{1,9},{5,13},{9,1},{13,5},{2,10},{6,14},... | collective-permute-start | bytes 3145736 | tf_op jit(solution)/shard_map/ppermute | solution.py:17
  89.5 14.7 %collective-permute-done.13 = bf16[256,2048]{1,0:T(8,128)(2,1)} collective-permute-done((bf16[256,2048]{1,0:T(8,128)(2,1)}, bf16[256,2048]{1,0:T(8,128)(2,1)}, u32[]{:S(2)}, u32[]{:S(2)}) %collective-permute-start.13) | collective-permute-done | bytes 1048608 | tf_op jit(solution)/shard_map/ppermute | solution.py:17
  108.2 51.3 %conditional.6 = (bf16[256,2048]{1,0:T(8,128)(2,1)}, bf16[512,128]{1,0:T(8,128)(2,1)}, bf16[512,128]{1,0:T(8,128)(2,1)}, bf16[192,2048]{1,0:T(8,128)(2,1)}, bf16...) conditional(s32[]{:T(128)} %convert_element_type.24, () %tuple.45, ...), branch_computations={%region_4.0_spmd, %region_5.0_spmd} | conditional | flops 1879310336 | bytes 49873200 | solution.py:570
  108.2 10.1 %hidden_grad.1 = (bf16[256,2048]{1,0:T(8,128)(2,1)}, bf16[512,128]{1,0:T(8,128)(2,1)}, bf16[192,2048]{1,0:T(8,128)(2,1)}, bf16[192,2048]{1,0:T(8,128)(2,1)}, bf1...) custom-call(bf16[256,2048]{1,0:T(8,128)(2,1)} %get-tuple-element.104.refs_0_, ...), custom_call_target="tpu_custom_call" | custom-call | flops 805306368 | bytes 17235968 | tf_op jit(solution)/shard_map/cond/branch_1_fun/hidden_grad/pallas_call | solution.py:68
  118.3 6.5 %weight_grads.4 = (bf16[2,16,8,32,128]{4,3,2,1,0:T(8,128)(2,1)}, bf16[2,16,8,32,128]{4,3,2,1,0:T(8,128)(2,1)}) custom-call(s32[2]{0:T(128)} %get-tuple-element.122.refs_0_, bf16[256,2048]{1,0:T(8,128)(2,1)} %get-tuple-element.242.refs_1_, bf16[256,2048]{1,0:T(8,128)(2,1)S(1)} %copy-done.4, bf16[256,2048]{1,0:T(8,128)(2,1)} %get-tuple-element.124.refs_3_, ...), custom_call_target="tpu_custom_call" | custom-call | flops 1073741824 | bytes 8650760 | tf_op jit(solution)/shard_map/cond/branch_1_fun/weight_grads/pallas_call | solution.py:68
  124.8 4.5 %collective-permute-done.6.refs_1_ = bf16[2,16,8,32,128]{4,3,2,1,0:T(8,128)(2,1)} collective-permute-done((bf16[2,16,8,32,128]{4,3,2,1,0:T(8,128)(2,1)}, bf16[2,16,8,32,128]{4,3,2,1,0:T(8,128)(2,1)}, u32[]{:S(2)}, u32[]{:S(2)}) %collective-permute-start.6) | collective-permute-done | bytes 2097184 | tf_op jit(solution)/shard_map/cond/branch_1_fun/ppermute | solution.py:17
  129.3 4.0 %core_sums.4 = bf16[16,8,32,128]{3,2,1,0:T(8,128)(2,1)} custom-call(bf16[2,16,8,32,128]{4,3,2,1,0:T(8,128)(2,1)} %get-tuple-element.249.refs_0_, bf16[2,16,8,32,128]{4,3,2,1,0:T(8,128)(2,1)} %collective-permute-done.6.refs_1_), custom_call_target="tpu_custom_call" | custom-call | bytes 5242880 | tf_op jit(solution)/shard_map/cond/branch_1_fun/core_sums/pallas_call | solution.py:68
  135.1 16.1 %collective-permute-done.4 = bf16[512,128]{1,0:T(8,128)(2,1)S(1)} collective-permute-done((bf16[512,128]{1,0:T(8,128)(2,1)S(1)}, bf16[512,128]{1,0:T(8,128)(2,1)S(1)}, u32[]{:S(2)}, u32[]{:S(2)}) %collective-permute-start.4) | collective-permute-done | bytes 131104 | tf_op jit(solution)/shard_map/cond/branch_1_fun/ppermute | solution.py:17
  153.0 6.5 %collective-permute-done.5 = bf16[512,128]{1,0:T(8,128)(2,1)} collective-permute-done((bf16[512,128]{1,0:T(8,128)(2,1)}, bf16[512,128]{1,0:T(8,128)(2,1)}, u32[]{:S(2)}, u32[]{:S(2)}) %collective-permute-start.5) | collective-permute-done | bytes 131104 | tf_op jit(solution)/shard_map/cond/branch_1_fun/ppermute | solution.py:17
  160.9 2.7 %collective-permute-start.17 = (bf16[192,2048]{1,0:T(8,128)(2,1)}, bf16[192,2048]{1,0:T(8,128)(2,1)S(1)}, u32[]{:S(2)}, u32[]{:S(2)}) collective-permute-start(bf16[192,2048]{1,0:T(8,128)(2,1)} %get-tuple-element.201.refs_3_), channel_id=1, source_target_pairs={{0,8},{4,12},{8,0},{12,4},{1,9},{5,13},{9,1},{13,5},{2,10},{6,14},... | collective-permute-start | bytes 2359304 | tf_op jit(solution)/shard_map/ppermute | solution.py:17
  165.8 25.8 %conditional.7 = (bf16[256,2048]{1,0:T(8,128)(2,1)}, bf16[2,16,4,32,128]{4,3,2,1,0:T(8,128)(2,1)}, bf16[2,16,4,32,128]{4,3,2,1,0:T(8,128)(2,1)}, bf16[16,4,32,128]{3,2,1,0:T(8,128)(2,1)}) conditional(s32[]{:T(128)} %convert_element_type.24, () %tuple.40, (s32[2]{0:T(128)S(1)}, bf16[256,2048]{1,0:T(8,128)(2,1)S(1)}, bf16[256,2048]{1,0:T(8,128)(2,1)}, ...), branch_computations={%region_6.0_spmd, %region_7.0_spmd} | conditional | flops 1744830464 | bytes 30671024 | solution.py:570
  165.8 5.0 %weight_grads.5 = (bf16[2,16,4,32,128]{4,3,2,1,0:T(8,128)(2,1)}, bf16[2,16,4,32,128]{4,3,2,1,0:T(8,128)(2,1)}) custom-call(s32[2]{0:T(128)S(1)} %get-tuple-element.135.refs_0_, bf16[256,2048]{1,0:T(8,128)(2,1)S(1)} %get-tuple-element.136.refs_1_, bf16[256,2048]{1,0:T(8,128)(2,1)} %get-tuple-element.129.refs_2_.refs_1_, ...), custom_call_target="tpu_custom_call" | custom-call | flops 536870912 | bytes 6815752 | tf_op jit(solution)/shard_map/cond/branch_1_fun/weight_grads/pallas_call | solution.py:68
  170.9 3.0 %collective-permute-done.1.refs_1_ = bf16[2,16,4,32,128]{4,3,2,1,0:T(8,128)(2,1)} collective-permute-done((bf16[2,16,4,32,128]{4,3,2,1,0:T(8,128)(2,1)}, bf16[2,16,4,32,128]{4,3,2,1,0:T(8,128)(2,1)}, u32[]{:S(2)}, u32[]{:S(2)}) %collective-permute-start.1) | collective-permute-done | bytes 1048608 | tf_op jit(solution)/shard_map/cond/branch_1_fun/ppermute | solution.py:17
  173.9 3.5 %core_sums.5 = bf16[16,4,32,128]{3,2,1,0:T(8,128)(2,1)} custom-call(bf16[2,16,4,32,128]{4,3,2,1,0:T(8,128)(2,1)} %get-tuple-element.257.refs_7_.refs_0_, bf16[2,16,4,32,128]{4,3,2,1,0:T(8,128)(2,1)} %collective-permute-done.1.refs_1_), custom_call_target="tpu_custom_call" | custom-call | bytes 2621440 | tf_op jit(solution)/shard_map/cond/branch_1_fun/core_sums/pallas_call | solution.py:68
  178.8 6.1 %result.1 = bf16[256,2048]{1,0:T(8,128)(2,1)} custom-call(bf16[256,2048]{1,0:T(8,128)(2,1)} %get-tuple-element.128.refs_0_, bf16[256,2048]{1,0:T(8,128)(2,1)S(1)} %copy-done.6, bf16[256,2048]{1,0:T(8,128)(2,1)} %get-tuple-element.130.refs_3_.refs_2_, bf16[16,7,128,128]{3,2,1,0:T(8,128)(2,1)} %get-tuple-element.131.refs_3_, ...), custom_call_target="tpu_custom_call" | custom-call | flops 1207959552 | bytes 8650752 | tf_op jit(solution)/shard_map/cond/branch_1_fun/result/pallas_call | solution.py:68
  184.9 6.7 %collective-permute-done.2 = bf16[16,4,32,128]{3,2,1,0:T(8,128)(2,1)} collective-permute-done((bf16[16,4,32,128]{3,2,1,0:T(8,128)(2,1)}, bf16[16,4,32,128]{3,2,1,0:T(8,128)(2,1)}, u32[]{:S(2)}, u32[]{:S(2)}) %collective-permute-start.2) | collective-permute-done | bytes 524320 | tf_op jit(solution)/shard_map/cond/branch_1_fun/ppermute | solution.py:17
  191.6 4.1 %last_sums.3 = (f32[16,7,32,128]{3,2,1,0:T(8,128)}, f32[32,2048]{1,0:T(8,128)}) custom-call(bf16[2,16,8,32,128]{4,3,2,1,0:T(8,128)(2,1)} %get-tuple-element.206.refs_0_, bf16[2,16,8,32,128]{4,3,2,1,0:T(8,128)(2,1)} %get-tuple-element.207.refs_1_, bf16[16,8,32,128]{3,2,1,0:T(8,128)(2,1)} %get-tuple-element.208.refs_2_, ...), custom_call_target="tpu_custom_call" | custom-call | bytes 7340032 | tf_op jit(solution)/shard_map/last_sums/pallas_call | solution.py:68
  195.7 4.2 %last_sums.2 = (f32[16,7,32,128]{3,2,1,0:T(8,128)}, f32[32,2048]{1,0:T(8,128)}, f32[32,2048]{1,0:T(8,128)}, f32[32,2048]{1,0:T(8,128)}) custom-call(bf16[2,16,6,32,128]{4,3,2,1,0:T(8,128)(2,1)} %get-tuple-element.192.refs_0_, bf16[2,16,6,32,128]{4,3,2,1,0:T(8,128)(2,1)} %get-tuple-element.193.refs_1_, bf16[16,6,32,128]{3,2,1,0:T(8,128)(2,1)S(1)} %copy-done.11, ...), custom_call_target="tpu_custom_call" | custom-call | bytes 9175040 | tf_op jit(solution)/shard_map/last_sums/pallas_call | solution.py:68
  200.9 4.8 %input_grad.1.refs_0_.refs_1_ = f32[256,2048]{1,0:T(8,128)S(1)} custom-call(bf16[256,2048]{1,0:T(8,128)(2,1)} %get-tuple-element.191.refs_0_, bf16[16,7,128,128]{3,2,1,0:T(8,128)(2,1)} %refs_1_.1, bf16[512,128]{1,0:T(8,128)(2,1)} %get-tuple-element.188.refs_2_, bf16[512,128]{1,0:T(8,128)(2,1)} %get-tuple-element.189.refs_3_, ...), custom_call_target="tpu_custom_call" | custom-call | flops 805306368 | bytes 7602176 | tf_op jit(solution)/shard_map/input_grad/pallas_call | solution.py:68
  (73 shorter events, 23.7 us)
Async XLA Ops:
  0.6 61.1 %collective-permute-start.8 = (bf16[256,2048]{1,0:T(8,128)(2,1)}, bf16[256,2048]{1,0:T(8,128)(2,1)S(1)}, u32[]{:S(2)}, u32[]{:S(2)}) collective-permute-start(bf16[256,2048]{1,0:T(8,128)(2,1)} %param.16), channel_id=1, source_target_pairs={{0,4},{4,0},{8,12},{12,8},{1,5},{5,1},{9,13},{13,9},{2,6},{6,2},{1... | collective-permute-start | bytes 3145736 | tf_op jit(solution)/shard_map/ppermute | solution.py:17
  3.7 58.0 %collective-permute-start.9 = (bf16[256,2048]{1,0:T(8,128)(2,1)}, bf16[256,2048]{1,0:T(8,128)(2,1)S(1)}, u32[]{:S(2)}, u32[]{:S(2)}) collective-permute-start(bf16[256,2048]{1,0:T(8,128)(2,1)} %param.16), channel_id=1, source_target_pairs={{0,8},{4,12},{8,0},{12,4},{1,9},{5,13},{9,1},{13,5},{2,10},{6,14},... | collective-permute-start | bytes 3145736 | tf_op jit(solution)/shard_map/ppermute | solution.py:17
  6.3 55.5 %copy-start.13 = (bf16[128,2048]{1,0:T(8,128)(2,1)S(1)}, bf16[128,2048]{1,0:T(8,128)(2,1)}, u32[]{:S(2)}) copy-start(bf16[128,2048]{1,0:T(8,128)(2,1)} %param.21) | copy-start | bytes 1572868
  9.6 42.8 %collective-permute-start.3 = (bf16[512,128]{1,0:T(8,128)(2,1)}, bf16[512,128]{1,0:T(8,128)(2,1)S(1)}, u32[]{:S(2)}, u32[]{:S(2)}) collective-permute-start(bf16[512,128]{1,0:T(8,128)(2,1)} %first_codes.1), channel_id=1, source_target_pairs={{0,4},{4,0},{8,12},{12,8},{1,5},{5,1},{9,13},{13,9},{2,6},{6,2},{1... | collective-permute-start | bytes 393224 | tf_op jit(solution)/shard_map/cond/branch_1_fun/ppermute | solution.py:17
  10.1 42.3 %copy-start.16 = (bf16[512,128]{1,0:T(8,128)(2,1)S(1)}, bf16[512,128]{1,0:T(8,128)(2,1)}, u32[]{:S(2)}) copy-start(bf16[512,128]{1,0:T(8,128)(2,1)} %first_codes.1) | copy-start | bytes 393220 | tf_op jit(solution)/shard_map/cond
  52.4 9.3 %collective-permute-start.10 = (bf16[512,128]{1,0:T(8,128)(2,1)S(1)}, bf16[512,128]{1,0:T(8,128)(2,1)S(1)}, u32[]{:S(2)}, u32[]{:S(2)}) collective-permute-start(bf16[512,128]{1,0:T(8,128)(2,1)S(1)} %get-tuple-element.181), channel_id=1, source_target_pairs={{0,8},{4,12},{8,0},{12,4},{1,9},{5,13},{9,1},{13,5},{2,10},{6,14},... | collective-permute-start | bytes 393224 | tf_op jit(solution)/shard_map/ppermute | solution.py:17
  55.3 49.0 %collective-permute-start.13 = (bf16[256,2048]{1,0:T(8,128)(2,1)}, bf16[256,2048]{1,0:T(8,128)(2,1)}, u32[]{:S(2)}, u32[]{:S(2)}) collective-permute-start(bf16[256,2048]{1,0:T(8,128)(2,1)} %get-tuple-element.183), channel_id=1, source_target_pairs={{0,4},{4,0},{8,12},{12,8},{1,5},{5,1},{9,13},{13,9},{2,6},{6,2},{1... | collective-permute-start | bytes 3145736 | tf_op jit(solution)/shard_map/ppermute | solution.py:17
  56.8 50.0 %collective-permute-start.14 = (bf16[256,2048]{1,0:T(8,128)(2,1)}, bf16[256,2048]{1,0:T(8,128)(2,1)}, u32[]{:S(2)}, u32[]{:S(2)}) collective-permute-start(bf16[256,2048]{1,0:T(8,128)(2,1)} %get-tuple-element.184), channel_id=1, source_target_pairs={{0,8},{4,12},{8,0},{12,4},{1,9},{5,13},{9,1},{13,5},{2,10},{6,14},... | collective-permute-start | bytes 3145736 | tf_op jit(solution)/shard_map/ppermute | solution.py:17
  57.3 4.5 %copy-start.18 = (s32[2]{0:T(128)}, s32[2]{0:T(128)S(1)}, u32[]{:S(2)}) copy-start(s32[2]{0:T(128)S(1)} %pad_add_fusion) | copy-start | bytes 28
  63.1 7.9 %copy-start.3 = (bf16[256,2048]{1,0:T(8,128)(2,1)S(1)}, bf16[256,2048]{1,0:T(8,128)(2,1)}, u32[]{:S(2)}) copy-start(bf16[256,2048]{1,0:T(8,128)(2,1)} %get-tuple-element.101.refs_1_) | copy-start | bytes 3145732 | tf_op jit(solution)/shard_map/cond
  76.7 3.8 %collective-permute-start = (bf16[2,16,6,32,128]{4,3,2,1,0:T(8,128)(2,1)}, bf16[2,16,6,32,128]{4,3,2,1,0:T(8,128)(2,1)}, u32[]{:S(2)}, u32[]{:S(2)}) collective-permute-start(bf16[2,16,6,32,128]{4,3,2,1,0:T(8,128)(2,1)} %get-tuple-element.103), channel_id=1, source_target_pairs={{0,1},{1,0},{2,3},{3,2},{4,5},{5,4},{6,7},{7,6},{8,9},{9,8},{10,11... | collective-permute-start | bytes 4718600 | tf_op jit(solution)/shard_map/cond/branch_1_fun/ppermute | solution.py:17
  84.2 75.3 %collective-permute-start.11 = (bf16[256,2048]{1,0:T(8,128)(2,1)}, bf16[256,2048]{1,0:T(8,128)(2,1)S(1)}, u32[]{:S(2)}, u32[]{:S(2)}) collective-permute-start(bf16[256,2048]{1,0:T(8,128)(2,1)} %get-tuple-element.182), channel_id=1, source_target_pairs={{0,4},{4,0},{8,12},{12,8},{1,5},{5,1},{9,13},{13,9},{2,6},{6,2},{1... | collective-permute-start | bytes 3145736 | tf_op jit(solution)/shard_map/ppermute | solution.py:17
  84.6 74.9 %collective-permute-start.12 = (bf16[256,2048]{1,0:T(8,128)(2,1)}, bf16[256,2048]{1,0:T(8,128)(2,1)S(1)}, u32[]{:S(2)}, u32[]{:S(2)}) collective-permute-start(bf16[256,2048]{1,0:T(8,128)(2,1)} %get-tuple-element.182), channel_id=1, source_target_pairs={{0,8},{4,12},{8,0},{12,4},{1,9},{5,13},{9,1},{13,5},{2,10},{6,14},... | collective-permute-start | bytes 3145736 | tf_op jit(solution)/shard_map/ppermute | solution.py:17
  88.1 19.2 %collective-permute-start.15 = (bf16[16,6,32,128]{3,2,1,0:T(8,128)(2,1)}, bf16[16,6,32,128]{3,2,1,0:T(8,128)(2,1)S(1)}, u32[]{:S(2)}, u32[]{:S(2)}) collective-permute-start(bf16[16,6,32,128]{3,2,1,0:T(8,128)(2,1)} %get-tuple-element.187), channel_id=1, source_target_pairs={{0,2},{2,0},{1,3},{3,1},{4,6},{6,4},{5,7},{7,5},{8,10},{10,8},{9,1... | collective-permute-start | bytes 2359304 | tf_op jit(solution)/shard_map/ppermute | solution.py:17
  108.2 10.1 %copy-start.4 = (bf16[256,2048]{1,0:T(8,128)(2,1)S(1)}, bf16[256,2048]{1,0:T(8,128)(2,1)}, u32[]{:S(2)}) copy-start(bf16[256,2048]{1,0:T(8,128)(2,1)} %get-tuple-element.123.refs_2_) | copy-start | bytes 3145732 | tf_op jit(solution)/shard_map/cond
  124.8 4.5 %collective-permute-start.6 = (bf16[2,16,8,32,128]{4,3,2,1,0:T(8,128)(2,1)}, bf16[2,16,8,32,128]{4,3,2,1,0:T(8,128)(2,1)}, u32[]{:S(2)}, u32[]{:S(2)}) collective-permute-start(bf16[2,16,8,32,128]{4,3,2,1,0:T(8,128)(2,1)} %get-tuple-element.127), channel_id=1, source_target_pairs={{0,1},{1,0},{2,3},{3,2},{4,5},{5,4},{6,7},{7,6},{8,9},{9,8},{10,11... | collective-permute-start | bytes 6291464 | tf_op jit(solution)/shard_map/cond/branch_1_fun/ppermute | solution.py:17
  129.3 5.5 %copy-start.17 = (bf16[512,128]{1,0:T(8,128)(2,1)S(1)}, bf16[512,128]{1,0:T(8,128)(2,1)}, u32[]{:S(2)}) copy-start(bf16[512,128]{1,0:T(8,128)(2,1)} %get-tuple-element.117) | copy-start | bytes 393220 | tf_op jit(solution)/shard_map/cond
  133.3 26.2 %collective-permute-start.7 = (bf16[16,8,32,128]{3,2,1,0:T(8,128)(2,1)}, bf16[16,8,32,128]{3,2,1,0:T(8,128)(2,1)}, u32[]{:S(2)}, u32[]{:S(2)}) collective-permute-start(bf16[16,8,32,128]{3,2,1,0:T(8,128)(2,1)} %core_sums.4), channel_id=1, source_target_pairs={{0,2},{2,0},{1,3},{3,1},{4,6},{6,4},{5,7},{7,5},{8,10},{10,8},{9,1... | collective-permute-start | bytes 3145736 | tf_op jit(solution)/shard_map/cond/branch_1_fun/ppermute | solution.py:17
  134.8 16.4 %collective-permute-start.4 = (bf16[512,128]{1,0:T(8,128)(2,1)S(1)}, bf16[512,128]{1,0:T(8,128)(2,1)S(1)}, u32[]{:S(2)}, u32[]{:S(2)}) collective-permute-start(bf16[512,128]{1,0:T(8,128)(2,1)S(1)} %copy-done.17), channel_id=1, source_target_pairs={{0,4},{4,0},{8,12},{12,8},{1,5},{5,1},{9,13},{13,9},{2,6},{6,2},{1... | collective-permute-start | bytes 393224 | tf_op jit(solution)/shard_map/cond/branch_1_fun/ppermute | solution.py:17
  151.9 7.6 %collective-permute-start.5 = (bf16[512,128]{1,0:T(8,128)(2,1)}, bf16[512,128]{1,0:T(8,128)(2,1)}, u32[]{:S(2)}, u32[]{:S(2)}) collective-permute-start(bf16[512,128]{1,0:T(8,128)(2,1)} %add_convert_fusion.1), channel_id=1, source_target_pairs={{0,8},{4,12},{8,0},{12,4},{1,9},{5,13},{9,1},{13,5},{2,10},{6,14},... | collective-permute-start | bytes 393224 | tf_op jit(solution)/shard_map/cond/branch_1_fun/ppermute | solution.py:17
  160.6 5.2 %copy-start.1 = (bf16[256,2048]{1,0:T(8,128)(2,1)S(1)}, bf16[256,2048]{1,0:T(8,128)(2,1)}, u32[]{:S(2)}) copy-start(bf16[256,2048]{1,0:T(8,128)(2,1)} %param.17) | copy-start | bytes 3145732
  160.6 5.2 %copy-start.19 = (s32[2]{0:T(128)S(1)}, s32[2]{0:T(128)}, u32[]{:S(2)}) copy-start(s32[2]{0:T(128)} %copy-done.18) | copy-start | bytes 28
  160.9 44.9 %collective-permute-start.16 = (bf16[192,2048]{1,0:T(8,128)(2,1)}, bf16[192,2048]{1,0:T(8,128)(2,1)S(1)}, u32[]{:S(2)}, u32[]{:S(2)}) collective-permute-start(bf16[192,2048]{1,0:T(8,128)(2,1)} %get-tuple-element.200.refs_2_), channel_id=1, source_target_pairs={{0,4},{4,0},{8,12},{12,8},{1,5},{5,1},{9,13},{13,9},{2,6},{6,2},{1... | collective-permute-start | bytes 2359304 | tf_op jit(solution)/shard_map/ppermute | solution.py:17
  160.9 44.9 %collective-permute-start.17 = (bf16[192,2048]{1,0:T(8,128)(2,1)}, bf16[192,2048]{1,0:T(8,128)(2,1)S(1)}, u32[]{:S(2)}, u32[]{:S(2)}) collective-permute-start(bf16[192,2048]{1,0:T(8,128)(2,1)} %get-tuple-element.201.refs_3_), channel_id=1, source_target_pairs={{0,8},{4,12},{8,0},{12,4},{1,9},{5,13},{9,1},{13,5},{2,10},{6,14},... | collective-permute-start | bytes 2359304 | tf_op jit(solution)/shard_map/ppermute | solution.py:17
  163.6 43.9 %collective-permute-start.18 = (bf16[64,2048]{1,0:T(8,128)(2,1)}, bf16[64,2048]{1,0:T(8,128)(2,1)S(1)}, u32[]{:S(2)}, u32[]{:S(2)}) collective-permute-start(bf16[64,2048]{1,0:T(8,128)(2,1)} %get-tuple-element.204), channel_id=1, source_target_pairs={{0,4},{4,0},{8,12},{12,8},{1,5},{5,1},{9,13},{13,9},{2,6},{6,2},{1... | collective-permute-start | bytes 786440 | tf_op jit(solution)/shard_map/ppermute | solution.py:17
  163.6 45.1 %collective-permute-start.19 = (bf16[64,2048]{1,0:T(8,128)(2,1)}, bf16[64,2048]{1,0:T(8,128)(2,1)S(1)}, u32[]{:S(2)}, u32[]{:S(2)}) collective-permute-start(bf16[64,2048]{1,0:T(8,128)(2,1)} %get-tuple-element.205), channel_id=1, source_target_pairs={{0,8},{4,12},{8,0},{12,4},{1,9},{5,13},{9,1},{13,5},{2,10},{6,14},... | collective-permute-start | bytes 786440 | tf_op jit(solution)/shard_map/ppermute | solution.py:17
  170.8 8.0 %copy-start.6 = (bf16[256,2048]{1,0:T(8,128)(2,1)S(1)}, bf16[256,2048]{1,0:T(8,128)(2,1)}, u32[]{:S(2)}) copy-start(bf16[256,2048]{1,0:T(8,128)(2,1)} %get-tuple-element.129.refs_2_.refs_1_) | copy-start | bytes 3145732 | tf_op jit(solution)/shard_map/cond
  170.8 8.0 %copy-start.14 = (bf16[128,2048]{1,0:T(8,128)(2,1)S(1)}, bf16[128,2048]{1,0:T(8,128)(2,1)}, u32[]{:S(2)}) copy-start(bf16[128,2048]{1,0:T(8,128)(2,1)} %get-tuple-element.134.refs_6_) | copy-start | bytes 1572868 | tf_op jit(solution)/shard_map/cond
  170.8 3.1 %collective-permute-start.1 = (bf16[2,16,4,32,128]{4,3,2,1,0:T(8,128)(2,1)}, bf16[2,16,4,32,128]{4,3,2,1,0:T(8,128)(2,1)}, u32[]{:S(2)}, u32[]{:S(2)}) collective-permute-start(bf16[2,16,4,32,128]{4,3,2,1,0:T(8,128)(2,1)} %get-tuple-element.139), channel_id=1, source_target_pairs={{0,1},{1,0},{2,3},{3,2},{4,5},{5,4},{6,7},{7,6},{8,9},{9,8},{10,11... | collective-permute-start | bytes 3145736 | tf_op jit(solution)/shard_map/cond/branch_1_fun/ppermute | solution.py:17
  177.3 14.3 %collective-permute-start.2 = (bf16[16,4,32,128]{3,2,1,0:T(8,128)(2,1)}, bf16[16,4,32,128]{3,2,1,0:T(8,128)(2,1)}, u32[]{:S(2)}, u32[]{:S(2)}) collective-permute-start(bf16[16,4,32,128]{3,2,1,0:T(8,128)(2,1)} %core_sums.5), channel_id=1, source_target_pairs={{0,2},{2,0},{1,3},{3,1},{4,6},{6,4},{5,7},{7,5},{8,10},{10,8},{9,1... | collective-permute-start | bytes 1572872 | tf_op jit(solution)/shard_map/cond/branch_1_fun/ppermute | solution.py:17
  191.6 4.1 %copy-start.11 = (bf16[16,6,32,128]{3,2,1,0:T(8,128)(2,1)S(1)}, bf16[16,6,32,128]{3,2,1,0:T(8,128)(2,1)}, u32[]{:S(2)}) copy-start(bf16[16,6,32,128]{3,2,1,0:T(8,128)(2,1)} %copy-done.10) | copy-start | bytes 2359300
  195.7 4.3 %copy-start.15 = (bf16[2048,128]{1,0:T(8,128)(2,1)S(1)}, bf16[2048,128]{1,0:T(8,128)(2,1)}, u32[]{:S(2)}) copy-start(bf16[2048,128]{1,0:T(8,128)(2,1)} %refs_4_.1) | copy-start | bytes 1572868
  (8 other events, 11.0 us)

commit v5 on v4

--- a/solution.py
+++ b/solution.py
@@ -9,7 +9,7 @@
 
 F32 = jnp.float32
 BF16 = jnp.bfloat16
-VMEM_LIMIT = 60 * 1024 * 1024
+VMEM_LIMIT = 28 * 1024 * 1024
 
 
 def exchange(value, axis, mask):

time: 211 us -> 209 us (level)
  Pallas kernels: 76.8 us -> 69 us
  waiting for transfers between devices: 102 us -> 107 us
    pallas_call x14, Pallas kernels: 73.6 us -> 65.8 us  [call(): pl.pallas_call(kernel, grid=grid, in_specs=list(ins) + [pl.BlockSpec(memo...]
    ppermute x20, waiting for transfers between devices: 102 us -> 107 us  [exchange(): return lax.ppermute(value, axis, pairs)]
  transfers between devices with their start and end apart: 20 -> 20, of which waited for: 12 -> 11; matrix products, arithmetic and copies ran while one was open for 0% -> 0% of each run, Pallas kernels for 36% -> 32%
where the time goes in v5:
time: 209 us; the launch traced here: 208 us
  waiting for transfers between devices  107 us (51%)
  Pallas kernels  69 us (33%)
  starting transfers between devices  25.7 us (12%)
  local copies, waits for them, and re-layouts  4.17 us (2%)
    ppermute x20, waiting for transfers between devices, exchange(): return lax.ppermute(value, axis, pairs)  107 us
    pallas_call x14, Pallas kernels, call(): pl.pallas_call(kernel, grid=grid, in_specs=list(ins) + [pl.BlockSpec(memo...  65.8 us
    ppermute x20, starting transfers between devices, exchange(): return lax.ppermute(value, axis, pairs)  25.7 us
  transfers between devices with their start and end apart: 20, of which 11 were waited for; matrix products, arithmetic and copies ran while one was open for 0% of the time, Pallas kernels for 32%

profile of v5, /device:TPU:0, one launch (start us, length us, event | category | flops | bytes accessed | tf_op | source)
XLA Modules:
  0.0 208.0 jit_solution(6126235745348914022)
XLA Ops:
  0.6 3.1 %collective-permute-start.8 = (bf16[256,2048]{1,0:T(8,128)(2,1)}, bf16[256,2048]{1,0:T(8,128)(2,1)S(1)}, u32[]{:S(2)}, u32[]{:S(2)}) collective-permute-start(bf16[256,2048]{1,0:T(8,128)(2,1)} %param.16), channel_id=1, source_target_pairs={{0,4},{4,0},{8,12},{12,8},{1,5},{5,1},{9,13},{13,9},{2,6},{6,2},{1... | collective-permute-start | bytes 3145736 | tf_op jit(solution)/shard_map/ppermute | solution.py:17
  3.7 2.6 %collective-permute-start.9 = (bf16[256,2048]{1,0:T(8,128)(2,1)}, bf16[256,2048]{1,0:T(8,128)(2,1)S(1)}, u32[]{:S(2)}, u32[]{:S(2)}) collective-permute-start(bf16[256,2048]{1,0:T(8,128)(2,1)} %param.16), channel_id=1, source_target_pairs={{0,8},{4,12},{8,0},{12,4},{1,9},{5,13},{9,1},{13,5},{2,10},{6,14},... | collective-permute-start | bytes 3145736 | tf_op jit(solution)/shard_map/ppermute | solution.py:17
  6.3 46.1 %conditional.4 = (bf16[256,2048]{1,0:T(8,128)(2,1)}, bf16[256,2048]{1,0:T(8,128)(2,1)}, bf16[512,128]{1,0:T(8,128)(2,1)S(1)}) conditional(s32[]{:T(128)} %convert_element_type.24, () %tuple.42, (bf16[256,2048]{1,0:T(8,128)(2,1)}, bf16[16,7,128,128]{3,2,1,0:T(8,128)(2,1)}, bf16[256,2048]{1,0:T(8,128)(2,1)}, bf16[2048,128]{1,0:T(8,128)(2,1)}, ...), branch_computations={%region_0.0_spmd, %region_1.0_spmd} | conditional | flops 537133056 | bytes 15204444 | solution.py:570
  6.3 2.7 %first_codes.1 = bf16[512,128]{1,0:T(8,128)(2,1)S(1)} custom-call(bf16[256,2048]{1,0:T(8,128)(2,1)} %get-tuple-element.86.refs_0_, bf16[256,2048]{1,0:T(8,128)(2,1)} %get-tuple-element.82.refs_0_.refs_1_, bf16[2048,128]{1,0:T(8,128)(2,1)} %get-tuple-element.87.refs_2_, bf16[128,2048]{1,0:T(8,128)(2,1)} %get-tuple-element.88.refs_3_), custom_call_target="tpu_custom_call" | custom-call | flops 268435456 | bytes 3276800 | tf_op jit(solution)/shard_map/cond/branch_1_fun/first_codes/pallas_call | solution.py:68
  9.5 4.6 %far_products.1 = (bf16[256,2048]{1,0:T(8,128)(2,1)}, bf16[256,2048]{1,0:T(8,128)(2,1)}) custom-call(bf16[256,2048]{1,0:T(8,128)(2,1)S(1)} %copy-done.4, bf16[16,7,128,128]{3,2,1,0:T(8,128)(2,1)} %get-tuple-element.83.refs_1_), custom_call_target="tpu_custom_call" | custom-call | flops 268435456 | bytes 6815744 | tf_op jit(solution)/shard_map/cond/branch_1_fun/far_products/pallas_call | solution.py:68
  14.2 38.2 %collective-permute-done.3 = bf16[512,128]{1,0:T(8,128)(2,1)S(1)} collective-permute-done((bf16[512,128]{1,0:T(8,128)(2,1)S(1)}, bf16[512,128]{1,0:T(8,128)(2,1)S(1)}, u32[]{:S(2)}, u32[]{:S(2)}) %collective-permute-start.3) | collective-permute-done | bytes 131104 | tf_op jit(solution)/shard_map/cond/branch_1_fun/ppermute | solution.py:17
  52.4 2.9 %collective-permute-start.10 = (bf16[512,128]{1,0:T(8,128)(2,1)S(1)}, bf16[512,128]{1,0:T(8,128)(2,1)S(1)}, u32[]{:S(2)}, u32[]{:S(2)}) collective-permute-start(bf16[512,128]{1,0:T(8,128)(2,1)S(1)} %get-tuple-element.181), channel_id=1, source_target_pairs={{0,8},{4,12},{8,0},{12,4},{1,9},{5,13},{9,1},{13,5},{2,10},{6,14},... | collective-permute-start | bytes 393224 | tf_op jit(solution)/shard_map/ppermute | solution.py:17
  57.3 4.5 %collective-permute-done.10 = bf16[512,128]{1,0:T(8,128)(2,1)S(1)} collective-permute-done((bf16[512,128]{1,0:T(8,128)(2,1)S(1)}, bf16[512,128]{1,0:T(8,128)(2,1)S(1)}, u32[]{:S(2)}, u32[]{:S(2)}) %collective-permute-start.10) | collective-permute-done | bytes 131104 | tf_op jit(solution)/shard_map/ppermute | solution.py:17
  62.7 19.3 %conditional.5 = (bf16[256,2048]{1,0:T(8,128)(2,1)}, f32[256,2048]{1,0:T(8,128)S(1)}, bf16[256,128]{1,0:T(8,128)(2,1)S(1)}, bf16[2,16,6,32,128]{4,3,2,1,0:T(8,12...) conditional(s32[]{:T(128)} %convert_element_type.24, () %tuple.41, ...), branch_computations={%region_2.0_spmd, %region_3.0_spmd} | conditional | flops 2013265920 | bytes 32309372 | solution.py:570
  62.7 7.7 %hidden.1 = (bf16[256,2048]{1,0:T(8,128)(2,1)}, f32[256,2048]{1,0:T(8,128)S(1)}, bf16[256,128]{1,0:T(8,128)(2,1)S(1)}) custom-call(bf16[256,2048]{1,0:T(8,128)(2,1)} %get-tuple-element.89.refs_0_, bf16[256,2048]{1,0:T(8,128)(2,1)S(1)} %get-tuple-element.90.refs_1_, bf16[256,2048]{1,0:T(8,128)(2,1)S(1)} %get-tuple-element.91.refs_2_, ...), custom_call_target="tpu_custom_call" | custom-call | flops 1207959552 | bytes 11337728 | tf_op jit(solution)/shard_map/cond/branch_1_fun/hidden/pallas_call | solution.py:68
  70.5 5.4 %weight_grads.3 = (bf16[2,16,6,32,128]{4,3,2,1,0:T(8,128)(2,1)}, bf16[2,16,6,32,128]{4,3,2,1,0:T(8,128)(2,1)S(1)}) custom-call(s32[2]{0:T(128)S(1)} %get-tuple-element.100.refs_0_, bf16[256,2048]{1,0:T(8,128)(2,1)S(1)} %copy-done.5, bf16[256,2048]{1,0:T(8,128)(2,1)} %get-tuple-element.226.refs_2_.refs_5_, ...), custom_call_target="tpu_custom_call" | custom-call | flops 805306368 | bytes 6553608 | tf_op jit(solution)/shard_map/cond/branch_1_fun/weight_grads/pallas_call | solution.py:68
  75.9 3.5 %collective-permute-done.refs_1_ = bf16[2,16,6,32,128]{4,3,2,1,0:T(8,128)(2,1)} collective-permute-done((bf16[2,16,6,32,128]{4,3,2,1,0:T(8,128)(2,1)S(1)}, bf16[2,16,6,32,128]{4,3,2,1,0:T(8,128)(2,1)}, u32[]{:S(2)}, u32[]{:S(2)}) %collective-permute-start) | collective-permute-done | bytes 1572896 | tf_op jit(solution)/shard_map/cond/branch_1_fun/ppermute | solution.py:17
  79.4 2.6 %core_sums.3 = bf16[16,6,32,128]{3,2,1,0:T(8,128)(2,1)S(1)} custom-call(bf16[2,16,6,32,128]{4,3,2,1,0:T(8,128)(2,1)} %get-tuple-element.229.refs_0_, bf16[2,16,6,32,128]{4,3,2,1,0:T(8,128)(2,1)} %collective-permute-done.refs_1_), custom_call_target="tpu_custom_call" | custom-call | bytes 3932160 | tf_op jit(solution)/shard_map/cond/branch_1_fun/core_sums/pallas_call | solution.py:68
  82.5 3.4 %collective-permute-start.12 = (bf16[256,2048]{1,0:T(8,128)(2,1)}, bf16[256,2048]{1,0:T(8,128)(2,1)S(1)}, u32[]{:S(2)}, u32[]{:S(2)}) collective-permute-start(bf16[256,2048]{1,0:T(8,128)(2,1)} %get-tuple-element.182), channel_id=1, source_target_pairs={{0,8},{4,12},{8,0},{12,4},{1,9},{5,13},{9,1},{13,5},{2,10},{6,14},... | collective-permute-start | bytes 3145736 | tf_op jit(solution)/shard_map/ppermute | solution.py:17
  87.5 16.8 %collective-permute-done.13 = bf16[256,2048]{1,0:T(8,128)(2,1)} collective-permute-done((bf16[256,2048]{1,0:T(8,128)(2,1)}, bf16[256,2048]{1,0:T(8,128)(2,1)}, u32[]{:S(2)}, u32[]{:S(2)}) %collective-permute-start.13) | collective-permute-done | bytes 1048608 | tf_op jit(solution)/shard_map/ppermute | solution.py:17
  104.3 2.6 %collective-permute-done.14 = bf16[256,2048]{1,0:T(8,128)(2,1)} collective-permute-done((bf16[256,2048]{1,0:T(8,128)(2,1)}, bf16[256,2048]{1,0:T(8,128)(2,1)}, u32[]{:S(2)}, u32[]{:S(2)}) %collective-permute-start.14) | collective-permute-done | bytes 1048608 | tf_op jit(solution)/shard_map/ppermute | solution.py:17
  107.8 51.8 %conditional.6 = (bf16[256,2048]{1,0:T(8,128)(2,1)}, bf16[512,128]{1,0:T(8,128)(2,1)}, bf16[512,128]{1,0:T(8,128)(2,1)}, bf16[192,2048]{1,0:T(8,128)(2,1)}, bf16...) conditional(s32[]{:T(128)} %convert_element_type.24, () %tuple.45, ...), branch_computations={%region_4.0_spmd, %region_5.0_spmd} | conditional | flops 1879310336 | bytes 53543216 | solution.py:570
  107.8 9.6 %hidden_grad.1 = (bf16[256,2048]{1,0:T(8,128)(2,1)}, bf16[512,128]{1,0:T(8,128)(2,1)S(1)}, bf16[192,2048]{1,0:T(8,128)(2,1)}, bf16[192,2048]{1,0:T(8,128)(2,1)},...) custom-call(bf16[256,2048]{1,0:T(8,128)(2,1)} %get-tuple-element.104.refs_0_, ...), custom_call_target="tpu_custom_call" | custom-call | flops 805306368 | bytes 17235968 | tf_op jit(solution)/shard_map/cond/branch_1_fun/hidden_grad/pallas_call | solution.py:68
  117.4 5.7 %weight_grads.4 = (bf16[2,16,8,32,128]{4,3,2,1,0:T(8,128)(2,1)}, bf16[2,16,8,32,128]{4,3,2,1,0:T(8,128)(2,1)S(1)}) custom-call(s32[2]{0:T(128)S(1)} %get-tuple-element.122.refs_0_, bf16[256,2048]{1,0:T(8,128)(2,1)} %get-tuple-element.242.refs_1_, bf16[256,2048]{1,0:T(8,128)(2,1)S(1)} %copy-done.6, bf16[256,2048]{1,0:T(8,128)(2,1)S(1)} %get-tuple-element.124.refs_3_, ...), custom_call_target="tpu_custom_call" | custom-call | flops 1073741824 | bytes 8650760 | tf_op jit(solution)/shard_map/cond/branch_1_fun/weight_grads/pallas_call | solution.py:68
  123.1 4.3 %collective-permute-done.6.refs_1_ = bf16[2,16,8,32,128]{4,3,2,1,0:T(8,128)(2,1)} collective-permute-done((bf16[2,16,8,32,128]{4,3,2,1,0:T(8,128)(2,1)S(1)}, bf16[2,16,8,32,128]{4,3,2,1,0:T(8,128)(2,1)}, u32[]{:S(2)}, u32[]{:S(2)}) %collective-permute-start.6) | collective-permute-done | bytes 2097184 | tf_op jit(solution)/shard_map/cond/branch_1_fun/ppermute | solution.py:17
  127.4 2.9 %core_sums.4 = bf16[16,8,32,128]{3,2,1,0:T(8,128)(2,1)S(1)} custom-call(bf16[2,16,8,32,128]{4,3,2,1,0:T(8,128)(2,1)} %get-tuple-element.249.refs_0_, bf16[2,16,8,32,128]{4,3,2,1,0:T(8,128)(2,1)} %collective-permute-done.6.refs_1_), custom_call_target="tpu_custom_call" | custom-call | bytes 5242880 | tf_op jit(solution)/shard_map/cond/branch_1_fun/core_sums/pallas_call | solution.py:68
  132.3 19.0 %collective-permute-done.4 = bf16[512,128]{1,0:T(8,128)(2,1)S(1)} collective-permute-done((bf16[512,128]{1,0:T(8,128)(2,1)S(1)}, bf16[512,128]{1,0:T(8,128)(2,1)S(1)}, u32[]{:S(2)}, u32[]{:S(2)}) %collective-permute-start.4) | collective-permute-done | bytes 131104 | tf_op jit(solution)/shard_map/cond/branch_1_fun/ppermute | solution.py:17
  153.1 6.5 %collective-permute-done.5 = bf16[512,128]{1,0:T(8,128)(2,1)} collective-permute-done((bf16[512,128]{1,0:T(8,128)(2,1)}, bf16[512,128]{1,0:T(8,128)(2,1)}, u32[]{:S(2)}, u32[]{:S(2)}) %collective-permute-start.5) | collective-permute-done | bytes 131104 | tf_op jit(solution)/shard_map/cond/branch_1_fun/ppermute | solution.py:17
  162.6 2.8 %collective-permute-start.19 = (bf16[64,2048]{1,0:T(8,128)(2,1)}, bf16[64,2048]{1,0:T(8,128)(2,1)S(1)}, u32[]{:S(2)}, u32[]{:S(2)}) collective-permute-start(bf16[64,2048]{1,0:T(8,128)(2,1)} %get-tuple-element.205), channel_id=1, source_target_pairs={{0,8},{4,12},{8,0},{12,4},{1,9},{5,13},{9,1},{13,5},{2,10},{6,14},... | collective-permute-start | bytes 786440 | tf_op jit(solution)/shard_map/ppermute | solution.py:17
  165.5 24.3 %conditional.7 = (bf16[256,2048]{1,0:T(8,128)(2,1)S(1)}, bf16[2,16,4,32,128]{4,3,2,1,0:T(8,128)(2,1)}, bf16[2,16,4,32,128]{4,3,2,1,0:T(8,128)(2,1)}, bf16[16,4,32,128]{3,2,1,0:T(8,128)(2,1)}) conditional(s32[]{:T(128)} %convert_element_type.24, () %tuple.40, (s32[2]{0:T(128)S(1)}, bf16[256,2048]{1,0:T(8,128)(2,1)S(1)}, bf16[256,2048]{1,0:T(8,128)(2,1)}, ...), branch_computations={%region_6.0_spmd, %region_7.0_spmd} | conditional | flops 1744830464 | bytes 49545448 | solution.py:570
  165.5 4.9 %weight_grads.5 = (bf16[2,16,4,32,128]{4,3,2,1,0:T(8,128)(2,1)}, bf16[2,16,4,32,128]{4,3,2,1,0:T(8,128)(2,1)S(1)}) custom-call(s32[2]{0:T(128)S(1)} %get-tuple-element.135.refs_0_, bf16[256,2048]{1,0:T(8,128)(2,1)S(1)} %get-tuple-element.136.refs_1_, bf16[256,2048]{1,0:T(8,128)(2,1)} %get-tuple-element.129.refs_2_.refs_1_, ...), custom_call_target="tpu_custom_call" | custom-call | flops 536870912 | bytes 6815752 | tf_op jit(solution)/shard_map/cond/branch_1_fun/weight_grads/pallas_call | solution.py:68
  170.5 2.8 %collective-permute-done.1.refs_1_ = bf16[2,16,4,32,128]{4,3,2,1,0:T(8,128)(2,1)} collective-permute-done((bf16[2,16,4,32,128]{4,3,2,1,0:T(8,128)(2,1)S(1)}, bf16[2,16,4,32,128]{4,3,2,1,0:T(8,128)(2,1)}, u32[]{:S(2)}, u32[]{:S(2)}) %collective-permute-start.1) | collective-permute-done | bytes 1048608 | tf_op jit(solution)/shard_map/cond/branch_1_fun/ppermute | solution.py:17
  177.2 4.5 %result.1 = bf16[256,2048]{1,0:T(8,128)(2,1)S(1)} custom-call(bf16[256,2048]{1,0:T(8,128)(2,1)} %get-tuple-element.128.refs_0_, bf16[256,2048]{1,0:T(8,128)(2,1)S(1)} %copy-done.8, bf16[256,2048]{1,0:T(8,128)(2,1)S(1)} %copy-done.10, bf16[16,7,128,128]{3,2,1,0:T(8,128)(2,1)S(1)} %copy-done.1, bf16[512,128]{1,0:T(8,128)(2,1)} %get-tuple-element.132.refs_4_.refs_6_, ...), custom_call_target="tpu_custom_call" | custom-call | flops 1207959552 | bytes 8650752 | tf_op jit(solution)/shard_map/cond/branch_1_fun/result/pallas_call | solution.py:68
  181.7 8.1 %collective-permute-done.2 = bf16[16,4,32,128]{3,2,1,0:T(8,128)(2,1)} collective-permute-done((bf16[16,4,32,128]{3,2,1,0:T(8,128)(2,1)S(1)}, bf16[16,4,32,128]{3,2,1,0:T(8,128)(2,1)}, u32[]{:S(2)}, u32[]{:S(2)}) %collective-permute-start.2) | collective-permute-done | bytes 524320 | tf_op jit(solution)/shard_map/cond/branch_1_fun/ppermute | solution.py:17
  189.8 4.4 %last_sums.3 = (f32[16,7,32,128]{3,2,1,0:T(8,128)}, f32[32,2048]{1,0:T(8,128)}) custom-call(bf16[2,16,8,32,128]{4,3,2,1,0:T(8,128)(2,1)} %get-tuple-element.206.refs_0_, bf16[2,16,8,32,128]{4,3,2,1,0:T(8,128)(2,1)} %get-tuple-element.207.refs_1_, bf16[16,8,32,128]{3,2,1,0:T(8,128)(2,1)} %get-tuple-element.208.refs_2_, ...), custom_call_target="tpu_custom_call" | custom-call | bytes 7340032 | tf_op jit(solution)/shard_map/last_sums/pallas_call | solution.py:68
  194.3 4.6 %last_sums.2 = (f32[16,7,32,128]{3,2,1,0:T(8,128)}, f32[32,2048]{1,0:T(8,128)}, f32[32,2048]{1,0:T(8,128)}, f32[32,2048]{1,0:T(8,128)}) custom-call(bf16[2,16,6,32,128]{4,3,2,1,0:T(8,128)(2,1)} %get-tuple-element.192.refs_0_, bf16[2,16,6,32,128]{4,3,2,1,0:T(8,128)(2,1)} %get-tuple-element.193.refs_1_, bf16[16,6,32,128]{3,2,1,0:T(8,128)(2,1)S(1)} %copy-done.15, ...), custom_call_target="tpu_custom_call" | custom-call | bytes 9175040 | tf_op jit(solution)/shard_map/last_sums/pallas_call | solution.py:68
  199.8 3.8 %input_grad.1.refs_0_.refs_1_ = f32[256,2048]{1,0:T(8,128)S(1)} custom-call(bf16[256,2048]{1,0:T(8,128)(2,1)} %get-tuple-element.191.refs_0_, bf16[16,7,128,128]{3,2,1,0:T(8,128)(2,1)S(1)} %copy-done.2, bf16[512,128]{1,0:T(8,128)(2,1)} %get-tuple-element.188.refs_2_, bf16[512,128]{1,0:T(8,128)(2,1)} %get-tuple-element.189.refs_3_, ...), custom_call_target="tpu_custom_call" | custom-call | flops 805306368 | bytes 7602176 | tf_op jit(solution)/shard_map/input_grad/pallas_call | solution.py:68
  (75 shorter events, 22.6 us)
Async XLA Ops:
  0.6 61.1 %collective-permute-start.8 = (bf16[256,2048]{1,0:T(8,128)(2,1)}, bf16[256,2048]{1,0:T(8,128)(2,1)S(1)}, u32[]{:S(2)}, u32[]{:S(2)}) collective-permute-start(bf16[256,2048]{1,0:T(8,128)(2,1)} %param.16), channel_id=1, source_target_pairs={{0,4},{4,0},{8,12},{12,8},{1,5},{5,1},{9,13},{13,9},{2,6},{6,2},{1... | collective-permute-start | bytes 3145736 | tf_op jit(solution)/shard_map/ppermute | solution.py:17
  3.7 58.0 %collective-permute-start.9 = (bf16[256,2048]{1,0:T(8,128)(2,1)}, bf16[256,2048]{1,0:T(8,128)(2,1)S(1)}, u32[]{:S(2)}, u32[]{:S(2)}) collective-permute-start(bf16[256,2048]{1,0:T(8,128)(2,1)} %param.16), channel_id=1, source_target_pairs={{0,8},{4,12},{8,0},{12,4},{1,9},{5,13},{9,1},{13,5},{2,10},{6,14},... | collective-permute-start | bytes 3145736 | tf_op jit(solution)/shard_map/ppermute | solution.py:17
  6.3 55.4 %copy-start.16 = (bf16[128,2048]{1,0:T(8,128)(2,1)S(1)}, bf16[128,2048]{1,0:T(8,128)(2,1)}, u32[]{:S(2)}) copy-start(bf16[128,2048]{1,0:T(8,128)(2,1)} %param.21) | copy-start | bytes 1572868
  6.3 55.4 %copy-start.17 = (bf16[2048,128]{1,0:T(8,128)(2,1)S(1)}, bf16[2048,128]{1,0:T(8,128)(2,1)}, u32[]{:S(2)}) copy-start(bf16[2048,128]{1,0:T(8,128)(2,1)} %param.22) | copy-start | bytes 1572868
  9.0 43.4 %collective-permute-start.3 = (bf16[512,128]{1,0:T(8,128)(2,1)S(1)}, bf16[512,128]{1,0:T(8,128)(2,1)S(1)}, u32[]{:S(2)}, u32[]{:S(2)}) collective-permute-start(bf16[512,128]{1,0:T(8,128)(2,1)S(1)} %first_codes.1), channel_id=1, source_target_pairs={{0,4},{4,0},{8,12},{12,8},{1,5},{5,1},{9,13},{13,9},{2,6},{6,2},{1... | collective-permute-start | bytes 393224 | tf_op jit(solution)/shard_map/cond/branch_1_fun/ppermute | solution.py:17
  52.4 9.3 %collective-permute-start.10 = (bf16[512,128]{1,0:T(8,128)(2,1)S(1)}, bf16[512,128]{1,0:T(8,128)(2,1)S(1)}, u32[]{:S(2)}, u32[]{:S(2)}) collective-permute-start(bf16[512,128]{1,0:T(8,128)(2,1)S(1)} %get-tuple-element.181), channel_id=1, source_target_pairs={{0,8},{4,12},{8,0},{12,4},{1,9},{5,13},{9,1},{13,5},{2,10},{6,14},... | collective-permute-start | bytes 393224 | tf_op jit(solution)/shard_map/ppermute | solution.py:17
  55.3 49.0 %collective-permute-start.13 = (bf16[256,2048]{1,0:T(8,128)(2,1)}, bf16[256,2048]{1,0:T(8,128)(2,1)}, u32[]{:S(2)}, u32[]{:S(2)}) collective-permute-start(bf16[256,2048]{1,0:T(8,128)(2,1)} %get-tuple-element.183), channel_id=1, source_target_pairs={{0,4},{4,0},{8,12},{12,8},{1,5},{5,1},{9,13},{13,9},{2,6},{6,2},{1... | collective-permute-start | bytes 3145736 | tf_op jit(solution)/shard_map/ppermute | solution.py:17
  56.8 50.0 %collective-permute-start.14 = (bf16[256,2048]{1,0:T(8,128)(2,1)}, bf16[256,2048]{1,0:T(8,128)(2,1)}, u32[]{:S(2)}, u32[]{:S(2)}) collective-permute-start(bf16[256,2048]{1,0:T(8,128)(2,1)} %get-tuple-element.184), channel_id=1, source_target_pairs={{0,8},{4,12},{8,0},{12,4},{1,9},{5,13},{9,1},{13,5},{2,10},{6,14},... | collective-permute-start | bytes 3145736 | tf_op jit(solution)/shard_map/ppermute | solution.py:17
  62.7 7.7 %copy-start.5 = (bf16[256,2048]{1,0:T(8,128)(2,1)S(1)}, bf16[256,2048]{1,0:T(8,128)(2,1)}, u32[]{:S(2)}) copy-start(bf16[256,2048]{1,0:T(8,128)(2,1)} %get-tuple-element.101.refs_1_) | copy-start | bytes 3145732 | tf_op jit(solution)/shard_map/cond
  75.9 3.5 %collective-permute-start = (bf16[2,16,6,32,128]{4,3,2,1,0:T(8,128)(2,1)S(1)}, bf16[2,16,6,32,128]{4,3,2,1,0:T(8,128)(2,1)}, u32[]{:S(2)}, u32[]{:S(2)}) collective-permute-start(bf16[2,16,6,32,128]{4,3,2,1,0:T(8,128)(2,1)S(1)} %get-tuple-element.103), channel_id=1, source_target_pairs={{0,1},{1,0},{2,3},{3,2},{4,5},{5,4},{6,7},{7,6},{8,9},{9,8},{10,11... | collective-permute-start | bytes 4718600 | tf_op jit(solution)/shard_map/cond/branch_1_fun/ppermute | solution.py:17
  82.1 77.5 %collective-permute-start.11 = (bf16[256,2048]{1,0:T(8,128)(2,1)}, bf16[256,2048]{1,0:T(8,128)(2,1)S(1)}, u32[]{:S(2)}, u32[]{:S(2)}) collective-permute-start(bf16[256,2048]{1,0:T(8,128)(2,1)} %get-tuple-element.182), channel_id=1, source_target_pairs={{0,4},{4,0},{8,12},{12,8},{1,5},{5,1},{9,13},{13,9},{2,6},{6,2},{1... | collective-permute-start | bytes 3145736 | tf_op jit(solution)/shard_map/ppermute | solution.py:17
  82.5 77.0 %collective-permute-start.12 = (bf16[256,2048]{1,0:T(8,128)(2,1)}, bf16[256,2048]{1,0:T(8,128)(2,1)S(1)}, u32[]{:S(2)}, u32[]{:S(2)}) collective-permute-start(bf16[256,2048]{1,0:T(8,128)(2,1)} %get-tuple-element.182), channel_id=1, source_target_pairs={{0,8},{4,12},{8,0},{12,4},{1,9},{5,13},{9,1},{13,5},{2,10},{6,14},... | collective-permute-start | bytes 3145736 | tf_op jit(solution)/shard_map/ppermute | solution.py:17
  86.0 20.9 %collective-permute-start.15 = (bf16[16,6,32,128]{3,2,1,0:T(8,128)(2,1)S(1)}, bf16[16,6,32,128]{3,2,1,0:T(8,128)(2,1)S(1)}, u32[]{:S(2)}, u32[]{:S(2)}) collective-permute-start(bf16[16,6,32,128]{3,2,1,0:T(8,128)(2,1)S(1)} %get-tuple-element.187), channel_id=1, source_target_pairs={{0,2},{2,0},{1,3},{3,1},{4,6},{6,4},{5,7},{7,5},{8,10},{10,8},{9,1... | collective-permute-start | bytes 2359304 | tf_op jit(solution)/shard_map/ppermute | solution.py:17
  107.8 9.6 %copy-start.6 = (bf16[256,2048]{1,0:T(8,128)(2,1)S(1)}, bf16[256,2048]{1,0:T(8,128)(2,1)}, u32[]{:S(2)}) copy-start(bf16[256,2048]{1,0:T(8,128)(2,1)} %get-tuple-element.123.refs_2_) | copy-start | bytes 3145732 | tf_op jit(solution)/shard_map/cond
  107.8 9.6 %copy-start.13 = (bf16[256,2048]{1,0:T(8,128)(2,1)S(1)}, bf16[256,2048]{1,0:T(8,128)(2,1)}, u32[]{:S(2)}) copy-start(bf16[256,2048]{1,0:T(8,128)(2,1)} %get-tuple-element.125.refs_4_) | copy-start | bytes 3145732 | tf_op jit(solution)/shard_map/cond
  123.1 4.3 %collective-permute-start.6 = (bf16[2,16,8,32,128]{4,3,2,1,0:T(8,128)(2,1)S(1)}, bf16[2,16,8,32,128]{4,3,2,1,0:T(8,128)(2,1)}, u32[]{:S(2)}, u32[]{:S(2)}) collective-permute-start(bf16[2,16,8,32,128]{4,3,2,1,0:T(8,128)(2,1)S(1)} %get-tuple-element.127), channel_id=1, source_target_pairs={{0,1},{1,0},{2,3},{3,2},{4,5},{5,4},{6,7},{7,6},{8,9},{9,8},{10,11... | collective-permute-start | bytes 6291464 | tf_op jit(solution)/shard_map/cond/branch_1_fun/ppermute | solution.py:17
  130.3 29.2 %collective-permute-start.7 = (bf16[16,8,32,128]{3,2,1,0:T(8,128)(2,1)S(1)}, bf16[16,8,32,128]{3,2,1,0:T(8,128)(2,1)}, u32[]{:S(2)}, u32[]{:S(2)}) collective-permute-start(bf16[16,8,32,128]{3,2,1,0:T(8,128)(2,1)S(1)} %core_sums.4), channel_id=1, source_target_pairs={{0,2},{2,0},{1,3},{3,1},{4,6},{6,4},{5,7},{7,5},{8,10},{10,8},{9,1... | collective-permute-start | bytes 3145736 | tf_op jit(solution)/shard_map/cond/branch_1_fun/ppermute | solution.py:17
  131.7 19.5 %collective-permute-start.4 = (bf16[512,128]{1,0:T(8,128)(2,1)S(1)}, bf16[512,128]{1,0:T(8,128)(2,1)S(1)}, u32[]{:S(2)}, u32[]{:S(2)}) collective-permute-start(bf16[512,128]{1,0:T(8,128)(2,1)S(1)} %get-tuple-element.117), channel_id=1, source_target_pairs={{0,4},{4,0},{8,12},{12,8},{1,5},{5,1},{9,13},{13,9},{2,6},{6,2},{1... | collective-permute-start | bytes 393224 | tf_op jit(solution)/shard_map/cond/branch_1_fun/ppermute | solution.py:17
  152.0 7.6 %collective-permute-start.5 = (bf16[512,128]{1,0:T(8,128)(2,1)}, bf16[512,128]{1,0:T(8,128)(2,1)}, u32[]{:S(2)}, u32[]{:S(2)}) collective-permute-start(bf16[512,128]{1,0:T(8,128)(2,1)} %add_convert_fusion.1), channel_id=1, source_target_pairs={{0,8},{4,12},{8,0},{12,4},{1,9},{5,13},{9,1},{13,5},{2,10},{6,14},... | collective-permute-start | bytes 393224 | tf_op jit(solution)/shard_map/cond/branch_1_fun/ppermute | solution.py:17
  159.6 5.9 %copy-start.3 = (bf16[256,2048]{1,0:T(8,128)(2,1)S(1)}, bf16[256,2048]{1,0:T(8,128)(2,1)}, u32[]{:S(2)}) copy-start(bf16[256,2048]{1,0:T(8,128)(2,1)} %param.17) | copy-start | bytes 3145732
  160.5 43.0 %collective-permute-start.16 = (bf16[192,2048]{1,0:T(8,128)(2,1)}, bf16[192,2048]{1,0:T(8,128)(2,1)S(1)}, u32[]{:S(2)}, u32[]{:S(2)}) collective-permute-start(bf16[192,2048]{1,0:T(8,128)(2,1)} %get-tuple-element.200.refs_2_), channel_id=1, source_target_pairs={{0,4},{4,0},{8,12},{12,8},{1,5},{5,1},{9,13},{13,9},{2,6},{6,2},{1... | collective-permute-start | bytes 2359304 | tf_op jit(solution)/shard_map/ppermute | solution.py:17
  160.9 42.7 %collective-permute-start.17 = (bf16[192,2048]{1,0:T(8,128)(2,1)}, bf16[192,2048]{1,0:T(8,128)(2,1)S(1)}, u32[]{:S(2)}, u32[]{:S(2)}) collective-permute-start(bf16[192,2048]{1,0:T(8,128)(2,1)} %get-tuple-element.201.refs_3_), channel_id=1, source_target_pairs={{0,8},{4,12},{8,0},{12,4},{1,9},{5,13},{9,1},{13,5},{2,10},{6,14},... | collective-permute-start | bytes 2359304 | tf_op jit(solution)/shard_map/ppermute | solution.py:17
  162.2 43.1 %collective-permute-start.18 = (bf16[64,2048]{1,0:T(8,128)(2,1)S(1)}, bf16[64,2048]{1,0:T(8,128)(2,1)S(1)}, u32[]{:S(2)}, u32[]{:S(2)}) collective-permute-start(bf16[64,2048]{1,0:T(8,128)(2,1)S(1)} %get-tuple-element.204), channel_id=1, source_target_pairs={{0,4},{4,0},{8,12},{12,8},{1,5},{5,1},{9,13},{13,9},{2,6},{6,2},{1... | collective-permute-start | bytes 786440 | tf_op jit(solution)/shard_map/ppermute | solution.py:17
  162.6 43.9 %collective-permute-start.19 = (bf16[64,2048]{1,0:T(8,128)(2,1)}, bf16[64,2048]{1,0:T(8,128)(2,1)S(1)}, u32[]{:S(2)}, u32[]{:S(2)}) collective-permute-start(bf16[64,2048]{1,0:T(8,128)(2,1)} %get-tuple-element.205), channel_id=1, source_target_pairs={{0,8},{4,12},{8,0},{12,4},{1,9},{5,13},{9,1},{13,5},{2,10},{6,14},... | collective-permute-start | bytes 786440 | tf_op jit(solution)/shard_map/ppermute | solution.py:17
  165.5 11.7 %copy-start.1 = (bf16[16,7,128,128]{3,2,1,0:T(8,128)(2,1)S(1)}, bf16[16,7,128,128]{3,2,1,0:T(8,128)(2,1)}, u32[]{:S(2)}) copy-start(bf16[16,7,128,128]{3,2,1,0:T(8,128)(2,1)} %get-tuple-element.131.refs_3_) | copy-start | bytes 11010052 | tf_op jit(solution)/shard_map/cond
  170.4 6.8 %copy-start.8 = (bf16[256,2048]{1,0:T(8,128)(2,1)S(1)}, bf16[256,2048]{1,0:T(8,128)(2,1)}, u32[]{:S(2)}) copy-start(bf16[256,2048]{1,0:T(8,128)(2,1)} %get-tuple-element.129.refs_2_.refs_1_) | copy-start | bytes 3145732 | tf_op jit(solution)/shard_map/cond
  170.4 6.8 %copy-start.10 = (bf16[256,2048]{1,0:T(8,128)(2,1)S(1)}, bf16[256,2048]{1,0:T(8,128)(2,1)}, u32[]{:S(2)}) copy-start(bf16[256,2048]{1,0:T(8,128)(2,1)} %get-tuple-element.130.refs_3_.refs_2_) | copy-start | bytes 3145732 | tf_op jit(solution)/shard_map/cond
  170.4 6.8 %copy-start.18 = (bf16[128,2048]{1,0:T(8,128)(2,1)S(1)}, bf16[128,2048]{1,0:T(8,128)(2,1)}, u32[]{:S(2)}) copy-start(bf16[128,2048]{1,0:T(8,128)(2,1)} %get-tuple-element.134.refs_6_) | copy-start | bytes 1572868 | tf_op jit(solution)/shard_map/cond
  170.5 2.9 %collective-permute-start.1 = (bf16[2,16,4,32,128]{4,3,2,1,0:T(8,128)(2,1)S(1)}, bf16[2,16,4,32,128]{4,3,2,1,0:T(8,128)(2,1)}, u32[]{:S(2)}, u32[]{:S(2)}) collective-permute-start(bf16[2,16,4,32,128]{4,3,2,1,0:T(8,128)(2,1)S(1)} %get-tuple-element.139), channel_id=1, source_target_pairs={{0,1},{1,0},{2,3},{3,2},{4,5},{5,4},{6,7},{7,6},{8,9},{9,8},{10,11... | collective-permute-start | bytes 3145736 | tf_op jit(solution)/shard_map/cond/branch_1_fun/ppermute | solution.py:17
  175.7 14.1 %collective-permute-start.2 = (bf16[16,4,32,128]{3,2,1,0:T(8,128)(2,1)S(1)}, bf16[16,4,32,128]{3,2,1,0:T(8,128)(2,1)}, u32[]{:S(2)}, u32[]{:S(2)}) collective-permute-start(bf16[16,4,32,128]{3,2,1,0:T(8,128)(2,1)S(1)} %core_sums.5), channel_id=1, source_target_pairs={{0,2},{2,0},{1,3},{3,1},{4,6},{6,4},{5,7},{7,5},{8,10},{10,8},{9,1... | collective-permute-start | bytes 1572872 | tf_op jit(solution)/shard_map/cond/branch_1_fun/ppermute | solution.py:17
  194.2 4.6 %copy-start.2 = (bf16[16,7,128,128]{3,2,1,0:T(8,128)(2,1)S(1)}, bf16[16,7,128,128]{3,2,1,0:T(8,128)(2,1)}, u32[]{:S(2)}) copy-start(bf16[16,7,128,128]{3,2,1,0:T(8,128)(2,1)} %refs_1_.1) | copy-start | bytes 11010052
  194.2 4.6 %copy-start.19 = (bf16[2048,128]{1,0:T(8,128)(2,1)S(1)}, bf16[2048,128]{1,0:T(8,128)(2,1)}, u32[]{:S(2)}) copy-start(bf16[2048,128]{1,0:T(8,128)(2,1)} %refs_4_.1) | copy-start | bytes 1572868
  (9 other events, 19.8 us)

commit v6 on v5

--- a/solution.py
+++ b/solution.py
@@ -624,9 +624,9 @@
         inputs, cotangent, w_in, w_out, v_in, u_out, far_inputs, far_cot, slope, code, first,
         sums_early[2],
     )
-    ready = pin(products[0], *far_acts)
-    far_pre = to_partners(ready)
-    far_rest = to_partners(pin(products[1], *ready))
+    ready = pin([*products[0], *products[1]], *far_acts)
+    far_pre = to_partners(ready[: layer.far])
+    far_rest = to_partners(ready[layer.far :])
     output, sums_late = block(
         last_step, inputs, cotangent, w_out, v_out, act, far_acts, last
     )

time: 209 us -> 209 us (level)
  transfers between devices with their start and end apart: 20 -> 20, of which waited for: 11 -> 11; matrix products, arithmetic and copies ran while one was open for 0% -> 0% of each run, Pallas kernels for 32% -> 33%
where the time goes in v6:
time: 209 us; the launch traced here: 208 us
  waiting for transfers between devices  107 us (51%)
  Pallas kernels  69.1 us (33%)
  starting transfers between devices  26 us (12%)
  local copies, waits for them, and re-layouts  4.16 us (2%)
    ppermute x20, waiting for transfers between devices, exchange(): return lax.ppermute(value, axis, pairs)  107 us
    pallas_call x14, Pallas kernels, call(): pl.pallas_call(kernel, grid=grid, in_specs=list(ins) + [pl.BlockSpec(memo...  65.9 us
    ppermute x20, starting transfers between devices, exchange(): return lax.ppermute(value, axis, pairs)  26 us
  transfers between devices with their start and end apart: 20, of which 11 were waited for; matrix products, arithmetic and copies ran while one was open for 0% of the time, Pallas kernels for 33%

profile of v6, /device:TPU:0, one launch (start us, length us, event | category | flops | bytes accessed | tf_op | source)
XLA Modules:
  0.0 208.0 jit_solution(16792218300184927273)
XLA Ops:
  0.6 3.1 %collective-permute-start.8 = (bf16[256,2048]{1,0:T(8,128)(2,1)}, bf16[256,2048]{1,0:T(8,128)(2,1)S(1)}, u32[]{:S(2)}, u32[]{:S(2)}) collective-permute-start(bf16[256,2048]{1,0:T(8,128)(2,1)} %param.16), channel_id=1, source_target_pairs={{0,4},{4,0},{8,12},{12,8},{1,5},{5,1},{9,13},{13,9},{2,6},{6,2},{1... | collective-permute-start | bytes 3145736 | tf_op jit(solution)/shard_map/ppermute | solution.py:17
  3.7 2.6 %collective-permute-start.9 = (bf16[256,2048]{1,0:T(8,128)(2,1)}, bf16[256,2048]{1,0:T(8,128)(2,1)S(1)}, u32[]{:S(2)}, u32[]{:S(2)}) collective-permute-start(bf16[256,2048]{1,0:T(8,128)(2,1)} %param.16), channel_id=1, source_target_pairs={{0,8},{4,12},{8,0},{12,4},{1,9},{5,13},{9,1},{13,5},{2,10},{6,14},... | collective-permute-start | bytes 3145736 | tf_op jit(solution)/shard_map/ppermute | solution.py:17
  6.3 46.1 %conditional.4 = (bf16[256,2048]{1,0:T(8,128)(2,1)}, bf16[256,2048]{1,0:T(8,128)(2,1)}, bf16[512,128]{1,0:T(8,128)(2,1)S(1)}) conditional(s32[]{:T(128)} %convert_element_type.24, () %tuple.42, (bf16[256,2048]{1,0:T(8,128)(2,1)}, bf16[16,7,128,128]{3,2,1,0:T(8,128)(2,1)}, bf16[256,2048]{1,0:T(8,128)(2,1)}, bf16[2048,128]{1,0:T(8,128)(2,1)}, ...), branch_computations={%region_0.0_spmd, %region_1.0_spmd} | conditional | flops 537133056 | bytes 15204444 | solution.py:570
  6.3 2.7 %first_codes.1 = bf16[512,128]{1,0:T(8,128)(2,1)S(1)} custom-call(bf16[256,2048]{1,0:T(8,128)(2,1)} %get-tuple-element.86.refs_0_, bf16[256,2048]{1,0:T(8,128)(2,1)} %get-tuple-element.82.refs_0_.refs_1_, bf16[2048,128]{1,0:T(8,128)(2,1)} %get-tuple-element.87.refs_2_, bf16[128,2048]{1,0:T(8,128)(2,1)} %get-tuple-element.88.refs_3_), custom_call_target="tpu_custom_call" | custom-call | flops 268435456 | bytes 3276800 | tf_op jit(solution)/shard_map/cond/branch_1_fun/first_codes/pallas_call | solution.py:68
  9.5 4.6 %far_products.1 = (bf16[256,2048]{1,0:T(8,128)(2,1)}, bf16[256,2048]{1,0:T(8,128)(2,1)}) custom-call(bf16[256,2048]{1,0:T(8,128)(2,1)S(1)} %copy-done.4, bf16[16,7,128,128]{3,2,1,0:T(8,128)(2,1)} %get-tuple-element.83.refs_1_), custom_call_target="tpu_custom_call" | custom-call | flops 268435456 | bytes 6815744 | tf_op jit(solution)/shard_map/cond/branch_1_fun/far_products/pallas_call | solution.py:68
  14.2 38.2 %collective-permute-done.3 = bf16[512,128]{1,0:T(8,128)(2,1)S(1)} collective-permute-done((bf16[512,128]{1,0:T(8,128)(2,1)S(1)}, bf16[512,128]{1,0:T(8,128)(2,1)S(1)}, u32[]{:S(2)}, u32[]{:S(2)}) %collective-permute-start.3) | collective-permute-done | bytes 131104 | tf_op jit(solution)/shard_map/cond/branch_1_fun/ppermute | solution.py:17
  52.4 2.9 %collective-permute-start.10 = (bf16[512,128]{1,0:T(8,128)(2,1)S(1)}, bf16[512,128]{1,0:T(8,128)(2,1)S(1)}, u32[]{:S(2)}, u32[]{:S(2)}) collective-permute-start(bf16[512,128]{1,0:T(8,128)(2,1)S(1)} %get-tuple-element.181), channel_id=1, source_target_pairs={{0,8},{4,12},{8,0},{12,4},{1,9},{5,13},{9,1},{13,5},{2,10},{6,14},... | collective-permute-start | bytes 393224 | tf_op jit(solution)/shard_map/ppermute | solution.py:17
  57.3 4.5 %collective-permute-done.10 = bf16[512,128]{1,0:T(8,128)(2,1)S(1)} collective-permute-done((bf16[512,128]{1,0:T(8,128)(2,1)S(1)}, bf16[512,128]{1,0:T(8,128)(2,1)S(1)}, u32[]{:S(2)}, u32[]{:S(2)}) %collective-permute-start.10) | collective-permute-done | bytes 131104 | tf_op jit(solution)/shard_map/ppermute | solution.py:17
  62.7 19.3 %conditional.5 = (bf16[256,2048]{1,0:T(8,128)(2,1)}, f32[256,2048]{1,0:T(8,128)S(1)}, bf16[256,128]{1,0:T(8,128)(2,1)S(1)}, bf16[2,16,6,32,128]{4,3,2,1,0:T(8,12...) conditional(s32[]{:T(128)} %convert_element_type.24, () %tuple.41, ...), branch_computations={%region_2.0_spmd, %region_3.0_spmd} | conditional | flops 2013265920 | bytes 32309372 | solution.py:570
  62.7 7.7 %hidden.1 = (bf16[256,2048]{1,0:T(8,128)(2,1)}, f32[256,2048]{1,0:T(8,128)S(1)}, bf16[256,128]{1,0:T(8,128)(2,1)S(1)}) custom-call(bf16[256,2048]{1,0:T(8,128)(2,1)} %get-tuple-element.89.refs_0_, bf16[256,2048]{1,0:T(8,128)(2,1)S(1)} %get-tuple-element.90.refs_1_, bf16[256,2048]{1,0:T(8,128)(2,1)S(1)} %get-tuple-element.91.refs_2_, ...), custom_call_target="tpu_custom_call" | custom-call | flops 1207959552 | bytes 11337728 | tf_op jit(solution)/shard_map/cond/branch_1_fun/hidden/pallas_call | solution.py:68
  70.5 5.4 %weight_grads.3 = (bf16[2,16,6,32,128]{4,3,2,1,0:T(8,128)(2,1)}, bf16[2,16,6,32,128]{4,3,2,1,0:T(8,128)(2,1)S(1)}) custom-call(s32[2]{0:T(128)S(1)} %get-tuple-element.100.refs_0_, bf16[256,2048]{1,0:T(8,128)(2,1)S(1)} %copy-done.5, bf16[256,2048]{1,0:T(8,128)(2,1)} %get-tuple-element.226.refs_2_.refs_5_, ...), custom_call_target="tpu_custom_call" | custom-call | flops 805306368 | bytes 6553608 | tf_op jit(solution)/shard_map/cond/branch_1_fun/weight_grads/pallas_call | solution.py:68
  75.9 3.5 %collective-permute-done.refs_1_ = bf16[2,16,6,32,128]{4,3,2,1,0:T(8,128)(2,1)} collective-permute-done((bf16[2,16,6,32,128]{4,3,2,1,0:T(8,128)(2,1)S(1)}, bf16[2,16,6,32,128]{4,3,2,1,0:T(8,128)(2,1)}, u32[]{:S(2)}, u32[]{:S(2)}) %collective-permute-start) | collective-permute-done | bytes 1572896 | tf_op jit(solution)/shard_map/cond/branch_1_fun/ppermute | solution.py:17
  79.4 2.6 %core_sums.3 = bf16[16,6,32,128]{3,2,1,0:T(8,128)(2,1)S(1)} custom-call(bf16[2,16,6,32,128]{4,3,2,1,0:T(8,128)(2,1)} %get-tuple-element.229.refs_0_, bf16[2,16,6,32,128]{4,3,2,1,0:T(8,128)(2,1)} %collective-permute-done.refs_1_), custom_call_target="tpu_custom_call" | custom-call | bytes 3932160 | tf_op jit(solution)/shard_map/cond/branch_1_fun/core_sums/pallas_call | solution.py:68
  82.5 3.4 %collective-permute-start.12 = (bf16[256,2048]{1,0:T(8,128)(2,1)}, bf16[256,2048]{1,0:T(8,128)(2,1)S(1)}, u32[]{:S(2)}, u32[]{:S(2)}) collective-permute-start(bf16[256,2048]{1,0:T(8,128)(2,1)} %get-tuple-element.182), channel_id=1, source_target_pairs={{0,8},{4,12},{8,0},{12,4},{1,9},{5,13},{9,1},{13,5},{2,10},{6,14},... | collective-permute-start | bytes 3145736 | tf_op jit(solution)/shard_map/ppermute | solution.py:17
  87.5 16.8 %collective-permute-done.13 = bf16[256,2048]{1,0:T(8,128)(2,1)} collective-permute-done((bf16[256,2048]{1,0:T(8,128)(2,1)}, bf16[256,2048]{1,0:T(8,128)(2,1)}, u32[]{:S(2)}, u32[]{:S(2)}) %collective-permute-start.13) | collective-permute-done | bytes 1048608 | tf_op jit(solution)/shard_map/ppermute | solution.py:17
  104.3 2.6 %collective-permute-done.14 = bf16[256,2048]{1,0:T(8,128)(2,1)} collective-permute-done((bf16[256,2048]{1,0:T(8,128)(2,1)}, bf16[256,2048]{1,0:T(8,128)(2,1)}, u32[]{:S(2)}, u32[]{:S(2)}) %collective-permute-start.14) | collective-permute-done | bytes 1048608 | tf_op jit(solution)/shard_map/ppermute | solution.py:17
  107.8 51.8 %conditional.6 = (bf16[256,2048]{1,0:T(8,128)(2,1)}, bf16[512,128]{1,0:T(8,128)(2,1)}, bf16[512,128]{1,0:T(8,128)(2,1)}, bf16[192,2048]{1,0:T(8,128)(2,1)}, bf16...) conditional(s32[]{:T(128)} %convert_element_type.24, () %tuple.45, ...), branch_computations={%region_4.0_spmd, %region_5.0_spmd} | conditional | flops 1879310336 | bytes 53543216 | solution.py:570
  107.8 9.6 %hidden_grad.1 = (bf16[256,2048]{1,0:T(8,128)(2,1)}, bf16[512,128]{1,0:T(8,128)(2,1)S(1)}, bf16[192,2048]{1,0:T(8,128)(2,1)}, bf16[192,2048]{1,0:T(8,128)(2,1)},...) custom-call(bf16[256,2048]{1,0:T(8,128)(2,1)} %get-tuple-element.104.refs_0_, ...), custom_call_target="tpu_custom_call" | custom-call | flops 805306368 | bytes 17235968 | tf_op jit(solution)/shard_map/cond/branch_1_fun/hidden_grad/pallas_call | solution.py:68
  117.4 5.7 %weight_grads.4 = (bf16[2,16,8,32,128]{4,3,2,1,0:T(8,128)(2,1)}, bf16[2,16,8,32,128]{4,3,2,1,0:T(8,128)(2,1)S(1)}) custom-call(s32[2]{0:T(128)S(1)} %get-tuple-element.122.refs_0_, bf16[256,2048]{1,0:T(8,128)(2,1)} %get-tuple-element.242.refs_1_, bf16[256,2048]{1,0:T(8,128)(2,1)S(1)} %copy-done.6, bf16[256,2048]{1,0:T(8,128)(2,1)S(1)} %get-tuple-element.124.refs_3_, ...), custom_call_target="tpu_custom_call" | custom-call | flops 1073741824 | bytes 8650760 | tf_op jit(solution)/shard_map/cond/branch_1_fun/weight_grads/pallas_call | solution.py:68
  123.1 4.3 %collective-permute-done.6.refs_1_ = bf16[2,16,8,32,128]{4,3,2,1,0:T(8,128)(2,1)} collective-permute-done((bf16[2,16,8,32,128]{4,3,2,1,0:T(8,128)(2,1)S(1)}, bf16[2,16,8,32,128]{4,3,2,1,0:T(8,128)(2,1)}, u32[]{:S(2)}, u32[]{:S(2)}) %collective-permute-start.6) | collective-permute-done | bytes 2097184 | tf_op jit(solution)/shard_map/cond/branch_1_fun/ppermute | solution.py:17
  127.4 2.9 %core_sums.4 = bf16[16,8,32,128]{3,2,1,0:T(8,128)(2,1)S(1)} custom-call(bf16[2,16,8,32,128]{4,3,2,1,0:T(8,128)(2,1)} %get-tuple-element.249.refs_0_, bf16[2,16,8,32,128]{4,3,2,1,0:T(8,128)(2,1)} %collective-permute-done.6.refs_1_), custom_call_target="tpu_custom_call" | custom-call | bytes 5242880 | tf_op jit(solution)/shard_map/cond/branch_1_fun/core_sums/pallas_call | solution.py:68
  132.3 18.9 %collective-permute-done.4 = bf16[512,128]{1,0:T(8,128)(2,1)S(1)} collective-permute-done((bf16[512,128]{1,0:T(8,128)(2,1)S(1)}, bf16[512,128]{1,0:T(8,128)(2,1)S(1)}, u32[]{:S(2)}, u32[]{:S(2)}) %collective-permute-start.4) | collective-permute-done | bytes 131104 | tf_op jit(solution)/shard_map/cond/branch_1_fun/ppermute | solution.py:17
  153.0 6.5 %collective-permute-done.5 = bf16[512,128]{1,0:T(8,128)(2,1)} collective-permute-done((bf16[512,128]{1,0:T(8,128)(2,1)}, bf16[512,128]{1,0:T(8,128)(2,1)}, u32[]{:S(2)}, u32[]{:S(2)}) %collective-permute-start.5) | collective-permute-done | bytes 131104 | tf_op jit(solution)/shard_map/cond/branch_1_fun/ppermute | solution.py:17
  162.9 2.9 %collective-permute-start.19 = (bf16[64,2048]{1,0:T(8,128)(2,1)}, bf16[64,2048]{1,0:T(8,128)(2,1)S(1)}, u32[]{:S(2)}, u32[]{:S(2)}) collective-permute-start(bf16[64,2048]{1,0:T(8,128)(2,1)} %get-tuple-element.205), channel_id=1, source_target_pairs={{0,8},{4,12},{8,0},{12,4},{1,9},{5,13},{9,1},{13,5},{2,10},{6,14},... | collective-permute-start | bytes 786440 | tf_op jit(solution)/shard_map/ppermute | solution.py:17
  165.8 24.4 %conditional.7 = (bf16[256,2048]{1,0:T(8,128)(2,1)S(1)}, bf16[2,16,4,32,128]{4,3,2,1,0:T(8,128)(2,1)}, bf16[2,16,4,32,128]{4,3,2,1,0:T(8,128)(2,1)}, bf16[16,4,32,128]{3,2,1,0:T(8,128)(2,1)}) conditional(s32[]{:T(128)} %convert_element_type.24, () %tuple.40, (s32[2]{0:T(128)S(1)}, bf16[256,2048]{1,0:T(8,128)(2,1)S(1)}, bf16[256,2048]{1,0:T(8,128)(2,1)}, ...), branch_computations={%region_6.0_spmd, %region_7.0_spmd} | conditional | flops 1744830464 | bytes 49545448 | solution.py:570
  165.8 5.0 %weight_grads.5 = (bf16[2,16,4,32,128]{4,3,2,1,0:T(8,128)(2,1)}, bf16[2,16,4,32,128]{4,3,2,1,0:T(8,128)(2,1)S(1)}) custom-call(s32[2]{0:T(128)S(1)} %get-tuple-element.135.refs_0_, bf16[256,2048]{1,0:T(8,128)(2,1)S(1)} %get-tuple-element.136.refs_1_, bf16[256,2048]{1,0:T(8,128)(2,1)} %get-tuple-element.129.refs_2_.refs_1_, ...), custom_call_target="tpu_custom_call" | custom-call | flops 536870912 | bytes 6815752 | tf_op jit(solution)/shard_map/cond/branch_1_fun/weight_grads/pallas_call | solution.py:68
  170.9 2.8 %collective-permute-done.1.refs_1_ = bf16[2,16,4,32,128]{4,3,2,1,0:T(8,128)(2,1)} collective-permute-done((bf16[2,16,4,32,128]{4,3,2,1,0:T(8,128)(2,1)S(1)}, bf16[2,16,4,32,128]{4,3,2,1,0:T(8,128)(2,1)}, u32[]{:S(2)}, u32[]{:S(2)}) %collective-permute-start.1) | collective-permute-done | bytes 1048608 | tf_op jit(solution)/shard_map/cond/branch_1_fun/ppermute | solution.py:17
  177.6 4.5 %result.1 = bf16[256,2048]{1,0:T(8,128)(2,1)S(1)} custom-call(bf16[256,2048]{1,0:T(8,128)(2,1)} %get-tuple-element.128.refs_0_, bf16[256,2048]{1,0:T(8,128)(2,1)S(1)} %copy-done.8, bf16[256,2048]{1,0:T(8,128)(2,1)S(1)} %copy-done.10, bf16[16,7,128,128]{3,2,1,0:T(8,128)(2,1)S(1)} %copy-done.1, bf16[512,128]{1,0:T(8,128)(2,1)} %get-tuple-element.132.refs_4_.refs_6_, ...), custom_call_target="tpu_custom_call" | custom-call | flops 1207959552 | bytes 8650752 | tf_op jit(solution)/shard_map/cond/branch_1_fun/result/pallas_call | solution.py:68
  182.1 8.1 %collective-permute-done.2 = bf16[16,4,32,128]{3,2,1,0:T(8,128)(2,1)} collective-permute-done((bf16[16,4,32,128]{3,2,1,0:T(8,128)(2,1)S(1)}, bf16[16,4,32,128]{3,2,1,0:T(8,128)(2,1)}, u32[]{:S(2)}, u32[]{:S(2)}) %collective-permute-start.2) | collective-permute-done | bytes 524320 | tf_op jit(solution)/shard_map/cond/branch_1_fun/ppermute | solution.py:17
  190.2 4.4 %last_sums.3 = (f32[16,7,32,128]{3,2,1,0:T(8,128)}, f32[32,2048]{1,0:T(8,128)}) custom-call(bf16[2,16,8,32,128]{4,3,2,1,0:T(8,128)(2,1)} %get-tuple-element.206.refs_0_, bf16[2,16,8,32,128]{4,3,2,1,0:T(8,128)(2,1)} %get-tuple-element.207.refs_1_, bf16[16,8,32,128]{3,2,1,0:T(8,128)(2,1)} %get-tuple-element.208.refs_2_, ...), custom_call_target="tpu_custom_call" | custom-call | bytes 7340032 | tf_op jit(solution)/shard_map/last_sums/pallas_call | solution.py:68
  194.6 4.6 %last_sums.2 = (f32[16,7,32,128]{3,2,1,0:T(8,128)}, f32[32,2048]{1,0:T(8,128)}, f32[32,2048]{1,0:T(8,128)}, f32[32,2048]{1,0:T(8,128)}) custom-call(bf16[2,16,6,32,128]{4,3,2,1,0:T(8,128)(2,1)} %get-tuple-element.192.refs_0_, bf16[2,16,6,32,128]{4,3,2,1,0:T(8,128)(2,1)} %get-tuple-element.193.refs_1_, bf16[16,6,32,128]{3,2,1,0:T(8,128)(2,1)S(1)} %copy-done.15, ...), custom_call_target="tpu_custom_call" | custom-call | bytes 9175040 | tf_op jit(solution)/shard_map/last_sums/pallas_call | solution.py:68
  200.1 3.8 %input_grad.1.refs_0_.refs_1_ = f32[256,2048]{1,0:T(8,128)S(1)} custom-call(bf16[256,2048]{1,0:T(8,128)(2,1)} %get-tuple-element.191.refs_0_, bf16[16,7,128,128]{3,2,1,0:T(8,128)(2,1)S(1)} %copy-done.2, bf16[512,128]{1,0:T(8,128)(2,1)} %get-tuple-element.188.refs_2_, bf16[512,128]{1,0:T(8,128)(2,1)} %get-tuple-element.189.refs_3_, ...), custom_call_target="tpu_custom_call" | custom-call | flops 805306368 | bytes 7602176 | tf_op jit(solution)/shard_map/input_grad/pallas_call | solution.py:68
  (72 shorter events, 22.5 us)
Async XLA Ops:
  0.6 61.1 %collective-permute-start.8 = (bf16[256,2048]{1,0:T(8,128)(2,1)}, bf16[256,2048]{1,0:T(8,128)(2,1)S(1)}, u32[]{:S(2)}, u32[]{:S(2)}) collective-permute-start(bf16[256,2048]{1,0:T(8,128)(2,1)} %param.16), channel_id=1, source_target_pairs={{0,4},{4,0},{8,12},{12,8},{1,5},{5,1},{9,13},{13,9},{2,6},{6,2},{1... | collective-permute-start | bytes 3145736 | tf_op jit(solution)/shard_map/ppermute | solution.py:17
  3.7 58.0 %collective-permute-start.9 = (bf16[256,2048]{1,0:T(8,128)(2,1)}, bf16[256,2048]{1,0:T(8,128)(2,1)S(1)}, u32[]{:S(2)}, u32[]{:S(2)}) collective-permute-start(bf16[256,2048]{1,0:T(8,128)(2,1)} %param.16), channel_id=1, source_target_pairs={{0,8},{4,12},{8,0},{12,4},{1,9},{5,13},{9,1},{13,5},{2,10},{6,14},... | collective-permute-start | bytes 3145736 | tf_op jit(solution)/shard_map/ppermute | solution.py:17
  6.3 55.4 %copy-start.16 = (bf16[128,2048]{1,0:T(8,128)(2,1)S(1)}, bf16[128,2048]{1,0:T(8,128)(2,1)}, u32[]{:S(2)}) copy-start(bf16[128,2048]{1,0:T(8,128)(2,1)} %param.21) | copy-start | bytes 1572868
  6.3 55.4 %copy-start.17 = (bf16[2048,128]{1,0:T(8,128)(2,1)S(1)}, bf16[2048,128]{1,0:T(8,128)(2,1)}, u32[]{:S(2)}) copy-start(bf16[2048,128]{1,0:T(8,128)(2,1)} %param.22) | copy-start | bytes 1572868
  9.0 43.4 %collective-permute-start.3 = (bf16[512,128]{1,0:T(8,128)(2,1)S(1)}, bf16[512,128]{1,0:T(8,128)(2,1)S(1)}, u32[]{:S(2)}, u32[]{:S(2)}) collective-permute-start(bf16[512,128]{1,0:T(8,128)(2,1)S(1)} %first_codes.1), channel_id=1, source_target_pairs={{0,4},{4,0},{8,12},{12,8},{1,5},{5,1},{9,13},{13,9},{2,6},{6,2},{1... | collective-permute-start | bytes 393224 | tf_op jit(solution)/shard_map/cond/branch_1_fun/ppermute | solution.py:17
  52.4 9.3 %collective-permute-start.10 = (bf16[512,128]{1,0:T(8,128)(2,1)S(1)}, bf16[512,128]{1,0:T(8,128)(2,1)S(1)}, u32[]{:S(2)}, u32[]{:S(2)}) collective-permute-start(bf16[512,128]{1,0:T(8,128)(2,1)S(1)} %get-tuple-element.181), channel_id=1, source_target_pairs={{0,8},{4,12},{8,0},{12,4},{1,9},{5,13},{9,1},{13,5},{2,10},{6,14},... | collective-permute-start | bytes 393224 | tf_op jit(solution)/shard_map/ppermute | solution.py:17
  55.3 49.0 %collective-permute-start.13 = (bf16[256,2048]{1,0:T(8,128)(2,1)}, bf16[256,2048]{1,0:T(8,128)(2,1)}, u32[]{:S(2)}, u32[]{:S(2)}) collective-permute-start(bf16[256,2048]{1,0:T(8,128)(2,1)} %get-tuple-element.183), channel_id=1, source_target_pairs={{0,4},{4,0},{8,12},{12,8},{1,5},{5,1},{9,13},{13,9},{2,6},{6,2},{1... | collective-permute-start | bytes 3145736 | tf_op jit(solution)/shard_map/ppermute | solution.py:17
  56.8 50.0 %collective-permute-start.14 = (bf16[256,2048]{1,0:T(8,128)(2,1)}, bf16[256,2048]{1,0:T(8,128)(2,1)}, u32[]{:S(2)}, u32[]{:S(2)}) collective-permute-start(bf16[256,2048]{1,0:T(8,128)(2,1)} %get-tuple-element.184), channel_id=1, source_target_pairs={{0,8},{4,12},{8,0},{12,4},{1,9},{5,13},{9,1},{13,5},{2,10},{6,14},... | collective-permute-start | bytes 3145736 | tf_op jit(solution)/shard_map/ppermute | solution.py:17
  62.7 7.7 %copy-start.5 = (bf16[256,2048]{1,0:T(8,128)(2,1)S(1)}, bf16[256,2048]{1,0:T(8,128)(2,1)}, u32[]{:S(2)}) copy-start(bf16[256,2048]{1,0:T(8,128)(2,1)} %get-tuple-element.101.refs_1_) | copy-start | bytes 3145732 | tf_op jit(solution)/shard_map/cond
  75.9 3.5 %collective-permute-start = (bf16[2,16,6,32,128]{4,3,2,1,0:T(8,128)(2,1)S(1)}, bf16[2,16,6,32,128]{4,3,2,1,0:T(8,128)(2,1)}, u32[]{:S(2)}, u32[]{:S(2)}) collective-permute-start(bf16[2,16,6,32,128]{4,3,2,1,0:T(8,128)(2,1)S(1)} %get-tuple-element.103), channel_id=1, source_target_pairs={{0,1},{1,0},{2,3},{3,2},{4,5},{5,4},{6,7},{7,6},{8,9},{9,8},{10,11... | collective-permute-start | bytes 4718600 | tf_op jit(solution)/shard_map/cond/branch_1_fun/ppermute | solution.py:17
  82.1 77.5 %collective-permute-start.11 = (bf16[256,2048]{1,0:T(8,128)(2,1)}, bf16[256,2048]{1,0:T(8,128)(2,1)S(1)}, u32[]{:S(2)}, u32[]{:S(2)}) collective-permute-start(bf16[256,2048]{1,0:T(8,128)(2,1)} %get-tuple-element.182), channel_id=1, source_target_pairs={{0,4},{4,0},{8,12},{12,8},{1,5},{5,1},{9,13},{13,9},{2,6},{6,2},{1... | collective-permute-start | bytes 3145736 | tf_op jit(solution)/shard_map/ppermute | solution.py:17
  82.5 77.0 %collective-permute-start.12 = (bf16[256,2048]{1,0:T(8,128)(2,1)}, bf16[256,2048]{1,0:T(8,128)(2,1)S(1)}, u32[]{:S(2)}, u32[]{:S(2)}) collective-permute-start(bf16[256,2048]{1,0:T(8,128)(2,1)} %get-tuple-element.182), channel_id=1, source_target_pairs={{0,8},{4,12},{8,0},{12,4},{1,9},{5,13},{9,1},{13,5},{2,10},{6,14},... | collective-permute-start | bytes 3145736 | tf_op jit(solution)/shard_map/ppermute | solution.py:17
  86.0 20.9 %collective-permute-start.15 = (bf16[16,6,32,128]{3,2,1,0:T(8,128)(2,1)S(1)}, bf16[16,6,32,128]{3,2,1,0:T(8,128)(2,1)S(1)}, u32[]{:S(2)}, u32[]{:S(2)}) collective-permute-start(bf16[16,6,32,128]{3,2,1,0:T(8,128)(2,1)S(1)} %get-tuple-element.187), channel_id=1, source_target_pairs={{0,2},{2,0},{1,3},{3,1},{4,6},{6,4},{5,7},{7,5},{8,10},{10,8},{9,1... | collective-permute-start | bytes 2359304 | tf_op jit(solution)/shard_map/ppermute | solution.py:17
  107.8 9.6 %copy-start.6 = (bf16[256,2048]{1,0:T(8,128)(2,1)S(1)}, bf16[256,2048]{1,0:T(8,128)(2,1)}, u32[]{:S(2)}) copy-start(bf16[256,2048]{1,0:T(8,128)(2,1)} %get-tuple-element.123.refs_2_) | copy-start | bytes 3145732 | tf_op jit(solution)/shard_map/cond
  107.8 9.6 %copy-start.13 = (bf16[256,2048]{1,0:T(8,128)(2,1)S(1)}, bf16[256,2048]{1,0:T(8,128)(2,1)}, u32[]{:S(2)}) copy-start(bf16[256,2048]{1,0:T(8,128)(2,1)} %get-tuple-element.125.refs_4_) | copy-start | bytes 3145732 | tf_op jit(solution)/shard_map/cond
  123.1 4.3 %collective-permute-start.6 = (bf16[2,16,8,32,128]{4,3,2,1,0:T(8,128)(2,1)S(1)}, bf16[2,16,8,32,128]{4,3,2,1,0:T(8,128)(2,1)}, u32[]{:S(2)}, u32[]{:S(2)}) collective-permute-start(bf16[2,16,8,32,128]{4,3,2,1,0:T(8,128)(2,1)S(1)} %get-tuple-element.127), channel_id=1, source_target_pairs={{0,1},{1,0},{2,3},{3,2},{4,5},{5,4},{6,7},{7,6},{8,9},{9,8},{10,11... | collective-permute-start | bytes 6291464 | tf_op jit(solution)/shard_map/cond/branch_1_fun/ppermute | solution.py:17
  130.4 29.2 %collective-permute-start.7 = (bf16[16,8,32,128]{3,2,1,0:T(8,128)(2,1)S(1)}, bf16[16,8,32,128]{3,2,1,0:T(8,128)(2,1)}, u32[]{:S(2)}, u32[]{:S(2)}) collective-permute-start(bf16[16,8,32,128]{3,2,1,0:T(8,128)(2,1)S(1)} %core_sums.4), channel_id=1, source_target_pairs={{0,2},{2,0},{1,3},{3,1},{4,6},{6,4},{5,7},{7,5},{8,10},{10,8},{9,1... | collective-permute-start | bytes 3145736 | tf_op jit(solution)/shard_map/cond/branch_1_fun/ppermute | solution.py:17
  131.8 19.5 %collective-permute-start.4 = (bf16[512,128]{1,0:T(8,128)(2,1)S(1)}, bf16[512,128]{1,0:T(8,128)(2,1)S(1)}, u32[]{:S(2)}, u32[]{:S(2)}) collective-permute-start(bf16[512,128]{1,0:T(8,128)(2,1)S(1)} %get-tuple-element.117), channel_id=1, source_target_pairs={{0,4},{4,0},{8,12},{12,8},{1,5},{5,1},{9,13},{13,9},{2,6},{6,2},{1... | collective-permute-start | bytes 393224 | tf_op jit(solution)/shard_map/cond/branch_1_fun/ppermute | solution.py:17
  151.9 7.6 %collective-permute-start.5 = (bf16[512,128]{1,0:T(8,128)(2,1)}, bf16[512,128]{1,0:T(8,128)(2,1)}, u32[]{:S(2)}, u32[]{:S(2)}) collective-permute-start(bf16[512,128]{1,0:T(8,128)(2,1)} %add_convert_fusion.1), channel_id=1, source_target_pairs={{0,8},{4,12},{8,0},{12,4},{1,9},{5,13},{9,1},{13,5},{2,10},{6,14},... | collective-permute-start | bytes 393224 | tf_op jit(solution)/shard_map/cond/branch_1_fun/ppermute | solution.py:17
  159.6 6.2 %copy-start.3 = (bf16[256,2048]{1,0:T(8,128)(2,1)S(1)}, bf16[256,2048]{1,0:T(8,128)(2,1)}, u32[]{:S(2)}) copy-start(bf16[256,2048]{1,0:T(8,128)(2,1)} %param.17) | copy-start | bytes 3145732
  160.9 43.0 %collective-permute-start.16 = (bf16[192,2048]{1,0:T(8,128)(2,1)}, bf16[192,2048]{1,0:T(8,128)(2,1)S(1)}, u32[]{:S(2)}, u32[]{:S(2)}) collective-permute-start(bf16[192,2048]{1,0:T(8,128)(2,1)} %get-tuple-element.202), channel_id=1, source_target_pairs={{0,4},{4,0},{8,12},{12,8},{1,5},{5,1},{9,13},{13,9},{2,6},{6,2},{1... | collective-permute-start | bytes 2359304 | tf_op jit(solution)/shard_map/ppermute | solution.py:17
  160.9 43.1 %collective-permute-start.17 = (bf16[192,2048]{1,0:T(8,128)(2,1)}, bf16[192,2048]{1,0:T(8,128)(2,1)S(1)}, u32[]{:S(2)}, u32[]{:S(2)}) collective-permute-start(bf16[192,2048]{1,0:T(8,128)(2,1)} %get-tuple-element.203), channel_id=1, source_target_pairs={{0,8},{4,12},{8,0},{12,4},{1,9},{5,13},{9,1},{13,5},{2,10},{6,14},... | collective-permute-start | bytes 2359304 | tf_op jit(solution)/shard_map/ppermute | solution.py:17
  162.6 43.1 %collective-permute-start.18 = (bf16[64,2048]{1,0:T(8,128)(2,1)}, bf16[64,2048]{1,0:T(8,128)(2,1)S(1)}, u32[]{:S(2)}, u32[]{:S(2)}) collective-permute-start(bf16[64,2048]{1,0:T(8,128)(2,1)} %get-tuple-element.204), channel_id=1, source_target_pairs={{0,4},{4,0},{8,12},{12,8},{1,5},{5,1},{9,13},{13,9},{2,6},{6,2},{1... | collective-permute-start | bytes 786440 | tf_op jit(solution)/shard_map/ppermute | solution.py:17
  162.9 43.7 %collective-permute-start.19 = (bf16[64,2048]{1,0:T(8,128)(2,1)}, bf16[64,2048]{1,0:T(8,128)(2,1)S(1)}, u32[]{:S(2)}, u32[]{:S(2)}) collective-permute-start(bf16[64,2048]{1,0:T(8,128)(2,1)} %get-tuple-element.205), channel_id=1, source_target_pairs={{0,8},{4,12},{8,0},{12,4},{1,9},{5,13},{9,1},{13,5},{2,10},{6,14},... | collective-permute-start | bytes 786440 | tf_op jit(solution)/shard_map/ppermute | solution.py:17
  165.8 11.8 %copy-start.1 = (bf16[16,7,128,128]{3,2,1,0:T(8,128)(2,1)S(1)}, bf16[16,7,128,128]{3,2,1,0:T(8,128)(2,1)}, u32[]{:S(2)}) copy-start(bf16[16,7,128,128]{3,2,1,0:T(8,128)(2,1)} %get-tuple-element.131.refs_3_) | copy-start | bytes 11010052 | tf_op jit(solution)/shard_map/cond
  170.8 6.8 %copy-start.8 = (bf16[256,2048]{1,0:T(8,128)(2,1)S(1)}, bf16[256,2048]{1,0:T(8,128)(2,1)}, u32[]{:S(2)}) copy-start(bf16[256,2048]{1,0:T(8,128)(2,1)} %get-tuple-element.129.refs_2_.refs_1_) | copy-start | bytes 3145732 | tf_op jit(solution)/shard_map/cond
  170.8 6.8 %copy-start.10 = (bf16[256,2048]{1,0:T(8,128)(2,1)S(1)}, bf16[256,2048]{1,0:T(8,128)(2,1)}, u32[]{:S(2)}) copy-start(bf16[256,2048]{1,0:T(8,128)(2,1)} %get-tuple-element.130.refs_3_.refs_2_) | copy-start | bytes 3145732 | tf_op jit(solution)/shard_map/cond
  170.8 6.8 %copy-start.18 = (bf16[128,2048]{1,0:T(8,128)(2,1)S(1)}, bf16[128,2048]{1,0:T(8,128)(2,1)}, u32[]{:S(2)}) copy-start(bf16[128,2048]{1,0:T(8,128)(2,1)} %get-tuple-element.134.refs_6_) | copy-start | bytes 1572868 | tf_op jit(solution)/shard_map/cond
  170.8 2.9 %collective-permute-start.1 = (bf16[2,16,4,32,128]{4,3,2,1,0:T(8,128)(2,1)S(1)}, bf16[2,16,4,32,128]{4,3,2,1,0:T(8,128)(2,1)}, u32[]{:S(2)}, u32[]{:S(2)}) collective-permute-start(bf16[2,16,4,32,128]{4,3,2,1,0:T(8,128)(2,1)S(1)} %get-tuple-element.139), channel_id=1, source_target_pairs={{0,1},{1,0},{2,3},{3,2},{4,5},{5,4},{6,7},{7,6},{8,9},{9,8},{10,11... | collective-permute-start | bytes 3145736 | tf_op jit(solution)/shard_map/cond/branch_1_fun/ppermute | solution.py:17
  176.0 14.1 %collective-permute-start.2 = (bf16[16,4,32,128]{3,2,1,0:T(8,128)(2,1)S(1)}, bf16[16,4,32,128]{3,2,1,0:T(8,128)(2,1)}, u32[]{:S(2)}, u32[]{:S(2)}) collective-permute-start(bf16[16,4,32,128]{3,2,1,0:T(8,128)(2,1)S(1)} %core_sums.5), channel_id=1, source_target_pairs={{0,2},{2,0},{1,3},{3,1},{4,6},{6,4},{5,7},{7,5},{8,10},{10,8},{9,1... | collective-permute-start | bytes 1572872 | tf_op jit(solution)/shard_map/cond/branch_1_fun/ppermute | solution.py:17
  194.6 4.6 %copy-start.2 = (bf16[16,7,128,128]{3,2,1,0:T(8,128)(2,1)S(1)}, bf16[16,7,128,128]{3,2,1,0:T(8,128)(2,1)}, u32[]{:S(2)}) copy-start(bf16[16,7,128,128]{3,2,1,0:T(8,128)(2,1)} %refs_1_.1) | copy-start | bytes 11010052
  194.6 4.6 %copy-start.19 = (bf16[2048,128]{1,0:T(8,128)(2,1)S(1)}, bf16[2048,128]{1,0:T(8,128)(2,1)}, u32[]{:S(2)}) copy-start(bf16[2048,128]{1,0:T(8,128)(2,1)} %refs_4_.1) | copy-start | bytes 1572868
  (8 other events, 17.2 us)
